TPU v7x, 256 devices: a whole 4x4x8 slice. The times are simulated.
256 devices in a mesh: leaf: 32 (over z_lo, y, core), top: 8 (over x, z_hi).
Axes of the slice: x: 4, y: 4, z: 8 (z_hi: 2, z_lo: 4; z = z_hi * 4 + z_lo), core: 2. Of those that a mesh axis runs over, the one named last changes fastest.
Arguments:
- vectors: bfloat16 [8, 32, 768, 512], P('top', 'leaf'), may hold values from -6 to 6
- near_tiles: bfloat16 [8, 32, 8, 768, 768], P('top', 'leaf'), may hold values from -0.078125 to 0.078125
- leaf_basis: bfloat16 [8, 32, 768, 128], P('top', 'leaf'), may hold values from -0.21875 to 0.21875
- transfer: bfloat16 [8, 32, 128, 128], P('top', 'leaf'), may hold values from -0.25 to 0.25
- coupling: bfloat16 [8, 32, 7, 128, 128], P('top', 'leaf'), may hold values from -0.1875 to 0.1875
- top_coupling: bfloat16 [8, 8, 128, 128], P('top'), may hold values from -0.1875 to 0.1875
- near_list: int32 [8, 32, 8], P('top', 'leaf'), may hold values from -4 to 4, as said below
- far_list: int32 [8, 32, 7], P('top', 'leaf'), may hold values from 0 to 31, as said below
- row_counts: int32 [8, 32], P('top', 'leaf'), may hold values from 384 to 768
Outputs:
- product: float32 [8, 32, 768, 512], P('top', 'leaf')
Inputs may be any that keep to these rules, and one draw needn't show every extreme that they name: `near_list`: each leaf's 8 offsets are distinct; an offset that leads outside the cluster's 32 leaves stands for an absent block. `far_list`: each leaf's entries are distinct positions in its cluster, each more than 4 away from the leaf's own position. `row_counts`: rows at and beyond the count are padding.
All inputs are finite; a program needn't handle non-finite values.
Results may differ from a plain program's by a relative error of at most 0.0045.
Values may be sent and summed in bfloat16 or wider, within the bound.
No kernel may reach another device: no remote copies, remote signals or barrier semaphores. Data moves between devices by JAX's collectives and lax.ppermute only.
A program may use at most 128 MiB of HBM per device.

v0:
```python
import jax
import jax.numpy as jnp
from jax import lax
from jax.sharding import PartitionSpec as P

REACH = 4


def passed_along(block, axis, distance):
    devices = range(lax.axis_size(axis))
    route = [(i - distance, i) for i in devices if i - distance in devices]
    return lax.ppermute(block, axis, route)


def body(
    vectors,
    near_tiles,
    leaf_basis,
    transfer,
    coupling,
    top_coupling,
    near_list,
    far_list,
    row_counts,
):
    leaf_rows = vectors.shape[2]
    row_index = jnp.arange(leaf_rows, dtype=jnp.int32)
    keep = (row_index < row_counts[0, 0]).astype(jnp.bfloat16)
    masked = vectors[0, 0] * keep[:, None]
    offsets = near_list[0, 0]
    tiles = near_tiles[0, 0]
    window = []
    for offset in range(-REACH, REACH + 1):
        if offset == 0:
            window.append(masked)
        else:
            window.append(passed_along(masked, "leaf", -offset))
    stacked = jnp.stack(window)
    span = jnp.arange(-REACH, REACH + 1, dtype=jnp.int32)
    picker = (offsets[:, None] == span[None, :]).astype(jnp.bfloat16)
    sources = jnp.einsum("kw,wrv->krv", picker, stacked, preferred_element_type=jnp.float32)
    near = jnp.einsum(
        "kij,kjv->iv", tiles, sources.astype(jnp.bfloat16), preferred_element_type=jnp.float32
    )
    basis = leaf_basis[0, 0]
    coeff = jnp.einsum("ir,iv->rv", basis, masked, preferred_element_type=jnp.float32).astype(
        jnp.bfloat16
    )
    nested = transfer[0, 0]
    upward = jnp.einsum("ab,av->bv", nested, coeff, preferred_element_type=jnp.float32)
    clusters = lax.axis_size("top")
    owner = (jnp.arange(clusters, dtype=jnp.int32) == lax.axis_index("top")).astype(jnp.float32)
    parents = lax.psum(owner[:, None, None] * upward[None], ("leaf", "top")).astype(jnp.bfloat16)
    sibling_ids = (lax.axis_index("top") + 1 + jnp.arange(clusters, dtype=jnp.int32)) % clusters
    top_pick = (sibling_ids[:, None] == jnp.arange(clusters, dtype=jnp.int32)[None, :]).astype(
        jnp.bfloat16
    )
    chosen = jnp.einsum(
        "mc,crv->mrv", top_pick, parents, preferred_element_type=jnp.float32
    ).astype(jnp.bfloat16)
    parent_field = jnp.einsum(
        "mab,mbv->av", top_coupling[0], chosen, preferred_element_type=jnp.float32
    ).astype(jnp.bfloat16)
    siblings = far_list[0, 0]
    matrices = coupling[0, 0]
    piece = lax.all_gather(coeff[None], "leaf", axis=0, tiled=True)
    blocks = jnp.arange(piece.shape[0], dtype=jnp.int32)
    chooser = (siblings[:, None] == blocks[None, :]).astype(jnp.bfloat16)
    gathered = jnp.einsum("mn,nrv->mrv", chooser, piece, preferred_element_type=jnp.float32).astype(
        jnp.bfloat16
    )
    local_field = jnp.einsum("mab,mbv->av", matrices, gathered, preferred_element_type=jnp.float32)
    local_field = (
        local_field + jnp.dot(nested, parent_field, preferred_element_type=jnp.float32)
    ).astype(jnp.bfloat16)
    result = near + jnp.dot(basis, local_field, preferred_element_type=jnp.float32)
    result = result * keep[:, None].astype(jnp.float32)
    return result[None, None]


def solution(mesh):
    in_specs = (
        P("top", "leaf", None, None),
        P("top", "leaf", None, None, None),
        P("top", "leaf", None, None),
        P("top", "leaf", None, None),
        P("top", "leaf", None, None, None),
        P("top", None, None, None),
        P("top", "leaf", None),
        P("top", "leaf", None),
        P("top", "leaf"),
    )
    out_specs = P("top", "leaf", None, None)
    return jax.shard_map(body, mesh=mesh, in_specs=in_specs, out_specs=out_specs, check_vma=False)
```

profile of v0, /device:TPU:49, one launch (start us, length us, event | category | flops | bytes accessed | tf_op | source)
XLA Modules:
  0.0 301.3 jit_solution(9302091048287589305)
XLA Ops:
  6.5 0.0 copy-start
  6.5 0.0 all-gather.3.cloned.1.call-start
  7.2 2.4 convolution_convert_fusion
  9.7 0.0 all-gather.3.cloned.1.call-update
  9.7 2.2 bitcast_multiply_fusion.1
  11.9 3.3 %collective-permute-start = (bf16[768,512]{1,0:T(8,128)(2,1)}, bf16[768,512]{1,0:T(8,128)(2,1)}, u32[]{:S(2)}, u32[]{:S(2)}) collective-permute-start(bf16[768,512]{1,0:T(8,128)(2,1)} %bitcast_multiply_fusion.1), channel_id=1, source_target_pairs={{0,32},{8,40},{16,48},{24,56},{32,64},{40,72},{48,80},{56,88},{64,... | collective-permute-start | bytes 2359304 | tf_op jit(solution)/shard_map/ppermute | solution.py:12
  15.2 5.7 %collective-permute-start.1 = (bf16[768,512]{1,0:T(8,128)(2,1)}, bf16[768,512]{1,0:T(8,128)(2,1)}, u32[]{:S(2)}, u32[]{:S(2)}) collective-permute-start(bf16[768,512]{1,0:T(8,128)(2,1)} %bitcast_multiply_fusion.1), channel_id=1, source_target_pairs={{0,24},{8,32},{16,40},{24,48},{32,56},{40,64},{48,72},{56,80},{64,... | collective-permute-start | bytes 2359304 | tf_op jit(solution)/shard_map/ppermute | solution.py:12
  20.9 2.9 collective-permute-start.2
  23.8 2.1 collective-permute-start.3
  25.9 2.2 collective-permute-start.4
  28.1 1.1 convolution_bitcast_fusion.1
  29.3 0.3 broadcast_multiply_fusion
  29.6 143.7 %all-reduce.1 = bf16[8,128,512]{2,1,0:T(8,128)(2,1)S(1)} all-reduce(f32[8,128,512]{2,1,0:T(8,128)S(1)} %broadcast_multiply_fusion), channel_id=1, replica_groups=mesh['leaf'=32,'top'=8] {'leaf','top'}, use_global_device_ids=true, to_apply=%region_0.0 | all-reduce | flops 524288 | bytes 3145728 | tf_op jit(solution)/shard_map/psum | solution.py:53
  173.4 0.0 copy-start.1
  173.4 0.7 fusion.14
  174.2 0.6 fusion.11
  174.7 0.0 copy-start.4
  174.7 0.0 collective-permute-done
  174.7 2.2 collective-permute-start.5
  176.9 1.2 bitcast_dynamic-update-slice_fusion.7
  178.1 0.0 collective-permute-done.1
  178.1 2.9 collective-permute-start.6
  181.0 1.2 bitcast_dynamic-update-slice_fusion.6
  182.2 0.0 collective-permute-done.2
  182.2 4.3 %collective-permute-start.7 = (bf16[768,512]{1,0:T(8,128)(2,1)}, bf16[768,512]{1,0:T(8,128)(2,1)S(1)}, u32[]{:S(2)}, u32[]{:S(2)}) collective-permute-start(bf16[768,512]{1,0:T(8,128)(2,1)} %bitcast_multiply_fusion.1), channel_id=1, source_target_pairs={{32,0},{40,8},{48,16},{56,24},{64,32},{72,40},{80,48},{88,56},{96,... | collective-permute-start | bytes 2359304 | tf_op jit(solution)/shard_map/ppermute | solution.py:12
  186.5 1.2 bitcast_dynamic-update-slice_fusion.5
  187.7 0.0 collective-permute-done.3
  187.7 1.2 bitcast_dynamic-update-slice_fusion.4
  188.9 0.2 fusion.17
  189.1 0.0 collective-permute-done.4
  189.2 1.2 bitcast_dynamic-update-slice_fusion.3
  190.3 5.7 %collective-permute-done.5 = bf16[768,512]{1,0:T(8,128)(2,1)S(1)} collective-permute-done((bf16[768,512]{1,0:T(8,128)(2,1)}, bf16[768,512]{1,0:T(8,128)(2,1)S(1)}, u32[]{:S(2)}, u32[]{:S(2)}) %collective-permute-start.5) | collective-permute-done | bytes 786464 | tf_op jit(solution)/shard_map/ppermute | solution.py:12
  196.0 0.1 bitcast_dynamic-update-slice_fusion.2
  196.1 34.1 %collective-permute-done.6 = bf16[768,512]{1,0:T(8,128)(2,1)S(1)} collective-permute-done((bf16[768,512]{1,0:T(8,128)(2,1)}, bf16[768,512]{1,0:T(8,128)(2,1)S(1)}, u32[]{:S(2)}, u32[]{:S(2)}) %collective-permute-start.6) | collective-permute-done | bytes 786464 | tf_op jit(solution)/shard_map/ppermute | solution.py:12
  230.2 0.1 bitcast_dynamic-update-slice_fusion.1
  230.2 17.2 %collective-permute-done.7 = bf16[768,512]{1,0:T(8,128)(2,1)S(1)} collective-permute-done((bf16[768,512]{1,0:T(8,128)(2,1)}, bf16[768,512]{1,0:T(8,128)(2,1)S(1)}, u32[]{:S(2)}, u32[]{:S(2)}) %collective-permute-start.7) | collective-permute-done | bytes 786464 | tf_op jit(solution)/shard_map/ppermute | solution.py:12
  247.4 0.1 bitcast_dynamic-update-slice_fusion
  247.5 0.0 copy-done.4
  247.5 8.7 %fusion = bf16[8,768,512]{2,0,1:T(8,128)(2,1)} fusion(bf16[9,768,512]{2,1,0:T(8,128)(2,1)S(1)} %bitcast_dynamic-update-slice_fusion, s32[9]{0:T(128)S(1)} %iota_add_fusion, s32[8]{0:T(128)S(1)} %bitcast.91), kind=kOutput, calls=%fused_computation | convolution fusion | flops 56623176 | bytes 13369412 | tf_op jit(solution)/shard_map/kw,wrv->krv/dot_general | solution.py:41
  256.1 9.1 %copy.12 = bf16[8,768,512]{1,2,0:T(8,128)(2,1)} copy(bf16[8,768,512]{2,0,1:T(8,128)(2,1)} %fusion) | data formatting | bytes 12582912 | tf_op jit(solution)/shard_map/kw,wrv->krv/dot_general | solution.py:41
  265.2 5.5 %copy.17 = bf16[64,8,32,128]{3,2,1,0:T(8,128)(2,1)} copy(bf16[64,8,32,128]{3,1,2,0:T(8,128)(2,1)} %bitcast.89) | data formatting | bytes 8388608
  270.7 8.6 %copy.13 = bf16[32,128,512]{2,0,1:T(8,128)(2,1)} copy(bf16[32,128,512]{1,0,2:T(8,128)(2,1)} %bitcast.88) | data formatting | bytes 8388608 | tf_op jit(solution)/shard_map/all_gather | solution.py:66
  279.3 0.0 copy-done.5
  279.3 2.9 fusion.29
  282.2 0.6 convolution_bitcast_fusion.2
  282.8 0.5 fusion.13
  283.4 9.5 %fusion.6 = f32[1,1,768,512]{2,3,1,0:T(8,128)S(1)} fusion(f32[512,768]{1,0:T(8,128)S(1)} %fusion.13, bf16[1,1,8,768,768]{4,3,2,1,0:T(8,128)(2,1)} %param.10, bf16[8,768,512]{1,2,0:T(8,128)(2,1)} %copy.12, f32[768]{0:T(1024)S(1)} %fusion.39), kind=kOutput, calls=%fused_computation.9 | convolution fusion | flops 4832624640 | bytes 18877440 | tf_op jit(solution)/shard_map/kij,kjv->iv/dot_general | solution.py:42
  292.9 1.6 copy.10
  (15 shorter events, 0.0 us)
Async XLA Ops:
  6.5 167.6 %copy-start = (bf16[1,8,128,128]{3,2,1,0:T(8,128)(2,1)S(1)}, bf16[1,8,128,128]{3,2,1,0:T(8,128)(2,1)}, u32[]{:S(2)}) copy-start(bf16[1,8,128,128]{3,2,1,0:T(8,128)(2,1)} %param.14) | copy-start | bytes 786436
  6.5 258.7 %all-gather.3.cloned.1.call-start = ((), (), s32[]{:S(2)}) async-start(), calls=%async_computation | async-start | bytes 4325376 | tf_op jit(solution)/shard_map/all_gather | solution.py:66
  11.9 162.9 %collective-permute-start = (bf16[768,512]{1,0:T(8,128)(2,1)}, bf16[768,512]{1,0:T(8,128)(2,1)}, u32[]{:S(2)}, u32[]{:S(2)}) collective-permute-start(bf16[768,512]{1,0:T(8,128)(2,1)} %bitcast_multiply_fusion.1), channel_id=1, source_target_pairs={{0,32},{8,40},{16,48},{24,56},{32,64},{40,72},{48,80},{56,88},{64,... | collective-permute-start | bytes 2359304 | tf_op jit(solution)/shard_map/ppermute | solution.py:12
  15.2 163.0 %collective-permute-start.1 = (bf16[768,512]{1,0:T(8,128)(2,1)}, bf16[768,512]{1,0:T(8,128)(2,1)}, u32[]{:S(2)}, u32[]{:S(2)}) collective-permute-start(bf16[768,512]{1,0:T(8,128)(2,1)} %bitcast_multiply_fusion.1), channel_id=1, source_target_pairs={{0,24},{8,32},{16,40},{24,48},{32,56},{40,64},{48,72},{56,80},{64,... | collective-permute-start | bytes 2359304 | tf_op jit(solution)/shard_map/ppermute | solution.py:12
  20.9 161.4 %collective-permute-start.2 = (bf16[768,512]{1,0:T(8,128)(2,1)}, bf16[768,512]{1,0:T(8,128)(2,1)}, u32[]{:S(2)}, u32[]{:S(2)}) collective-permute-start(bf16[768,512]{1,0:T(8,128)(2,1)} %bitcast_multiply_fusion.1), channel_id=1, source_target_pairs={{0,16},{8,24},{16,32},{24,40},{32,48},{40,56},{48,64},{56,72},{64,... | collective-permute-start | bytes 2359304 | tf_op jit(solution)/shard_map/ppermute | solution.py:12
  23.8 163.9 %collective-permute-start.3 = (bf16[768,512]{1,0:T(8,128)(2,1)}, bf16[768,512]{1,0:T(8,128)(2,1)}, u32[]{:S(2)}, u32[]{:S(2)}) collective-permute-start(bf16[768,512]{1,0:T(8,128)(2,1)} %bitcast_multiply_fusion.1), channel_id=1, source_target_pairs={{0,8},{8,16},{16,24},{24,32},{32,40},{40,48},{48,56},{56,64},{64,7... | collective-permute-start | bytes 2359304 | tf_op jit(solution)/shard_map/ppermute | solution.py:12
  25.9 163.3 %collective-permute-start.4 = (bf16[768,512]{1,0:T(8,128)(2,1)}, bf16[768,512]{1,0:T(8,128)(2,1)}, u32[]{:S(2)}, u32[]{:S(2)}) collective-permute-start(bf16[768,512]{1,0:T(8,128)(2,1)} %bitcast_multiply_fusion.1), channel_id=1, source_target_pairs={{8,0},{16,8},{24,16},{32,24},{40,32},{48,40},{56,48},{64,56},{72,6... | collective-permute-start | bytes 2359304 | tf_op jit(solution)/shard_map/ppermute | solution.py:12
  173.4 15.5 %copy-start.1 = (bf16[1,1,768,512]{3,2,1,0:T(8,128)(2,1)S(1)}, bf16[1,1,768,512]{3,2,1,0:T(8,128)(2,1)}, u32[]{:S(2)}) copy-start(bf16[1,1,768,512]{3,2,1,0:T(8,128)(2,1)} %param.9) | copy-start | bytes 2359300
  174.7 72.7 %copy-start.4 = (s32[1,1,8]{2,1,0:T(1,128)S(1)}, s32[1,1,8]{2,1,0:T(1,128)}, u32[]{:S(2)}) copy-start(s32[1,1,8]{2,1,0:T(1,128)} %param.15) | copy-start | bytes 100
  174.7 21.3 %collective-permute-start.5 = (bf16[768,512]{1,0:T(8,128)(2,1)}, bf16[768,512]{1,0:T(8,128)(2,1)S(1)}, u32[]{:S(2)}, u32[]{:S(2)}) collective-permute-start(bf16[768,512]{1,0:T(8,128)(2,1)} %bitcast_multiply_fusion.1), channel_id=1, source_target_pairs={{16,0},{24,8},{32,16},{40,24},{48,32},{56,40},{64,48},{72,56},{80,... | collective-permute-start | bytes 2359304 | tf_op jit(solution)/shard_map/ppermute | solution.py:12
  178.1 52.0 %collective-permute-start.6 = (bf16[768,512]{1,0:T(8,128)(2,1)}, bf16[768,512]{1,0:T(8,128)(2,1)S(1)}, u32[]{:S(2)}, u32[]{:S(2)}) collective-permute-start(bf16[768,512]{1,0:T(8,128)(2,1)} %bitcast_multiply_fusion.1), channel_id=1, source_target_pairs={{24,0},{32,8},{40,16},{48,24},{56,32},{64,40},{72,48},{80,56},{88,... | collective-permute-start | bytes 2359304 | tf_op jit(solution)/shard_map/ppermute | solution.py:12
  182.2 65.2 %collective-permute-start.7 = (bf16[768,512]{1,0:T(8,128)(2,1)}, bf16[768,512]{1,0:T(8,128)(2,1)S(1)}, u32[]{:S(2)}, u32[]{:S(2)}) collective-permute-start(bf16[768,512]{1,0:T(8,128)(2,1)} %bitcast_multiply_fusion.1), channel_id=1, source_target_pairs={{32,0},{40,8},{48,16},{56,24},{64,32},{72,40},{80,48},{88,56},{96,... | collective-permute-start | bytes 2359304 | tf_op jit(solution)/shard_map/ppermute | solution.py:12
  265.2 14.1 %copy-start.5 = (s32[1,1,7]{2,1,0:T(1,128)S(1)}, s32[1,1,7]{2,1,0:T(1,128)}, u32[]{:S(2)}) copy-start(s32[1,1,7]{2,1,0:T(1,128)} %param.16) | copy-start | bytes 88
  270.7 11.5 %copy-start.6 = (bf16[1,1,7,128,128]{4,3,2,1,0:T(8,128)(2,1)S(1)}, bf16[1,1,7,128,128]{4,3,2,1,0:T(8,128)(2,1)}, u32[]{:S(2)}) copy-start(bf16[1,1,7,128,128]{4,3,2,1,0:T(8,128)(2,1)} %param.13) | copy-start | bytes 688132
  270.7 12.1 %copy-start.2 = (bf16[1,1,768,128]{3,2,1,0:T(8,128)(2,1)S(1)}, bf16[1,1,768,128]{3,2,1,0:T(8,128)(2,1)}, u32[]{:S(2)}) copy-start(bf16[1,1,768,128]{3,2,1,0:T(8,128)(2,1)} %param.11) | copy-start | bytes 589828
  270.7 12.1 %copy-start.3 = (bf16[1,1,128,128]{3,2,1,0:T(8,128)(2,1)S(1)}, bf16[1,1,128,128]{3,2,1,0:T(8,128)(2,1)}, u32[]{:S(2)}) copy-start(bf16[1,1,128,128]{3,2,1,0:T(8,128)(2,1)} %param.12) | copy-start | bytes 98308
Sparse Core Ops, SparseCore 0:
  9.8 97.4 all-gather.2
where the time goes:
time: 302 us; the launch traced here: 301 us
  blocking collectives  144 us (48%)
  waiting for transfers between devices  57 us (19%)
  local copies, waits for them, and re-layouts  30.9 us (10%)
  matrix products  27 us (9%)
  starting transfers between devices  25.6 us (8%)
  between operations  14.4 us (5%)
    psum x1, blocking collectives, body(): lax.psum(owner[:, None, None] * upward[None], ('leaf', 'top'))  144 us
    ppermute x8, waiting for transfers between devices, passed_along(): return lax.ppermute(block, axis, route)  57 us
    ppermute x8, starting transfers between devices, passed_along(): return lax.ppermute(block, axis, route)  25.6 us
    unnamed x22, local copies, waits for them, and re-layouts  11.6 us
    dot_general x1, matrix products, body(): jnp.einsum('kij,kjv->iv', tiles, sources.astype(jnp.bfloat16), preferred_...  9.49 us
    dot_general x1, local copies, waits for them, and re-layouts, body(): jnp.einsum('kw,wrv->krv', picker, stacked, preferred_element_type=jnp.flo...  9.05 us
    dot_general x1, matrix products, body(): jnp.einsum('kw,wrv->krv', picker, stacked, preferred_element_type=jnp.flo...  8.67 us
    all_gather x1, local copies, waits for them, and re-layouts, body(): piece = lax.all_gather(coeff[None], 'leaf', axis=0, tiled=True)  8.61 us
  transfers between devices with their start and end apart: 9, of which 3 were waited for; matrix products, arithmetic and copies ran while one was open for 10% of the time, Pallas kernels for 0%

commit v1 on v0

v1 whole, which is shorter than its diff:
```python
import functools

import jax
import jax.numpy as jnp
from jax import lax
from jax.experimental import pallas as pl
from jax.experimental.pallas import tpu as pltpu
from jax.sharding import PartitionSpec as P

Z, Y, CORES = 4, 4, 2
ROW = Y * CORES
CHIPS = Z * Y
F32, BF16 = jnp.float32, jnp.bfloat16
LIMIT = 48 * 1024 * 1024


def chip_step(distance):
    return [
        (p * 2 + c, (p + distance) * 2 + c)
        for p in range(CHIPS)
        for c in range(2)
        if 0 <= p + distance < CHIPS
    ]


def turn(dz, dy):
    return [
        (z * ROW + y * 2 + c, ((z + dz) % Z) * ROW + ((y + dy) % Y) * 2 + c)
        for z in range(Z)
        for y in range(Y)
        for c in range(2)
    ]


SWAP = [(i, i ^ 1) for i in range(2 * CHIPS)]
TO_FIRST = [(2 * p + 1, 2 * p) for p in range(CHIPS)]
TO_SECOND = [(2 * p, 2 * p + 1) for p in range(CHIPS)]


def send(block, route):
    return lax.ppermute(block, "leaf", route)


def dot(a, b, dims=((1,), (0,))):
    return lax.dot_general(a, b, (dims, ((), ())), preferred_element_type=F32)


def cost(flops, moved):
    return pl.CostEstimate(flops=int(flops), bytes_accessed=int(moved), transcendentals=0)


VMEM = pl.BlockSpec(memory_space=pltpu.VMEM)
SMEM = pl.BlockSpec(memory_space=pltpu.SMEM)


def upward_kernel(count_ref, vec_ref, basis_ref, transfer_ref, masked_ref, coeff_ref, up_ref):
    rows = lax.broadcasted_iota(jnp.int32, vec_ref.shape, 0)
    masked = jnp.where(rows < count_ref[0], vec_ref[...].astype(F32), 0.0).astype(BF16)
    masked_ref[...] = masked
    coeff = dot(basis_ref[...], masked, ((0,), (0,))).astype(BF16)
    coeff_ref[...] = coeff
    up_ref[...] = dot(coeff, transfer_ref[...], ((0,), (0,))).astype(BF16)


def upward(count, vec, basis, transfer):
    rows, vecs = vec.shape
    rank = basis.shape[1]
    return pl.pallas_call(
        upward_kernel,
        out_shape=[
            jax.ShapeDtypeStruct((rows, vecs), BF16),
            jax.ShapeDtypeStruct((rank, vecs), BF16),
            jax.ShapeDtypeStruct((vecs, rank), BF16),
        ],
        in_specs=[SMEM, VMEM, VMEM, VMEM],
        out_specs=[VMEM] * 3,
        compiler_params=pltpu.CompilerParams(vmem_limit_bytes=LIMIT),
        cost_estimate=cost(2 * rows * rank * vecs, 2 * rows * vecs * 2),
    )(count, vec, basis, transfer)


def partial_kernel(rank, pick_ref, *refs):
    couplings, coeffs, outs, acc = refs[:Z], refs[Z : Z + ROW], refs[Z + ROW : -1], refs[-1]
    for d in range(Z):
        acc[...] = jnp.zeros_like(acc)
        for s in range(ROW):
            which = pick_ref[d * ROW + s]

            @pl.when(which >= 0)
            def add():
                start = pl.multiple_of(which * rank, rank)
                acc[...] += dot(couplings[d][pl.ds(start, rank), :], coeffs[s][...])

        outs[d][...] = acc[...].astype(outs[d].dtype)


def far_partials(pick, couplings, coeffs):
    rank, vecs = coeffs[0].shape
    return pl.pallas_call(
        functools.partial(partial_kernel, rank),
        out_shape=[jax.ShapeDtypeStruct((rank, vecs), F32 if d == 0 else BF16) for d in range(Z)],
        in_specs=[SMEM] + [VMEM] * (Z + ROW),
        out_specs=[VMEM] * Z,
        scratch_shapes=[pltpu.VMEM((rank, vecs), F32)],
        compiler_params=pltpu.CompilerParams(vmem_limit_bytes=LIMIT),
        cost_estimate=cost(2 * 16 * rank * rank * vecs, 12 * rank * vecs * 2),
    )(pick, *couplings, *coeffs)


def top_kernel(shift_ref, parents_ref, coupling_ref, out_ref):
    total = jnp.zeros(out_ref.shape, F32)
    for c in range(parents_ref.shape[0]):
        total += dot(parents_ref[c], coupling_ref[shift_ref[c]], ((1,), (1,)))
    out_ref[...] = total.astype(BF16)


def top_field(shift, parents, coupling):
    return pl.pallas_call(
        top_kernel,
        out_shape=jax.ShapeDtypeStruct(parents.shape[1:], BF16),
        in_specs=[SMEM, VMEM, VMEM],
        out_specs=VMEM,
        compiler_params=pltpu.CompilerParams(vmem_limit_bytes=LIMIT),
        cost_estimate=cost(2 * 8 * 16 * 128 * 128, 8 * 128 * 128 * 2),
    )(shift, parents, coupling)


def near_first_kernel(count, pick_ref, tile_ref, *refs):
    sources, out_ref = refs[:count], refs[count]
    step = pl.program_id(0)

    @pl.when(step == 0)
    def clear():
        out_ref[...] = jnp.zeros_like(out_ref)

    for s in range(count):

        @pl.when((step == s) & (pick_ref[s] >= 0))
        def add():
            out_ref[...] += dot(tile_ref[0], sources[s][...])


def whole(shape):
    return pl.BlockSpec(shape, lambda i, pick: (0,) * len(shape))


def tile_spec(tiles):
    _, rows, cols = tiles.shape
    return pl.BlockSpec((1, rows, cols), lambda i, pick: (jnp.maximum(pick[i], 0), 0, 0))


def near_first(pick, tiles, sources):
    count = len(sources)
    rows, vecs = sources[0].shape
    return pl.pallas_call(
        functools.partial(near_first_kernel, count),
        out_shape=jax.ShapeDtypeStruct((rows, vecs), F32),
        grid_spec=pltpu.PrefetchScalarGridSpec(
            num_scalar_prefetch=1,
            grid=(count,),
            in_specs=[tile_spec(tiles)] + [whole(s.shape) for s in sources],
            out_specs=whole((rows, vecs)),
        ),
        compiler_params=pltpu.CompilerParams(vmem_limit_bytes=LIMIT),
        cost_estimate=cost(2 * count * rows * rows * vecs, count * rows * (rows + vecs) * 2),
    )(pick, tiles, *sources)


def near_last_kernel(count, pick_ref, tile_ref, *refs):
    sources = refs[:count]
    near_ref, basis_ref, transfer_ref, field_ref, own_ref, a_ref, b_ref, c_ref, out_ref = refs[count:]
    step = pl.program_id(0)

    @pl.when(step == 0)
    def far():
        local = own_ref[...] + a_ref[...].astype(F32) + b_ref[...].astype(F32)
        local += c_ref[...].astype(F32) + dot(transfer_ref[...], field_ref[...], ((1,), (1,)))
        out_ref[...] = near_ref[...] + dot(basis_ref[...], local.astype(BF16))

    for s in range(count):

        @pl.when((step == s) & (pick_ref[s] >= 0))
        def add():
            out_ref[...] += dot(tile_ref[0], sources[s][...])

    @pl.when(step == count - 1)
    def cut():
        rows = lax.broadcasted_iota(jnp.int32, out_ref.shape, 0)
        out_ref[...] = jnp.where(rows < pick_ref[count], out_ref[...], 0.0)


def near_last(pick, tiles, sources, rest):
    count = len(sources)
    rows, vecs = sources[0].shape
    return pl.pallas_call(
        functools.partial(near_last_kernel, count),
        out_shape=jax.ShapeDtypeStruct((rows, vecs), F32),
        grid_spec=pltpu.PrefetchScalarGridSpec(
            num_scalar_prefetch=1,
            grid=(count,),
            in_specs=[tile_spec(tiles)] + [whole(s.shape) for s in (*sources, *rest)],
            out_specs=whole((rows, vecs)),
        ),
        compiler_params=pltpu.CompilerParams(vmem_limit_bytes=LIMIT),
        cost_estimate=cost(2 * count * rows * rows * vecs, count * rows * (rows + vecs) * 2),
    )(pick, tiles, *sources, *rest)


def index_of(wanted, entries):
    places = jnp.arange(entries.shape[-1], dtype=jnp.int32)
    return jnp.max(jnp.where(entries == wanted[..., None], places, -1), axis=-1).astype(jnp.int32)


def body(
    vectors,
    near_tiles,
    leaf_basis,
    transfer,
    coupling,
    top_coupling,
    near_list,
    far_list,
    row_counts,
):
    me = lax.axis_index("leaf").astype(jnp.int32)
    mine = lax.axis_index("top").astype(jnp.int32)
    clusters = lax.axis_size("top")
    leaves = lax.axis_size("leaf")
    core, chip_y, row = me % 2, (me // 2) % Y, me // ROW
    basis, nested, tiles = leaf_basis[0, 0], transfer[0, 0], near_tiles[0, 0]
    far_count, rank, _ = coupling.shape[2:]
    vecs = vectors.shape[3]
    count = row_counts[0]

    masked, coeff, up = upward(count, vectors[0, 0], basis, nested)

    from_low = send(masked, chip_step(1))
    from_high = send(masked, chip_step(-1))
    beside = send(masked, SWAP)

    listed = jnp.zeros((16, rank), BF16).at[0, :far_count].set(far_list[0, 0].astype(BF16))
    packet = jnp.concatenate([coupling[0, 0].reshape(far_count * rank, rank), listed])
    packets = [packet] + [send(packet, turn(d, 0)) for d in range(1, Z)]

    across = [coeff] + [send(coeff, turn(0, d)) for d in range(1, Y)]
    coeffs = across + [send(block, SWAP) for block in across]
    steps = jnp.arange(Y, dtype=jnp.int32)
    seats = ((chip_y - steps) % Y) * 2 + row * ROW
    owners = jnp.concatenate([seats + core, seats + 1 - core])
    lists = jnp.stack([p[far_count * rank, :far_count] for p in packets]).astype(jnp.int32)
    lists = lists.at[0].set(far_list[0, 0])
    far_pick = index_of(jnp.broadcast_to(owners[None], (Z, ROW)), lists[:, None, :])

    pieces = lax.all_to_all(up, "leaf", 0, 0, tiled=True).reshape(leaves, vecs // leaves, rank)
    parent = jnp.sum(pieces.astype(F32), axis=0).astype(BF16)
    parents = lax.all_to_all(
        jnp.broadcast_to(parent[None], (clusters, *parent.shape)), "top", 0, 0, tiled=True
    )
    shift = (jnp.arange(clusters, dtype=jnp.int32) + 2 * clusters - 1 - mine) % clusters
    piece = top_field(shift, parents, top_coupling[0])
    field = lax.all_to_all(
        jnp.broadcast_to(piece[None], (leaves, *piece.shape)), "leaf", 0, 0, tiled=True
    ).reshape(vecs, rank)

    own, *others = far_partials(far_pick.reshape(-1), packets, coeffs)
    back = [send(block, turn(-d, 0)) for d, block in zip(range(1, Z), others, strict=True)]

    from_low2 = send(from_low, chip_step(1))
    from_high2 = send(from_high, chip_step(-1))
    low_beside = send(from_low, SWAP)
    high_beside = send(from_high, SWAP)
    side = 1 - 2 * core
    zero = jnp.int32(0)
    first_at = jnp.stack([zero, side, zero - 2, zero + 2, side - 2, side + 2])
    absent = jnp.int32(99)
    last_at = jnp.stack(
        [zero - 4, zero + 4, jnp.where(core == 0, -3, absent), jnp.where(core == 1, 3, absent)]
    )
    offsets = near_list[0, 0][None]
    near = near_first(
        index_of(first_at, offsets),
        tiles,
        [masked, beside, from_low, from_high, low_beside, high_beside],
    )
    low2_beside = send(from_low2, TO_FIRST)
    high2_beside = send(from_high2, TO_SECOND)
    result = near_last(
        jnp.concatenate([index_of(last_at, offsets), count]),
        tiles,
        [from_low2, from_high2, low2_beside, high2_beside],
        [near, basis, nested, field, own, *back],
    )
    return result[None, None]


def solution(mesh):
    in_specs = (
        P("top", "leaf", None, None),
        P("top", "leaf", None, None, None),
        P("top", "leaf", None, None),
        P("top", "leaf", None, None),
        P("top", "leaf", None, None, None),
        P("top", None, None, None),
        P("top", "leaf", None),
        P("top", "leaf", None),
        P("top", "leaf"),
    )
    out_specs = P("top", "leaf", None, None)
    return jax.shard_map(body, mesh=mesh, in_specs=in_specs, out_specs=out_specs, check_vma=False)
```

time: 302 us -> 150 us (0.50)
  the two profiles are of different devices: /device:TPU:49 before, /device:TPU:1 now
where the time goes in v1:
time: 150 us; the launch traced here: 148 us
  starting transfers between devices  65.3 us (44%)
  waiting for transfers between devices  31.7 us (21%)
  local copies, waits for them, and re-layouts  23.5 us (16%)
  Pallas kernels  21.3 us (14%)
  other arithmetic  5.7 us (4%)
    ppermute x22, starting transfers between devices, send(): return lax.ppermute(block, 'leaf', route)  34.7 us
    unnamed x60, local copies, waits for them, and re-layouts  19.2 us
    ppermute x22, waiting for transfers between devices, send(): return lax.ppermute(block, 'leaf', route)  19 us
    all_to_all x1, waiting for transfers between devices, body(): lax.all_to_all(up, 'leaf', 0, 0, tiled=True)  12.6 us
    all_to_all x1, starting transfers between devices, body(): lax.all_to_all(jnp.broadcast_to(piece[None], (leaves, *piece.shape)), 'le...  11.6 us
    all_to_all x1, starting transfers between devices, body(): lax.all_to_all(up, 'leaf', 0, 0, tiled=True)  10.3 us
    pallas_call x1, Pallas kernels, near_first(): pl.pallas_call(functools.partial(near_first_kernel, count), out_shape=jax...  8.96 us
    all_to_all x1, starting transfers between devices, body(): lax.all_to_all(jnp.broadcast_to(parent[None], (clusters, *parent.shape)),...  8.75 us
  transfers between devices with their start and end apart: 25, of which 8 were waited for; matrix products, arithmetic and copies ran while one was open for 7% of the time, Pallas kernels for 9%

profile of v1, /device:TPU:1, one launch (start us, length us, event | category | flops | bytes accessed | tf_op | source)
XLA Modules:
  0.0 148.4 jit_solution(2358693667657630623)
XLA Ops:
  0.7 0.9 copy-done.1
  1.6 1.1 copy-done.3
  2.8 0.8 copy-done.13
  4.7 4.1 %collective-permute-start = (bf16[768,512]{1,0:T(8,128)(2,1)S(1)}, bf16[768,512]{1,0:T(8,128)(2,1)S(1)}, u32[]{:S(2)}, u32[]{:S(2)}) collective-permute-start(bf16[768,512]{1,0:T(8,128)(2,1)S(1)} %get-tuple-element.36.refs_0_), channel_id=1, source_target_pairs={{0,16},{8,24},{16,32},{24,40},{32,48},{40,56},{48,64},{56,72},{64,... | collective-permute-start | bytes 2359304 | tf_op jit(solution)/shard_map/ppermute | solution.py:41
  8.8 1.3 collective-permute-start.2
  10.1 2.2 %collective-permute-start.12 = (bf16[128,512]{1,0:T(8,128)(2,1)S(1)}, bf16[128,512]{1,0:T(8,128)(2,1)S(1)}, u32[]{:S(2)}, u32[]{:S(2)}) collective-permute-start(bf16[128,512]{1,0:T(8,128)(2,1)S(1)} %get-tuple-element.38.refs_4_), channel_id=1, source_target_pairs={{0,16},{8,24},{16,32},{24,40},{32,48},{40,56},{48,0},{56,8},{64,80... | collective-permute-start | bytes 393224 | tf_op jit(solution)/shard_map/ppermute | solution.py:41
  12.3 2.6 %collective-permute-start.13 = (bf16[128,512]{1,0:T(8,128)(2,1)S(1)}, bf16[128,512]{1,0:T(8,128)(2,1)S(1)}, u32[]{:S(2)}, u32[]{:S(2)}) collective-permute-start(bf16[128,512]{1,0:T(8,128)(2,1)S(1)} %get-tuple-element.38.refs_4_), channel_id=1, source_target_pairs={{0,32},{8,40},{16,48},{24,56},{32,0},{40,8},{48,16},{56,24},{64,96... | collective-permute-start | bytes 393224 | tf_op jit(solution)/shard_map/ppermute | solution.py:41
  14.8 1.1 collective-permute-start.14
  15.9 11.8 %collective-permute-done.12.refs_5_ = bf16[128,512]{1,0:T(8,128)(2,1)S(1)} collective-permute-done((bf16[128,512]{1,0:T(8,128)(2,1)S(1)}, bf16[128,512]{1,0:T(8,128)(2,1)S(1)}, u32[]{:S(2)}, u32[]{:S(2)}) %collective-permute-start.12) | collective-permute-done | bytes 131104 | tf_op jit(solution)/shard_map/ppermute | solution.py:41
  27.8 2.7 %collective-permute-start.15 = (bf16[128,512]{1,0:T(8,128)(2,1)S(1)}, bf16[128,512]{1,0:T(8,128)(2,1)S(1)}, u32[]{:S(2)}, u32[]{:S(2)}) collective-permute-start(bf16[128,512]{1,0:T(8,128)(2,1)S(1)} %get-tuple-element.38.refs_4_), channel_id=1, source_target_pairs={{0,8},{8,0},{16,24},{24,16},{32,40},{40,32},{48,56},{56,48},{64,72... | collective-permute-start | bytes 393224 | tf_op jit(solution)/shard_map/ppermute | solution.py:41
  30.5 0.7 convert_bitcast_fusion
  31.2 1.0 fusion.1.refs_0_
  32.2 1.8 %collective-permute-done.13.refs_6_ = bf16[128,512]{1,0:T(8,128)(2,1)S(1)} collective-permute-done((bf16[128,512]{1,0:T(8,128)(2,1)S(1)}, bf16[128,512]{1,0:T(8,128)(2,1)S(1)}, u32[]{:S(2)}, u32[]{:S(2)}) %collective-permute-start.13) | collective-permute-done | bytes 131104 | tf_op jit(solution)/shard_map/ppermute | solution.py:41
  33.9 2.6 %collective-permute-start.9 = (bf16[912,128]{1,0:T(8,128)(2,1)S(1)}, bf16[912,128]{1,0:T(8,128)(2,1)}, u32[]{:S(2)}, u32[]{:S(2)}) collective-permute-start(bf16[912,128]{1,0:T(8,128)(2,1)S(1)} %fusion.1.refs_0_), channel_id=1, source_target_pairs={{0,64},{8,72},{16,80},{24,88},{32,96},{40,104},{48,112},{56,120},{... | collective-permute-start | bytes 700424 | tf_op jit(solution)/shard_map/ppermute | solution.py:41
  37.2 3.0 %collective-permute-start.10 = (bf16[912,128]{1,0:T(8,128)(2,1)S(1)}, bf16[912,128]{1,0:T(8,128)(2,1)}, u32[]{:S(2)}, u32[]{:S(2)}) collective-permute-start(bf16[912,128]{1,0:T(8,128)(2,1)S(1)} %fusion.1.refs_0_), channel_id=1, source_target_pairs={{0,128},{8,136},{16,144},{24,152},{32,160},{40,168},{48,176},{56,1... | collective-permute-start | bytes 700424 | tf_op jit(solution)/shard_map/ppermute | solution.py:41
  40.8 0.7 collective-permute-start.11
  41.6 1.3 collective-permute-start.1
  42.9 1.3 collective-permute-start.3
  44.2 10.3 %all-to-all-start = ((bf16[32,16,128]{2,1,0:T(8,128)(2,1)}), bf16[32,16,128]{2,1,0:T(8,128)(2,1)}, u32[]{:S(2)}, u32[]{:S(2)}) async-start(bf16[32,16,128]{2,1,0:T(8,128)(2,1)} %bitcast.29), calls=%async_computation | async-start | bytes 262144 | tf_op jit(solution)/shard_map/all_to_all | solution.py:254
  54.9 0.7 collective-permute-done.10.refs_2_
  58.9 4.7 %collective-permute-start.4 = (bf16[768,512]{1,0:T(8,128)(2,1)S(1)}, bf16[768,512]{1,0:T(8,128)(2,1)}, u32[]{:S(2)}, u32[]{:S(2)}) collective-permute-start(bf16[768,512]{1,0:T(8,128)(2,1)S(1)} %collective-permute-done.1.refs_0_), channel_id=1, source_target_pairs={{8,0},{24,16},{40,32},{56,48},{72,64},{88,80},{104,96},{120,112},{... | collective-permute-start | bytes 2359304 | tf_op jit(solution)/shard_map/ppermute | solution.py:41
  63.8 1.3 collective-permute-start.5
  65.5 0.7 slice.44
  67.6 12.6 %all-to-all-done = bf16[32,16,128]{2,1,0:T(8,128)(2,1)} async-done(((bf16[32,16,128]{2,1,0:T(8,128)(2,1)}), bf16[32,16,128]{2,1,0:T(8,128)(2,1)}, u32[]{:S(2)}, u32[]{:S(2)}) %all-to-all-start) | async-done | bytes 131104 | tf_op jit(solution)/shard_map/all_to_all | solution.py:254
  80.3 0.9 reduce_sum.12
  81.8 8.7 %all-to-all-start.1 = ((bf16[8,16,128]{2,1,0:T(8,128)(2,1)}), bf16[8,16,128]{2,1,0:T(8,128)(2,1)S(1)}, u32[]{:S(2)}, u32[]{:S(2)}) async-start(bf16[8,16,128]{2,1,0:T(8,128)(2,1)} %broadcast_in_dim.48), calls=%async_computation.1 | async-start | bytes 65536 | tf_op jit(solution)/shard_map/all_to_all | solution.py:256
  90.6 1.3 select_reduce_fusion
  91.9 0.8 reshape.108.pick_ref
  92.6 0.9 copy-done.16
  93.6 0.9 copy-done.18
  94.5 0.9 copy-done.20
  95.4 0.9 copy-done.22
  96.3 3.0 %shard_map.94 = (f32[128,512]{1,0:T(8,128)S(1)}, bf16[128,512]{1,0:T(8,128)(2,1)S(1)}, bf16[128,512]{1,0:T(8,128)(2,1)S(1)}, bf16[128,512]{1,0:T(8,128)(2,1)S(1)}) custom-call(s32[32]{0:T(128)S(1)} %reshape.108.pick_ref, bf16[912,128]{1,0:T(8,128)(2,1)S(1)} %fusion.1.refs_0_, bf16[912,128]{1,0:T(8,128)(2,1)} %collective-permute-done.9.refs_1_, ...), custom_call_target="tpu_custom_call" | custom-call | flops 268435456 | bytes 1572864 | tf_op jit(solution)/shard_map/pallas_call | solution.py:99
  99.3 0.7 copy-done.4
  102.0 0.9 copy-done.6
  103.0 0.7 copy-done.24
  103.7 0.8 shard_map.93
  104.4 0.7 broadcast_in_dim.49
  105.1 11.6 %all-to-all-start.2 = ((bf16[32,16,128]{2,1,0:T(8,128)(2,1)}), bf16[32,16,128]{2,1,0:T(8,128)(2,1)S(1)}, u32[]{:S(2)}, u32[]{:S(2)}) async-start(bf16[32,16,128]{2,1,0:T(8,128)(2,1)} %broadcast_in_dim.49), calls=%async_computation.2 | async-start | bytes 262144 | tf_op jit(solution)/shard_map/all_to_all | solution.py:261
  116.8 3.3 %collective-permute-start.19 = (bf16[128,512]{1,0:T(8,128)(2,1)}, bf16[128,512]{1,0:T(8,128)(2,1)S(1)}, u32[]{:S(2)}, u32[]{:S(2)}) collective-permute-start(bf16[128,512]{1,0:T(8,128)(2,1)} %copy-done.27), channel_id=1, source_target_pairs={{0,192},{8,200},{16,208},{24,216},{32,224},{40,232},{48,240},{56,2... | collective-permute-start | bytes 393224 | tf_op jit(solution)/shard_map/ppermute | solution.py:41
  120.6 9.0 %shard_map.92.refs_4_ = f32[768,512]{1,0:T(8,128)} custom-call(s32[6]{0:T(128)S(1)} %select_reduce_fusion.1.pick_ref, bf16[8,768,768]{2,1,0:T(8,128)(2,1)} %bitcast.30, bf16[768,512]{1,0:T(8,128)(2,1)S(1)} %get-tuple-element.36.refs_0_, bf16[768,512]{1,0:T(8,128)(2,1)} %collective-permute-done.6.refs_1_, bf16[768,512]{1,0:T(8,128)(2,1)S(1)} %collective-permute-done.refs_2_, ...), custom_call_target="tpu_custom_call" | custom-call | flops 3623878656 | bytes 11796480 | tf_op jit(solution)/shard_map/pallas_call | solution.py:155
  130.2 3.7 %collective-permute-done.20.refs_10_ = bf16[128,512]{1,0:T(8,128)(2,1)S(1)} collective-permute-done((bf16[128,512]{1,0:T(8,128)(2,1)}, bf16[128,512]{1,0:T(8,128)(2,1)S(1)}, u32[]{:S(2)}, u32[]{:S(2)}) %collective-permute-start.20) | collective-permute-done | bytes 131104 | tf_op jit(solution)/shard_map/ppermute | solution.py:41
  135.3 1.4 copy-done
  136.7 0.9 copy-done.5
  137.7 0.9 copy-done.8
  138.6 0.9 copy-done.10
  139.5 0.9 copy-done.12
  140.4 8.0 %shard_map.95 = f32[768,512]{1,0:T(8,128)} custom-call(s32[5]{0:T(128)S(1)} %pad_add_fusion.1.pick_ref, bf16[8,768,768]{2,1,0:T(8,128)(2,1)} %bitcast.31, bf16[768,512]{1,0:T(8,128)(2,1)S(1)} %collective-permute-done.1.refs_0_, bf16[768,512]{1,0:T(8,128)(2,1)} %collective-permute-done.3.refs_1_, bf16[768,512]{1,0:T(8,128)(2,1)} %collective-permute-done.4.refs_2_, ...), custom_call_target="tpu_custom_call" | custom-call | flops 2415919104 | bytes 7864320 | tf_op jit(solution)/shard_map/pallas_call | solution.py:195
  (88 shorter events, 13.5 us)
Async XLA Ops:
  0.0 67.5 %copy-start.28 = (s32[1,1,7]{2,1,0:T(1,128)S(1)}, s32[1,1,7]{2,1,0:T(1,128)}, u32[]{:S(2)}) copy-start(s32[1,1,7]{2,1,0:T(1,128)} %param.20) | copy-start | bytes 88
  0.0 58.7 %copy-start.29 = (s32[1,1,8]{2,1,0:T(1,128)S(1)}, s32[1,1,8]{2,1,0:T(1,128)}, u32[]{:S(2)}) copy-start(s32[1,1,8]{2,1,0:T(1,128)} %param.19) | copy-start | bytes 100
  0.7 0.9 copy-start.1
  1.6 1.1 copy-start.3
  2.7 0.8 copy-start.13
  4.7 36.8 %collective-permute-start = (bf16[768,512]{1,0:T(8,128)(2,1)S(1)}, bf16[768,512]{1,0:T(8,128)(2,1)S(1)}, u32[]{:S(2)}, u32[]{:S(2)}) collective-permute-start(bf16[768,512]{1,0:T(8,128)(2,1)S(1)} %get-tuple-element.36.refs_0_), channel_id=1, source_target_pairs={{0,16},{8,24},{16,32},{24,40},{32,48},{40,56},{48,64},{56,72},{64,... | collective-permute-start | bytes 2359304 | tf_op jit(solution)/shard_map/ppermute | solution.py:41
  8.8 34.1 %collective-permute-start.2 = (bf16[768,512]{1,0:T(8,128)(2,1)S(1)}, bf16[768,512]{1,0:T(8,128)(2,1)S(1)}, u32[]{:S(2)}, u32[]{:S(2)}) collective-permute-start(bf16[768,512]{1,0:T(8,128)(2,1)S(1)} %get-tuple-element.36.refs_0_), channel_id=1, source_target_pairs={{16,0},{24,8},{32,16},{40,24},{48,32},{56,40},{64,48},{72,56},{80,... | collective-permute-start | bytes 2359304 | tf_op jit(solution)/shard_map/ppermute | solution.py:41
  10.1 17.7 %collective-permute-start.12 = (bf16[128,512]{1,0:T(8,128)(2,1)S(1)}, bf16[128,512]{1,0:T(8,128)(2,1)S(1)}, u32[]{:S(2)}, u32[]{:S(2)}) collective-permute-start(bf16[128,512]{1,0:T(8,128)(2,1)S(1)} %get-tuple-element.38.refs_4_), channel_id=1, source_target_pairs={{0,16},{8,24},{16,32},{24,40},{32,48},{40,56},{48,0},{56,8},{64,80... | collective-permute-start | bytes 393224 | tf_op jit(solution)/shard_map/ppermute | solution.py:41
  12.3 21.6 %collective-permute-start.13 = (bf16[128,512]{1,0:T(8,128)(2,1)S(1)}, bf16[128,512]{1,0:T(8,128)(2,1)S(1)}, u32[]{:S(2)}, u32[]{:S(2)}) collective-permute-start(bf16[128,512]{1,0:T(8,128)(2,1)S(1)} %get-tuple-element.38.refs_4_), channel_id=1, source_target_pairs={{0,32},{8,40},{16,48},{24,56},{32,0},{40,8},{48,16},{56,24},{64,96... | collective-permute-start | bytes 393224 | tf_op jit(solution)/shard_map/ppermute | solution.py:41
  14.8 22.3 %collective-permute-start.14 = (bf16[128,512]{1,0:T(8,128)(2,1)S(1)}, bf16[128,512]{1,0:T(8,128)(2,1)S(1)}, u32[]{:S(2)}, u32[]{:S(2)}) collective-permute-start(bf16[128,512]{1,0:T(8,128)(2,1)S(1)} %get-tuple-element.38.refs_4_), channel_id=1, source_target_pairs={{0,48},{8,56},{16,0},{24,8},{32,16},{40,24},{48,32},{56,40},{64,11... | collective-permute-start | bytes 393224 | tf_op jit(solution)/shard_map/ppermute | solution.py:41
  27.8 3.4 %copy-start.15 = (bf16[128,512]{1,0:T(8,128)(2,1)}, bf16[128,512]{1,0:T(8,128)(2,1)S(1)}, u32[]{:S(2)}) copy-start(bf16[128,512]{1,0:T(8,128)(2,1)S(1)} %collective-permute-done.12.refs_5_) | copy-start | bytes 393220
  27.8 12.4 %collective-permute-start.15 = (bf16[128,512]{1,0:T(8,128)(2,1)S(1)}, bf16[128,512]{1,0:T(8,128)(2,1)S(1)}, u32[]{:S(2)}, u32[]{:S(2)}) collective-permute-start(bf16[128,512]{1,0:T(8,128)(2,1)S(1)} %get-tuple-element.38.refs_4_), channel_id=1, source_target_pairs={{0,8},{8,0},{16,24},{24,16},{32,40},{40,32},{48,56},{56,48},{64,72... | collective-permute-start | bytes 393224 | tf_op jit(solution)/shard_map/ppermute | solution.py:41
  33.9 7.6 %copy-start.17 = (bf16[128,512]{1,0:T(8,128)(2,1)}, bf16[128,512]{1,0:T(8,128)(2,1)S(1)}, u32[]{:S(2)}) copy-start(bf16[128,512]{1,0:T(8,128)(2,1)S(1)} %collective-permute-done.13.refs_6_) | copy-start | bytes 393220
  33.9 20.6 %collective-permute-start.9 = (bf16[912,128]{1,0:T(8,128)(2,1)S(1)}, bf16[912,128]{1,0:T(8,128)(2,1)}, u32[]{:S(2)}, u32[]{:S(2)}) collective-permute-start(bf16[912,128]{1,0:T(8,128)(2,1)S(1)} %fusion.1.refs_0_), channel_id=1, source_target_pairs={{0,64},{8,72},{16,80},{24,88},{32,96},{40,104},{48,112},{56,120},{... | collective-permute-start | bytes 700424 | tf_op jit(solution)/shard_map/ppermute | solution.py:41
  37.2 4.4 %copy-start.19 = (bf16[128,512]{1,0:T(8,128)(2,1)}, bf16[128,512]{1,0:T(8,128)(2,1)S(1)}, u32[]{:S(2)}) copy-start(bf16[128,512]{1,0:T(8,128)(2,1)S(1)} %collective-permute-done.14.refs_7_) | copy-start | bytes 393220
  37.2 18.4 %collective-permute-start.10 = (bf16[912,128]{1,0:T(8,128)(2,1)S(1)}, bf16[912,128]{1,0:T(8,128)(2,1)}, u32[]{:S(2)}, u32[]{:S(2)}) collective-permute-start(bf16[912,128]{1,0:T(8,128)(2,1)S(1)} %fusion.1.refs_0_), channel_id=1, source_target_pairs={{0,128},{8,136},{16,144},{24,152},{32,160},{40,168},{48,176},{56,1... | collective-permute-start | bytes 700424 | tf_op jit(solution)/shard_map/ppermute | solution.py:41
  40.8 15.3 %collective-permute-start.11 = (bf16[912,128]{1,0:T(8,128)(2,1)S(1)}, bf16[912,128]{1,0:T(8,128)(2,1)}, u32[]{:S(2)}, u32[]{:S(2)}) collective-permute-start(bf16[912,128]{1,0:T(8,128)(2,1)S(1)} %fusion.1.refs_0_), channel_id=1, source_target_pairs={{0,192},{8,200},{16,208},{24,216},{32,224},{40,232},{48,240},{56,2... | collective-permute-start | bytes 700424 | tf_op jit(solution)/shard_map/ppermute | solution.py:41
  41.6 17.3 %collective-permute-start.1 = (bf16[768,512]{1,0:T(8,128)(2,1)S(1)}, bf16[768,512]{1,0:T(8,128)(2,1)S(1)}, u32[]{:S(2)}, u32[]{:S(2)}) collective-permute-start(bf16[768,512]{1,0:T(8,128)(2,1)S(1)} %collective-permute-done.refs_2_), channel_id=1, source_target_pairs={{0,16},{8,24},{16,32},{24,40},{32,48},{40,56},{48,64},{56,72},{64,... | collective-permute-start | bytes 2359304 | tf_op jit(solution)/shard_map/ppermute | solution.py:41
  42.9 20.9 %collective-permute-start.3 = (bf16[768,512]{1,0:T(8,128)(2,1)S(1)}, bf16[768,512]{1,0:T(8,128)(2,1)}, u32[]{:S(2)}, u32[]{:S(2)}) collective-permute-start(bf16[768,512]{1,0:T(8,128)(2,1)S(1)} %collective-permute-done.2.refs_3_), channel_id=1, source_target_pairs={{16,0},{24,8},{32,16},{40,24},{48,32},{56,40},{64,48},{72,56},{80,... | collective-permute-start | bytes 2359304 | tf_op jit(solution)/shard_map/ppermute | solution.py:41
  44.2 36.1 %all-to-all-start = ((bf16[32,16,128]{2,1,0:T(8,128)(2,1)}), bf16[32,16,128]{2,1,0:T(8,128)(2,1)}, u32[]{:S(2)}, u32[]{:S(2)}) async-start(bf16[32,16,128]{2,1,0:T(8,128)(2,1)} %bitcast.29), calls=%async_computation | async-start | bytes 262144 | tf_op jit(solution)/shard_map/all_to_all | solution.py:254
  54.5 2.2 %collective-permute-start.16 = (bf16[128,512]{1,0:T(8,128)(2,1)}, bf16[128,512]{1,0:T(8,128)(2,1)}, u32[]{:S(2)}, u32[]{:S(2)}) collective-permute-start(bf16[128,512]{1,0:T(8,128)(2,1)} %copy-done.15), channel_id=1, source_target_pairs={{0,8},{8,0},{16,24},{24,16},{32,40},{40,32},{48,56},{56,48},{64,72... | collective-permute-start | bytes 393224 | tf_op jit(solution)/shard_map/ppermute | solution.py:41
  55.6 1.9 %collective-permute-start.17 = (bf16[128,512]{1,0:T(8,128)(2,1)}, bf16[128,512]{1,0:T(8,128)(2,1)}, u32[]{:S(2)}, u32[]{:S(2)}) collective-permute-start(bf16[128,512]{1,0:T(8,128)(2,1)} %copy-done.17), channel_id=1, source_target_pairs={{0,8},{8,0},{16,24},{24,16},{32,40},{40,32},{48,56},{56,48},{64,72... | collective-permute-start | bytes 393224 | tf_op jit(solution)/shard_map/ppermute | solution.py:41
  56.1 1.7 %collective-permute-start.18 = (bf16[128,512]{1,0:T(8,128)(2,1)}, bf16[128,512]{1,0:T(8,128)(2,1)}, u32[]{:S(2)}, u32[]{:S(2)}) collective-permute-start(bf16[128,512]{1,0:T(8,128)(2,1)} %copy-done.19), channel_id=1, source_target_pairs={{0,8},{8,0},{16,24},{24,16},{32,40},{40,32},{48,56},{56,48},{64,72... | collective-permute-start | bytes 393224 | tf_op jit(solution)/shard_map/ppermute | solution.py:41
  56.8 60.0 %collective-permute-start.6 = (bf16[768,512]{1,0:T(8,128)(2,1)S(1)}, bf16[768,512]{1,0:T(8,128)(2,1)}, u32[]{:S(2)}, u32[]{:S(2)}) collective-permute-start(bf16[768,512]{1,0:T(8,128)(2,1)S(1)} %get-tuple-element.36.refs_0_), channel_id=1, source_target_pairs={{0,8},{8,0},{16,24},{24,16},{32,40},{40,32},{48,56},{56,48},{64,72... | collective-permute-start | bytes 2359304 | tf_op jit(solution)/shard_map/ppermute | solution.py:41
  57.5 62.6 %collective-permute-start.7 = (bf16[768,512]{1,0:T(8,128)(2,1)S(1)}, bf16[768,512]{1,0:T(8,128)(2,1)}, u32[]{:S(2)}, u32[]{:S(2)}) collective-permute-start(bf16[768,512]{1,0:T(8,128)(2,1)S(1)} %collective-permute-done.refs_2_), channel_id=1, source_target_pairs={{0,8},{8,0},{16,24},{24,16},{32,40},{40,32},{48,56},{56,48},{64,72... | collective-permute-start | bytes 2359304 | tf_op jit(solution)/shard_map/ppermute | solution.py:41
  57.8 62.2 %collective-permute-start.8 = (bf16[768,512]{1,0:T(8,128)(2,1)S(1)}, bf16[768,512]{1,0:T(8,128)(2,1)}, u32[]{:S(2)}, u32[]{:S(2)}) collective-permute-start(bf16[768,512]{1,0:T(8,128)(2,1)S(1)} %collective-permute-done.2.refs_3_), channel_id=1, source_target_pairs={{0,8},{8,0},{16,24},{24,16},{32,40},{40,32},{48,56},{56,48},{64,72... | collective-permute-start | bytes 2359304 | tf_op jit(solution)/shard_map/ppermute | solution.py:41
  58.9 76.4 %collective-permute-start.4 = (bf16[768,512]{1,0:T(8,128)(2,1)S(1)}, bf16[768,512]{1,0:T(8,128)(2,1)}, u32[]{:S(2)}, u32[]{:S(2)}) collective-permute-start(bf16[768,512]{1,0:T(8,128)(2,1)S(1)} %collective-permute-done.1.refs_0_), channel_id=1, source_target_pairs={{8,0},{24,16},{40,32},{56,48},{72,64},{88,80},{104,96},{120,112},{... | collective-permute-start | bytes 2359304 | tf_op jit(solution)/shard_map/ppermute | solution.py:41
  63.8 71.5 %collective-permute-start.5 = (bf16[768,512]{1,0:T(8,128)(2,1)}, bf16[768,512]{1,0:T(8,128)(2,1)}, u32[]{:S(2)}, u32[]{:S(2)}) collective-permute-start(bf16[768,512]{1,0:T(8,128)(2,1)} %collective-permute-done.3.refs_1_), channel_id=1, source_target_pairs={{0,8},{16,24},{32,40},{48,56},{64,72},{80,88},{96,104},{112,120},{... | collective-permute-start | bytes 2359304 | tf_op jit(solution)/shard_map/ppermute | solution.py:41
  81.8 20.2 %all-to-all-start.1 = ((bf16[8,16,128]{2,1,0:T(8,128)(2,1)}), bf16[8,16,128]{2,1,0:T(8,128)(2,1)S(1)}, u32[]{:S(2)}, u32[]{:S(2)}) async-start(bf16[8,16,128]{2,1,0:T(8,128)(2,1)} %broadcast_in_dim.48), calls=%async_computation.1 | async-start | bytes 65536 | tf_op jit(solution)/shard_map/all_to_all | solution.py:256
  92.6 0.9 copy-start.16
  93.6 0.9 copy-start.18
  94.5 0.9 copy-start.20
  95.4 0.9 copy-start.22
  99.3 0.7 copy-start.4
  100.7 0.7 copy-start.26
  102.0 1.0 copy-start.6
  103.0 0.7 copy-start.24
  105.1 30.1 %all-to-all-start.2 = ((bf16[32,16,128]{2,1,0:T(8,128)(2,1)}), bf16[32,16,128]{2,1,0:T(8,128)(2,1)S(1)}, u32[]{:S(2)}, u32[]{:S(2)}) async-start(bf16[32,16,128]{2,1,0:T(8,128)(2,1)} %broadcast_in_dim.49), calls=%async_computation.2 | async-start | bytes 262144 | tf_op jit(solution)/shard_map/all_to_all | solution.py:261
  116.8 12.8 %collective-permute-start.19 = (bf16[128,512]{1,0:T(8,128)(2,1)}, bf16[128,512]{1,0:T(8,128)(2,1)S(1)}, u32[]{:S(2)}, u32[]{:S(2)}) collective-permute-start(bf16[128,512]{1,0:T(8,128)(2,1)} %copy-done.27), channel_id=1, source_target_pairs={{0,192},{8,200},{16,208},{24,216},{32,224},{40,232},{48,240},{56,2... | collective-permute-start | bytes 393224 | tf_op jit(solution)/shard_map/ppermute | solution.py:41
  120.1 13.9 %collective-permute-start.20 = (bf16[128,512]{1,0:T(8,128)(2,1)}, bf16[128,512]{1,0:T(8,128)(2,1)S(1)}, u32[]{:S(2)}, u32[]{:S(2)}) collective-permute-start(bf16[128,512]{1,0:T(8,128)(2,1)} %copy-done.26), channel_id=1, source_target_pairs={{0,128},{8,136},{16,144},{24,152},{32,160},{40,168},{48,176},{56,1... | collective-permute-start | bytes 393224 | tf_op jit(solution)/shard_map/ppermute | solution.py:41
  120.1 14.5 %collective-permute-start.21 = (bf16[128,512]{1,0:T(8,128)(2,1)}, bf16[128,512]{1,0:T(8,128)(2,1)S(1)}, u32[]{:S(2)}, u32[]{:S(2)}) collective-permute-start(bf16[128,512]{1,0:T(8,128)(2,1)} %copy-done.25), channel_id=1, source_target_pairs={{0,64},{8,72},{16,80},{24,88},{32,96},{40,104},{48,112},{56,120},{... | collective-permute-start | bytes 393224 | tf_op jit(solution)/shard_map/ppermute | solution.py:41
  120.6 14.7 %copy-start.2 = (bf16[1,1,768,128]{3,2,1,0:T(8,128)(2,1)S(1)}, bf16[1,1,768,128]{3,2,1,0:T(8,128)(2,1)}, u32[]{:S(2)}) copy-start(bf16[1,1,768,128]{3,2,1,0:T(8,128)(2,1)} %param.15) | copy-start | bytes 589828
  120.6 14.7 %copy-start.14 = (bf16[1,1,128,128]{3,2,1,0:T(8,128)(2,1)S(1)}, bf16[1,1,128,128]{3,2,1,0:T(8,128)(2,1)}, u32[]{:S(2)}) copy-start(bf16[1,1,128,128]{3,2,1,0:T(8,128)(2,1)} %param.16) | copy-start | bytes 98308
  135.3 1.4 copy-start
  136.7 0.9 copy-start.5
  137.7 0.9 copy-start.8
  138.6 0.9 copy-start.10
  139.5 0.9 copy-start.12
  (7 other events, 4.6 us)

commit v2 on v0

v2 whole, which is shorter than its diff:
```python
import jax
import jax.numpy as jnp
from jax import lax
from jax.experimental import pallas as pl
from jax.experimental.pallas import tpu as pltpu
from jax.sharding import PartitionSpec as P

Z, Y, CORES = 4, 4, 2
ROW = Y * CORES
CHIPS = Z * Y
X, HALVES = 4, 2
F32, BF16 = jnp.float32, jnp.bfloat16
LIMIT, FULL = 40 * 1024 * 1024, 60 * 1024 * 1024


def chip_step(distance):
    return [
        (p * 2 + c, (p + distance) * 2 + c)
        for p in range(CHIPS)
        for c in range(2)
        if 0 <= p + distance < CHIPS
    ]


def seat_of(z, y, c):
    return z * ROW + y * 2 + c


def turn(dz, dy):
    return [
        (seat_of(z, y, c), seat_of((z + dz) % Z, (y + dy) % Y, c))
        for z in range(Z)
        for y in range(Y)
        for c in range(2)
    ]


SWAP = [(i, i ^ 1) for i in range(2 * CHIPS)]
TO_FIRST = [(2 * p + 1, 2 * p) for p in range(CHIPS)]
TO_SECOND = [(2 * p, 2 * p + 1) for p in range(CHIPS)]


def send(name, block, route, axis="leaf"):
    with jax.named_scope(name):
        return lax.ppermute(block, axis, route)


def exchange(name, blocks, groups, axis="leaf"):
    with jax.named_scope(name):
        return lax.all_to_all(blocks, axis, 0, 0, tiled=True, axis_index_groups=groups)


def after(blocks, other):
    return lax.optimization_barrier([*blocks, other])[:-1]


def dot(a, b, dims=((1,), (0,))):
    return lax.dot_general(a, b, (dims, ((), ())), preferred_element_type=F32)


def cost(flops, moved):
    return pl.CostEstimate(flops=int(flops), bytes_accessed=int(moved), transcendentals=0)


ANY = pl.BlockSpec(memory_space=pl.ANY)
SMEM = pl.BlockSpec(memory_space=pltpu.SMEM)


def shape(dims, dtype=BF16):
    return jax.ShapeDtypeStruct(dims, dtype)


def call(kernel, scalars, arrays, outs, scratch, copies, price, limit=LIMIT):
    return pl.pallas_call(
        kernel,
        out_shape=outs,
        in_specs=[SMEM] * len(scalars) + [ANY] * len(arrays),
        out_specs=[ANY] * len(outs),
        scratch_shapes=[*scratch, pltpu.SemaphoreType.DMA((copies,))],
        compiler_params=pltpu.CompilerParams(vmem_limit_bytes=limit),
        cost_estimate=price,
    )(*scalars, *arrays)


class Mover:
    def __init__(self, sems):
        self.sems, self.used = sems, 0

    def __call__(self, src, dst):
        copy = pltpu.make_async_copy(src, dst, self.sems.at[self.used])
        self.used += 1
        copy.start()
        return copy

    def later(self, src, dst):
        copy = pltpu.make_async_copy(src, dst, self.sems.at[self.used])
        self.used += 1
        return copy


def coeff_kernel(count_ref, vec, basis, transfer, masked, coeffs, up, v, b, t, c, u, sems):
    move = Mover(sems)
    arrive = [move(vec, v), move(basis, b), move(transfer, t)]
    arrive[0].wait()
    rows = lax.broadcasted_iota(jnp.int32, v.shape, 0)
    v[...] = jnp.where(rows < count_ref[0], v[...].astype(F32), 0.0).astype(BF16)
    leave = [move(v, masked)]
    arrive[1].wait()
    c[...] = dot(b[...], v[...], ((0,), (0,))).astype(BF16)
    leave.append(move(c, coeffs))
    arrive[2].wait()
    u[...] = dot(t[...], c[...], ((0,), (0,))).T.astype(BF16)
    leave.append(move(u, up))
    for copy in leave:
        copy.wait()


def coefficients(count, vec, basis, transfer):
    (rows, vecs), rank = vec.shape, basis.shape[1]
    return call(
        coeff_kernel,
        [count],
        [vec, basis, transfer],
        [shape((rows, vecs)), shape((rank, vecs)), shape((vecs, rank))],
        [
            pltpu.VMEM((rows, vecs), BF16),
            pltpu.VMEM((rows, rank), BF16),
            pltpu.VMEM((rank, rank), BF16),
            pltpu.VMEM((rank, vecs), BF16),
            pltpu.VMEM((vecs, rank), BF16),
        ],
        6,
        cost(2 * rows * rank * vecs, 2 * rows * vecs * 2),
        FULL,
    )


def parent_kernel(pieces, *refs):
    out, terms, total, sems = refs[-4:]
    move = Mover(sems)
    move(pieces, terms).wait()
    total[...] = jnp.sum(terms[...].astype(F32), axis=0).astype(BF16)
    leave = [move(total, out.at[c]) for c in range(X * HALVES)]
    for copy in leave:
        copy.wait()


def parents_of(pieces, before):
    leaves, width, rank = pieces.shape
    return call(
        parent_kernel,
        [],
        [pieces, *before],
        [shape((X * HALVES, width, rank))],
        [pltpu.VMEM(pieces.shape, BF16), pltpu.VMEM((width, rank), BF16)],
        1 + X * HALVES,
        cost(leaves * width * rank, leaves * width * rank * 2),
    )[0]


def top_kernel(mine_ref, coupling, parents_in, *refs):
    out, matrices, parents, value, sems = refs[-5:]
    move = Mover(sems)
    arrive = [move(coupling, matrices), move(parents_in, parents)]
    for copy in arrive:
        copy.wait()
    count = matrices.shape[0]
    value[...] = sum(
        dot(parents[i], matrices[(i + count - 1 - mine_ref[0]) & (count - 1)], ((1,), (1,)))
        for i in range(count)
    ).astype(BF16)
    leave = [move(value, out.at[i]) for i in range(out.shape[0])]
    for copy in leave:
        copy.wait()


def top_field(mine, coupling, parents, copies, before):
    _, width, rank = parents.shape
    return call(
        top_kernel,
        [mine],
        [coupling, parents, *before],
        [shape((copies, width, rank))],
        [
            pltpu.VMEM(coupling.shape, BF16),
            pltpu.VMEM(parents.shape, BF16),
            pltpu.VMEM((width, rank), BF16),
        ],
        copies + 2,
        cost(2 * 8 * width * rank * rank, 8 * rank * rank * 2),
    )[0]


def join_kernel(*refs):
    blocks, out, held, sems = refs[:Z], refs[Z], refs[Z + 1], refs[Z + 2]
    move = Mover(sems)
    arrive = [move(blocks[z], held.at[z]) for z in range(Z)]
    leave = []
    for z in range(Z):
        arrive[z].wait()
        leave.append(move(held.at[z], out.at[z]))
    for copy in leave:
        copy.wait()


def joined(blocks):
    dims = (Z, *blocks[0].shape)
    return call(join_kernel, [], blocks, [shape(dims)], [pltpu.VMEM(dims, BF16)], 2 * Z, cost(0, 0))[0]


def far_kernel(me_ref, far_ref, coupling, *refs):
    stores, (out, matrices, blocks, total, sems) = refs[:ROW], refs[-5:]
    move = Mover(sems)
    me = me_ref[0]
    arrive = move(coupling, matrices)
    copies = []
    for m in range(matrices.shape[0]):
        far = far_ref[m]
        back_z = (me // ROW - far // ROW) & (Z - 1)
        back_y = ((me >> 1) - (far >> 1)) & (Y - 1)
        store = ((far ^ me) & 1) * Y + back_y
        for i, source in enumerate(stores):
            copy = move.later(source.at[back_z], blocks.at[m])
            move.used -= 1
            pl.when(store == i)(copy.start)
        copies.append(move.later(stores[0].at[0], blocks.at[m]))
    arrive.wait()
    for m, copy in enumerate(copies):
        copy.wait()
        value = dot(matrices[m], blocks[m])
        if m:
            total[...] += value
        else:
            total[...] = value
    move(total, out).wait()


def far_field(me, far, coupling, stores, before):
    count, rank, _ = coupling.shape
    vecs = stores[0].shape[2]
    return call(
        far_kernel,
        [me, far],
        [coupling, *stores, *before],
        [shape((rank, vecs), F32)],
        [
            pltpu.VMEM(coupling.shape, BF16),
            pltpu.VMEM((count, rank, vecs), BF16),
            pltpu.VMEM((rank, vecs), F32),
        ],
        count + 2,
        cost(2 * count * rank * rank * vecs, count * rank * vecs * 2),
        FULL,
    )[0]


def tile_for(near_ref, offset):
    found = jnp.int32(-1)
    for k in range(near_ref.shape[0]):
        found = jnp.where(near_ref[k] == offset, jnp.int32(k), found)
    return found


class Products:
    def __init__(self, move, picks, tiles, sources, tile_slots, source_slots):
        self.picks, self.tiles, self.sources = picks, tile_slots, source_slots
        self.copies = []
        for s, pick in enumerate(picks):
            pair = [
                move.later(tiles.at[jnp.maximum(pick, 0)], tile_slots.at[s]),
                move.later(sources[s], source_slots.at[s]),
            ]
            self.copies.append(pair)

            @pl.when(pick >= 0)
            def begin(pair=pair):
                for copy in pair:
                    copy.start()

    def add_to(self, total):
        for s, pick in enumerate(self.picks):

            @pl.when(pick >= 0)
            def add(s=s):
                for copy in self.copies[s]:
                    copy.wait()
                total[...] += dot(self.tiles[s], self.sources[s])


FIRST, LAST = 6, 4


def near_first_kernel(me_ref, near_ref, tiles, *refs):
    sources, (out, tile_slots, source_slots, total, sems) = refs[:FIRST], refs[-5:]
    side = 1 - 2 * (me_ref[0] & 1)
    picks = [tile_for(near_ref, at) for at in (0, side, -2, 2, side - 2, side + 2)]
    move = Mover(sems)
    products = Products(move, picks, tiles, sources, tile_slots, source_slots)
    total[...] = jnp.zeros_like(total)
    products.add_to(total)
    move(total, out).wait()


def near_first(me, near, tiles, sources, before):
    rows, vecs = sources[0].shape
    return call(
        near_first_kernel,
        [me, near],
        [tiles, *sources, *before],
        [shape((rows, vecs), F32)],
        [
            pltpu.VMEM((FIRST, rows, rows), BF16),
            pltpu.VMEM((FIRST, rows, vecs), BF16),
            pltpu.VMEM((rows, vecs), F32),
        ],
        2 * FIRST + 1,
        cost(2 * FIRST * rows * rows * vecs, FIRST * rows * (rows + vecs) * 2),
        FULL,
    )[0]


def near_last_kernel(me_ref, near_ref, count_ref, tiles, *refs):
    sources, refs = refs[:LAST], refs[LAST:]
    near, basis, transfer, far_in, field_in, out = refs[:6]
    tile_slots, source_slots, total, b, t, local, field, sems = refs[6:]
    core = me_ref[0] & 1
    absent = jnp.int32(99)
    places = (-4, 4, jnp.where(core == 0, -3, absent), jnp.where(core == 1, 3, absent))
    picks = [tile_for(near_ref, at) for at in places]
    move = Mover(sems)
    arrive = [move(transfer, t), move(far_in, local), move(field_in, field)]
    arrive += [move(near, total), move(basis, b)]
    products = Products(move, picks, tiles, sources, tile_slots, source_slots)
    for copy in arrive:
        copy.wait()
    local[...] += dot(t[...], field[...], ((1,), (1,)))
    total[...] += dot(b[...], local[...].astype(BF16))
    products.add_to(total)
    live = lax.broadcasted_iota(jnp.int32, total.shape, 0) < count_ref[0]
    total[...] = jnp.where(live, total[...], 0.0)
    move(total, out).wait()


def near_last(me, near_list, count, tiles, sources, near, basis, transfer, far, field):
    (rows, vecs), rank = sources[0].shape, basis.shape[1]
    return call(
        near_last_kernel,
        [me, near_list, count],
        [tiles, *sources, near, basis, transfer, far, field],
        [shape((rows, vecs), F32)],
        [
            pltpu.VMEM((LAST, rows, rows), BF16),
            pltpu.VMEM((LAST, rows, vecs), BF16),
            pltpu.VMEM((rows, vecs), F32),
            pltpu.VMEM((rows, rank), BF16),
            pltpu.VMEM((rank, rank), BF16),
            pltpu.VMEM((rank, vecs), F32),
            pltpu.VMEM((vecs, rank), BF16),
        ],
        2 * LAST + 6,
        cost(2 * LAST * rows * rows * vecs, LAST * rows * (rows + vecs) * 2),
        FULL,
    )[0]


def body(
    vectors,
    near_tiles,
    leaf_basis,
    transfer,
    coupling,
    top_coupling,
    near_list,
    far_list,
    row_counts,
):
    leaf = lax.axis_index("leaf").astype(jnp.int32)
    cluster = lax.axis_index("top").astype(jnp.int32)
    me = leaf[None]
    leaves, clusters = lax.axis_size("leaf"), lax.axis_size("top")
    basis, nested, tiles = leaf_basis[0, 0], transfer[0, 0], near_tiles[0, 0]
    near_offsets, far, count = near_list[0, 0], far_list[0, 0], row_counts[0]
    rank, vecs = nested.shape[0], vectors.shape[3]

    masked, coeffs, up = coefficients(count, vectors[0, 0], basis, nested)

    pieces = exchange("rises", up, None).reshape(leaves, vecs // leaves, rank)
    parent = parents_of(pieces, [])
    parents = exchange("parents", parent, None, "top")

    by_z = [coeffs] + [send(f"coeffs_z{d}", coeffs, turn(d, 0)) for d in range(1, Z)]
    column = joined(after(by_z, pieces))
    stores = [column] + [send(f"coeffs_y{d}", column, turn(0, d)) for d in range(1, Y)]

    beside = send("own_swap", masked, SWAP)
    (masked,) = after([masked], by_z[-1])
    from_low = send("low_hop", masked, chip_step(1))
    from_high = send("high_hop", masked, chip_step(-1))

    field = top_field(cluster[None], top_coupling[0], parents, leaves, [from_low, from_high])
    from_low, from_high = after([from_low, from_high], parents)
    from_low2 = send("low_hop2", from_low, chip_step(1))
    from_high2 = send("high_hop2", from_high, chip_step(-1))
    low_beside = send("low_swap", from_low, SWAP)
    high_beside = send("high_swap", from_high, SWAP)
    near = near_first(
        me,
        near_offsets,
        tiles,
        [masked, beside, from_low, from_high, low_beside, high_beside],
        [field],
    )
    stores += [send(f"coeffs_swap{i}", block, SWAP) for i, block in enumerate(after(stores, parents))]
    field = exchange("fields", field, None).reshape(vecs, rank)
    far_sum = far_field(me, far, coupling[0, 0], stores, [near, field])
    from_low2, from_high2 = after([from_low2, from_high2], far_sum)
    low2_beside = send("low2_swap", from_low2, TO_FIRST)
    high2_beside = send("high2_swap", from_high2, TO_SECOND)
    result = near_last(
        me,
        near_offsets,
        count,
        tiles,
        [from_low2, from_high2, low2_beside, high2_beside],
        near,
        basis,
        nested,
        far_sum,
        field,
    )
    return result[None, None]


def solution(mesh):
    in_specs = (
        P("top", "leaf", None, None),
        P("top", "leaf", None, None, None),
        P("top", "leaf", None, None),
        P("top", "leaf", None, None),
        P("top", "leaf", None, None, None),
        P("top", None, None, None),
        P("top", "leaf", None),
        P("top", "leaf", None),
        P("top", "leaf"),
    )
    out_specs = P("top", "leaf", None, None)
    return jax.shard_map(body, mesh=mesh, in_specs=in_specs, out_specs=out_specs, check_vma=False)
```

time: 302 us -> 123 us (0.41)
  the two profiles are of different devices: /device:TPU:49 before, /device:TPU:1 now
where the time goes in v2:
time: 123 us
  starting transfers between devices  52 us (42%)
  waiting for transfers between devices  26.8 us (22%)
  Pallas kernels  22.6 us (18%)
  blocking collectives  17.3 us (14%)
  local copies, waits for them, and re-layouts  3.07 us (2%)
    ppermute x19, starting transfers between devices, send(): return lax.ppermute(block, axis, route)  33.9 us
    pallas_call x7, Pallas kernels, call(): pl.pallas_call(kernel, out_shape=outs, in_specs=[SMEM] * len(scalars) + [...  22.6 us
    ppermute x19, waiting for transfers between devices, send(): return lax.ppermute(block, axis, route)  19.4 us
    all_to_all x2, starting transfers between devices, exchange(): lax.all_to_all(blocks, axis, 0, 0, tiled=True, axis_index_groups=groups)  18.1 us
    all_to_all x1, blocking collectives, exchange(): lax.all_to_all(blocks, axis, 0, 0, tiled=True, axis_index_groups=groups)  17.3 us
    all_to_all x2, waiting for transfers between devices, exchange(): lax.all_to_all(blocks, axis, 0, 0, tiled=True, axis_index_groups=groups)  7.47 us
    unnamed x26, local copies, waits for them, and re-layouts  3.07 us
  transfers between devices with their start and end apart: 21, of which 6 were waited for; matrix products, arithmetic and copies ran while one was open for 0% of the time, Pallas kernels for 12%

profile of v2, /device:TPU:1, one launch (start us, length us, event | category | flops | bytes accessed | tf_op | source)
XLA Modules:
  0.0 122.9 jit_solution(10879572185189189340)
XLA Ops:
  0.7 2.6 %shard_map.91 = (bf16[768,512]{1,0:T(8,128)(2,1)}, bf16[128,512]{1,0:T(8,128)(2,1)}, bf16[512,128]{1,0:T(8,128)(2,1)}) custom-call(s32[1]{0:T(128)} %bitcast.14.count_ref, bf16[768,512]{1,0:T(8,128)(2,1)} %bitcast.23, bf16[768,128]{1,0:T(8,128)(2,1)} %bitcast.21, bf16[128,128]{1,0:T(8,128)(2,1)} %bitcast.25), custom_call_target="tpu_custom_call" | custom-call | flops 100663296 | bytes 1572864 | tf_op jit(solution)/shard_map/pallas_call | solution.py:74
  3.3 5.2 %collective-permute-start = (bf16[128,512]{1,0:T(8,128)(2,1)}, bf16[128,512]{1,0:T(8,128)(2,1)S(1)}, u32[]{:S(2)}, u32[]{:S(2)}) collective-permute-start(bf16[128,512]{1,0:T(8,128)(2,1)} %get-tuple-element.27.refs_0_), channel_id=1, source_target_pairs={{0,192},{8,200},{16,208},{24,216},{32,224},{40,232},{48,240},{56,2... | collective-permute-start | bytes 393224 | tf_op jit(solution)/shard_map/coeffs_z3/ppermute | solution.py:45
  8.5 2.5 %collective-permute-done.refs_3_ = bf16[128,512]{1,0:T(8,128)(2,1)S(1)} collective-permute-done((bf16[128,512]{1,0:T(8,128)(2,1)}, bf16[128,512]{1,0:T(8,128)(2,1)S(1)}, u32[]{:S(2)}, u32[]{:S(2)}) %collective-permute-start) | collective-permute-done | bytes 131104 | tf_op jit(solution)/shard_map/coeffs_z3/ppermute | solution.py:45
  11.0 3.2 %collective-permute-start.1 = (bf16[768,512]{1,0:T(8,128)(2,1)}, bf16[768,512]{1,0:T(8,128)(2,1)S(1)}, u32[]{:S(2)}, u32[]{:S(2)}) collective-permute-start(bf16[768,512]{1,0:T(8,128)(2,1)} %get-tuple-element.23.refs_0_), channel_id=1, source_target_pairs={{0,16},{8,24},{16,32},{24,40},{32,48},{40,56},{48,64},{56,72},{64,... | collective-permute-start | bytes 2359304 | tf_op jit(solution)/shard_map/low_hop/ppermute | solution.py:45
  14.2 1.3 %collective-permute-start.2 = (bf16[768,512]{1,0:T(8,128)(2,1)}, bf16[768,512]{1,0:T(8,128)(2,1)S(1)}, u32[]{:S(2)}, u32[]{:S(2)}) collective-permute-start(bf16[768,512]{1,0:T(8,128)(2,1)} %get-tuple-element.23.refs_0_), channel_id=1, source_target_pairs={{16,0},{24,8},{32,16},{40,24},{48,32},{56,40},{64,48},{72,56},{80,... | collective-permute-start | bytes 2359304 | tf_op jit(solution)/shard_map/high_hop/ppermute | solution.py:45
  15.5 11.1 %all-to-all-start = ((bf16[32,16,128]{2,1,0:T(8,128)(2,1)}), bf16[32,16,128]{2,1,0:T(8,128)(2,1)S(1)}, u32[]{:S(2)}, u32[]{:S(2)}) async-start(bf16[32,16,128]{2,1,0:T(8,128)(2,1)} %bitcast.27), calls=%async_computation | async-start | bytes 262144 | tf_op jit(solution)/shard_map/rises/all_to_all | solution.py:50
  26.7 1.5 %collective-permute-start.5 = (bf16[128,512]{1,0:T(8,128)(2,1)}, bf16[128,512]{1,0:T(8,128)(2,1)S(1)}, u32[]{:S(2)}, u32[]{:S(2)}) collective-permute-start(bf16[128,512]{1,0:T(8,128)(2,1)} %get-tuple-element.27.refs_0_), channel_id=1, source_target_pairs={{0,64},{8,72},{16,80},{24,88},{32,96},{40,104},{48,112},{56,120},{... | collective-permute-start | bytes 393224 | tf_op jit(solution)/shard_map/coeffs_z1/ppermute | solution.py:45
  28.1 2.1 %collective-permute-start.6 = (bf16[128,512]{1,0:T(8,128)(2,1)}, bf16[128,512]{1,0:T(8,128)(2,1)S(1)}, u32[]{:S(2)}, u32[]{:S(2)}) collective-permute-start(bf16[128,512]{1,0:T(8,128)(2,1)} %get-tuple-element.27.refs_0_), channel_id=1, source_target_pairs={{0,128},{8,136},{16,144},{24,152},{32,160},{40,168},{48,176},{56,1... | collective-permute-start | bytes 393224 | tf_op jit(solution)/shard_map/coeffs_z2/ppermute | solution.py:45
  30.2 13.8 %collective-permute-done.5.refs_1_ = bf16[128,512]{1,0:T(8,128)(2,1)S(1)} collective-permute-done((bf16[128,512]{1,0:T(8,128)(2,1)}, bf16[128,512]{1,0:T(8,128)(2,1)S(1)}, u32[]{:S(2)}, u32[]{:S(2)}) %collective-permute-start.5) | collective-permute-done | bytes 131104 | tf_op jit(solution)/shard_map/coeffs_z1/ppermute | solution.py:45
  44.0 0.3 all-to-all-done.pieces
  44.4 0.9 copy-done.4
  45.3 1.4 %shard_map.93.refs_0_ = bf16[4,128,512]{2,1,0:T(8,128)(2,1)S(1)} custom-call(bf16[128,512]{1,0:T(8,128)(2,1)S(1)} %copy-done.4, bf16[128,512]{1,0:T(8,128)(2,1)S(1)} %collective-permute-done.5.refs_1_, bf16[128,512]{1,0:T(8,128)(2,1)S(1)} %collective-permute-done.6.refs_2_, bf16[128,512]{1,0:T(8,128)(2,1)S(1)} %collective-permute-done.refs_3_), custom_call_target="tpu_custom_call" | custom-call | tf_op jit(solution)/shard_map/pallas_call | solution.py:74
  46.7 0.9 collective-permute-start.7
  47.6 3.3 %collective-permute-start.8 = (bf16[4,128,512]{2,1,0:T(8,128)(2,1)S(1)}, bf16[4,128,512]{2,1,0:T(8,128)(2,1)}, u32[]{:S(2)}, u32[]{:S(2)}) collective-permute-start(bf16[4,128,512]{2,1,0:T(8,128)(2,1)S(1)} %shard_map.93.refs_0_), channel_id=1, source_target_pairs={{0,32},{8,40},{16,48},{24,56},{32,0},{40,8},{48,16},{56,24},{64,96... | collective-permute-start | bytes 1572872 | tf_op jit(solution)/shard_map/coeffs_y2/ppermute | solution.py:45
  50.9 1.7 %collective-permute-start.9 = (bf16[4,128,512]{2,1,0:T(8,128)(2,1)S(1)}, bf16[4,128,512]{2,1,0:T(8,128)(2,1)}, u32[]{:S(2)}, u32[]{:S(2)}) collective-permute-start(bf16[4,128,512]{2,1,0:T(8,128)(2,1)S(1)} %shard_map.93.refs_0_), channel_id=1, source_target_pairs={{0,48},{8,56},{16,0},{24,8},{32,16},{40,24},{48,32},{56,40},{64,11... | collective-permute-start | bytes 1572872 | tf_op jit(solution)/shard_map/coeffs_y3/ppermute | solution.py:45
  52.6 0.0 collective-permute-done.1.refs_0_.refs_2_
  52.7 3.3 %collective-permute-start.14 = (bf16[768,512]{1,0:T(8,128)(2,1)}, bf16[768,512]{1,0:T(8,128)(2,1)S(1)}, u32[]{:S(2)}, u32[]{:S(2)}) collective-permute-start(bf16[768,512]{1,0:T(8,128)(2,1)} %get-tuple-element.23.refs_0_), channel_id=1, source_target_pairs={{0,8},{8,0},{16,24},{24,16},{32,40},{40,32},{48,56},{56,48},{64,72... | collective-permute-start | bytes 2359304 | tf_op jit(solution)/shard_map/own_swap/ppermute | solution.py:45
  55.9 0.3 shard_map.92
  56.2 17.3 %all_to_all.19.parents_in = bf16[8,16,128]{2,1,0:T(8,128)(2,1)S(1)} all-to-all(bf16[8,16,128]{2,1,0:T(8,128)(2,1)S(1)} %shard_map.92), channel_id=1, replica_groups=mesh['leaf'=32,'top'=8] {'top'}, dimensions={0} | all-to-all | bytes 65536 | tf_op jit(solution)/shard_map/parents/all_to_all | solution.py:50
  73.5 1.5 %collective-permute-start.15 = (bf16[768,512]{1,0:T(8,128)(2,1)S(1)}, bf16[768,512]{1,0:T(8,128)(2,1)S(1)}, u32[]{:S(2)}, u32[]{:S(2)}) collective-permute-start(bf16[768,512]{1,0:T(8,128)(2,1)S(1)} %collective-permute-done.1.refs_0_.refs_2_), channel_id=1, source_target_pairs={{0,8},{8,0},{16,24},{24,16},{32,40},{40,32},{48,56},{56,48},{64,72... | collective-permute-start | bytes 2359304 | tf_op jit(solution)/shard_map/low_swap/ppermute | solution.py:45
  75.0 0.1 collective-permute-start.16
  75.1 0.0 collective-permute-done.8.refs_2_
  75.1 0.0 collective-permute-done.9.refs_3_
  75.1 0.4 collective-permute-start.10
  75.5 2.6 %collective-permute-start.3 = (bf16[768,512]{1,0:T(8,128)(2,1)S(1)}, bf16[768,512]{1,0:T(8,128)(2,1)S(1)}, u32[]{:S(2)}, u32[]{:S(2)}) collective-permute-start(bf16[768,512]{1,0:T(8,128)(2,1)S(1)} %collective-permute-done.1.refs_0_.refs_2_), channel_id=1, source_target_pairs={{0,16},{8,24},{16,32},{24,40},{32,48},{40,56},{48,64},{56,72},{64,... | collective-permute-start | bytes 2359304 | tf_op jit(solution)/shard_map/low_hop2/ppermute | solution.py:45
  78.1 0.0 collective-permute-done.14.refs_1_
  78.2 1.3 %collective-permute-start.4 = (bf16[768,512]{1,0:T(8,128)(2,1)S(1)}, bf16[768,512]{1,0:T(8,128)(2,1)}, u32[]{:S(2)}, u32[]{:S(2)}) collective-permute-start(bf16[768,512]{1,0:T(8,128)(2,1)S(1)} %collective-permute-done.2.refs_1_.refs_3_), channel_id=1, source_target_pairs={{16,0},{24,8},{32,16},{40,24},{48,32},{56,40},{64,48},{72,56},{80,... | collective-permute-start | bytes 2359304 | tf_op jit(solution)/shard_map/high_hop2/ppermute | solution.py:45
  79.5 0.0 collective-permute-done.10.refs_4_
  79.5 0.5 collective-permute-start.11
  80.0 0.0 collective-permute-done.15.refs_4_
  80.0 0.1 collective-permute-start.12
  80.1 0.0 collective-permute-done.16.refs_5_
  80.1 0.5 collective-permute-start.13
  80.6 0.3 copy-done.8
  80.9 0.3 copy-done.9
  81.2 1.3 %shard_map.94.refs_6_ = bf16[32,16,128]{2,1,0:T(8,128)(2,1)} custom-call(s32[1]{0:T(128)} %bitcast.10.mine_ref, bf16[8,128,128]{2,1,0:T(8,128)(2,1)S(1)} %bitcast.16, bf16[8,16,128]{2,1,0:T(8,128)(2,1)S(1)} %all_to_all.19.parents_in, bf16[768,512]{1,0:T(8,128)(2,1)S(1)} %collective-permute-done.1.refs_0_.refs_2_, ...), custom_call_target="tpu_custom_call" | custom-call | flops 4194304 | bytes 262144 | tf_op jit(solution)/shard_map/pallas_call | solution.py:74
  82.5 7.0 %all-to-all-start.2 = ((bf16[32,16,128]{2,1,0:T(8,128)(2,1)}), bf16[32,16,128]{2,1,0:T(8,128)(2,1)S(1)}, u32[]{:S(2)}, u32[]{:S(2)}) async-start(bf16[32,16,128]{2,1,0:T(8,128)(2,1)} %shard_map.94.refs_6_), calls=%async_computation.2 | async-start | bytes 262144 | tf_op jit(solution)/shard_map/fields/all_to_all | solution.py:50
  89.6 8.3 %shard_map.95.refs_8_.refs_4_ = f32[768,512]{1,0:T(8,128)} custom-call(s32[1]{0:T(128)} %bitcast.me_ref, s32[8]{0:T(128)} %bitcast.28, bf16[8,768,768]{2,1,0:T(8,128)(2,1)} %bitcast.17, bf16[768,512]{1,0:T(8,128)(2,1)} %get-tuple-element.23.refs_0_, bf16[768,512]{1,0:T(8,128)(2,1)} %copy-done.7, bf16[768,512]{1,0:T(8,128)(2,1)} %copy-done, ...), custom_call_target="tpu_custom_call" | custom-call | flops 3623878656 | bytes 11796480 | tf_op jit(solution)/shard_map/pallas_call | solution.py:74
  97.8 7.1 %all-to-all-done.2 = bf16[32,16,128]{2,1,0:T(8,128)(2,1)S(1)} async-done(((bf16[32,16,128]{2,1,0:T(8,128)(2,1)}), bf16[32,16,128]{2,1,0:T(8,128)(2,1)S(1)}, u32[]{:S(2)}, u32[]{:S(2)}) %all-to-all-start.2) | async-done | bytes 131104 | tf_op jit(solution)/shard_map/fields/all_to_all | solution.py:50
  105.0 0.0 collective-permute-done.11.refs_5_
  105.0 0.6 copy-done.5
  105.6 3.0 %shard_map.96.refs_7_ = f32[128,512]{1,0:T(8,128)} custom-call(s32[1]{0:T(128)} %bitcast.me_ref, s32[7]{0:T(128)} %bitcast.30, bf16[7,128,128]{2,1,0:T(8,128)(2,1)} %bitcast.24, bf16[4,128,512]{2,1,0:T(8,128)(2,1)} %copy-done.2, bf16[4,128,512]{2,1,0:T(8,128)(2,1)} %collective-permute-done.7.refs_1_, bf16[4,128,512]{2,1,0:T(8,128)(2,1)} %collective-permute-done.8.refs_2_, ...), custom_call_target="tpu_custom_call" | custom-call | flops 117440512 | bytes 917504 | tf_op jit(solution)/shard_map/pallas_call | solution.py:74
  108.7 3.0 %collective-permute-start.17 = (bf16[768,512]{1,0:T(8,128)(2,1)S(1)}, bf16[768,512]{1,0:T(8,128)(2,1)S(1)}, u32[]{:S(2)}, u32[]{:S(2)}) collective-permute-start(bf16[768,512]{1,0:T(8,128)(2,1)S(1)} %collective-permute-done.3.refs_0_), channel_id=1, source_target_pairs={{8,0},{24,16},{40,32},{56,48},{72,64},{88,80},{104,96},{120,112},{... | collective-permute-start | bytes 2359304 | tf_op jit(solution)/shard_map/low2_swap/ppermute | solution.py:45
  111.7 1.3 %collective-permute-start.18 = (bf16[768,512]{1,0:T(8,128)(2,1)}, bf16[768,512]{1,0:T(8,128)(2,1)S(1)}, u32[]{:S(2)}, u32[]{:S(2)}) collective-permute-start(bf16[768,512]{1,0:T(8,128)(2,1)} %collective-permute-done.4.refs_1_), channel_id=1, source_target_pairs={{0,8},{16,24},{32,40},{48,56},{64,72},{80,88},{96,104},{112,120},{... | collective-permute-start | bytes 2359304 | tf_op jit(solution)/shard_map/high2_swap/ppermute | solution.py:45
  113.0 0.5 collective-permute-done.17.refs_2_
  113.6 2.5 %collective-permute-done.18.refs_3_ = bf16[768,512]{1,0:T(8,128)(2,1)S(1)} collective-permute-done((bf16[768,512]{1,0:T(8,128)(2,1)}, bf16[768,512]{1,0:T(8,128)(2,1)S(1)}, u32[]{:S(2)}, u32[]{:S(2)}) %collective-permute-start.18) | collective-permute-done | bytes 786464 | tf_op jit(solution)/shard_map/high2_swap/ppermute | solution.py:45
  116.1 0.9 copy-done.11
  117.0 5.8 %shard_map.97 = f32[768,512]{1,0:T(8,128)} custom-call(s32[1]{0:T(128)} %bitcast.me_ref, s32[8]{0:T(128)} %bitcast.29, s32[1]{0:T(128)} %bitcast.15.count_ref, bf16[8,768,768]{2,1,0:T(8,128)(2,1)} %bitcast.18, bf16[768,512]{1,0:T(8,128)(2,1)} %copy-done.6, bf16[768,512]{1,0:T(8,128)(2,1)} %collective-permute-done.4.refs_1_, bf16[768,512]{1,0:T(8,128)(2,1)} %copy-done.10, ...), custom_call_target="tpu_custom_call" | custom-call | flops 2415919104 | bytes 7864320 | tf_op jit(solution)/shard_map/pallas_call | solution.py:74
  (28 shorter events, 0.1 us)
Async XLA Ops:
  0.0 81.2 %copy-start.3 = (bf16[1,8,128,128]{3,2,1,0:T(8,128)(2,1)S(1)}, bf16[1,8,128,128]{3,2,1,0:T(8,128)(2,1)}, u32[]{:S(2)}) copy-start(bf16[1,8,128,128]{3,2,1,0:T(8,128)(2,1)} %param.14) | copy-start | bytes 786436
  3.3 7.7 %collective-permute-start = (bf16[128,512]{1,0:T(8,128)(2,1)}, bf16[128,512]{1,0:T(8,128)(2,1)S(1)}, u32[]{:S(2)}, u32[]{:S(2)}) collective-permute-start(bf16[128,512]{1,0:T(8,128)(2,1)} %get-tuple-element.27.refs_0_), channel_id=1, source_target_pairs={{0,192},{8,200},{16,208},{24,216},{32,224},{40,232},{48,240},{56,2... | collective-permute-start | bytes 393224 | tf_op jit(solution)/shard_map/coeffs_z3/ppermute | solution.py:45
  11.0 41.6 %collective-permute-start.1 = (bf16[768,512]{1,0:T(8,128)(2,1)}, bf16[768,512]{1,0:T(8,128)(2,1)S(1)}, u32[]{:S(2)}, u32[]{:S(2)}) collective-permute-start(bf16[768,512]{1,0:T(8,128)(2,1)} %get-tuple-element.23.refs_0_), channel_id=1, source_target_pairs={{0,16},{8,24},{16,32},{24,40},{32,48},{40,56},{48,64},{56,72},{64,... | collective-permute-start | bytes 2359304 | tf_op jit(solution)/shard_map/low_hop/ppermute | solution.py:45
  14.2 59.3 %collective-permute-start.2 = (bf16[768,512]{1,0:T(8,128)(2,1)}, bf16[768,512]{1,0:T(8,128)(2,1)S(1)}, u32[]{:S(2)}, u32[]{:S(2)}) collective-permute-start(bf16[768,512]{1,0:T(8,128)(2,1)} %get-tuple-element.23.refs_0_), channel_id=1, source_target_pairs={{16,0},{24,8},{32,16},{40,24},{48,32},{56,40},{64,48},{72,56},{80,... | collective-permute-start | bytes 2359304 | tf_op jit(solution)/shard_map/high_hop/ppermute | solution.py:45
  15.5 28.8 %all-to-all-start = ((bf16[32,16,128]{2,1,0:T(8,128)(2,1)}), bf16[32,16,128]{2,1,0:T(8,128)(2,1)S(1)}, u32[]{:S(2)}, u32[]{:S(2)}) async-start(bf16[32,16,128]{2,1,0:T(8,128)(2,1)} %bitcast.27), calls=%async_computation | async-start | bytes 262144 | tf_op jit(solution)/shard_map/rises/all_to_all | solution.py:50
  26.7 17.4 %collective-permute-start.5 = (bf16[128,512]{1,0:T(8,128)(2,1)}, bf16[128,512]{1,0:T(8,128)(2,1)S(1)}, u32[]{:S(2)}, u32[]{:S(2)}) collective-permute-start(bf16[128,512]{1,0:T(8,128)(2,1)} %get-tuple-element.27.refs_0_), channel_id=1, source_target_pairs={{0,64},{8,72},{16,80},{24,88},{32,96},{40,104},{48,112},{56,120},{... | collective-permute-start | bytes 393224 | tf_op jit(solution)/shard_map/coeffs_z1/ppermute | solution.py:45
  28.1 15.9 %collective-permute-start.6 = (bf16[128,512]{1,0:T(8,128)(2,1)}, bf16[128,512]{1,0:T(8,128)(2,1)S(1)}, u32[]{:S(2)}, u32[]{:S(2)}) collective-permute-start(bf16[128,512]{1,0:T(8,128)(2,1)} %get-tuple-element.27.refs_0_), channel_id=1, source_target_pairs={{0,128},{8,136},{16,144},{24,152},{32,160},{40,168},{48,176},{56,1... | collective-permute-start | bytes 393224 | tf_op jit(solution)/shard_map/coeffs_z2/ppermute | solution.py:45
  44.4 0.9 copy-start.4
  46.7 51.2 %copy-start.2 = (bf16[4,128,512]{2,1,0:T(8,128)(2,1)}, bf16[4,128,512]{2,1,0:T(8,128)(2,1)S(1)}, u32[]{:S(2)}) copy-start(bf16[4,128,512]{2,1,0:T(8,128)(2,1)S(1)} %shard_map.93.refs_0_) | copy-start | bytes 1572868
  46.7 28.3 %collective-permute-start.7 = (bf16[4,128,512]{2,1,0:T(8,128)(2,1)S(1)}, bf16[4,128,512]{2,1,0:T(8,128)(2,1)}, u32[]{:S(2)}, u32[]{:S(2)}) collective-permute-start(bf16[4,128,512]{2,1,0:T(8,128)(2,1)S(1)} %shard_map.93.refs_0_), channel_id=1, source_target_pairs={{0,16},{8,24},{16,32},{24,40},{32,48},{40,56},{48,0},{56,8},{64,80... | collective-permute-start | bytes 1572872 | tf_op jit(solution)/shard_map/coeffs_y1/ppermute | solution.py:45
  47.6 27.5 %collective-permute-start.8 = (bf16[4,128,512]{2,1,0:T(8,128)(2,1)S(1)}, bf16[4,128,512]{2,1,0:T(8,128)(2,1)}, u32[]{:S(2)}, u32[]{:S(2)}) collective-permute-start(bf16[4,128,512]{2,1,0:T(8,128)(2,1)S(1)} %shard_map.93.refs_0_), channel_id=1, source_target_pairs={{0,32},{8,40},{16,48},{24,56},{32,0},{40,8},{48,16},{56,24},{64,96... | collective-permute-start | bytes 1572872 | tf_op jit(solution)/shard_map/coeffs_y2/ppermute | solution.py:45
  50.9 24.2 %collective-permute-start.9 = (bf16[4,128,512]{2,1,0:T(8,128)(2,1)S(1)}, bf16[4,128,512]{2,1,0:T(8,128)(2,1)}, u32[]{:S(2)}, u32[]{:S(2)}) collective-permute-start(bf16[4,128,512]{2,1,0:T(8,128)(2,1)S(1)} %shard_map.93.refs_0_), channel_id=1, source_target_pairs={{0,48},{8,56},{16,0},{24,8},{32,16},{40,24},{48,32},{56,40},{64,11... | collective-permute-start | bytes 1572872 | tf_op jit(solution)/shard_map/coeffs_y3/ppermute | solution.py:45
  52.6 36.9 %copy-start = (bf16[768,512]{1,0:T(8,128)(2,1)}, bf16[768,512]{1,0:T(8,128)(2,1)S(1)}, u32[]{:S(2)}) copy-start(bf16[768,512]{1,0:T(8,128)(2,1)S(1)} %collective-permute-done.1.refs_0_.refs_2_) | copy-start | bytes 2359300
  52.7 25.5 %collective-permute-start.14 = (bf16[768,512]{1,0:T(8,128)(2,1)}, bf16[768,512]{1,0:T(8,128)(2,1)S(1)}, u32[]{:S(2)}, u32[]{:S(2)}) collective-permute-start(bf16[768,512]{1,0:T(8,128)(2,1)} %get-tuple-element.23.refs_0_), channel_id=1, source_target_pairs={{0,8},{8,0},{16,24},{24,16},{32,40},{40,32},{48,56},{56,48},{64,72... | collective-permute-start | bytes 2359304 | tf_op jit(solution)/shard_map/own_swap/ppermute | solution.py:45
  73.5 16.0 %copy-start.1 = (bf16[768,512]{1,0:T(8,128)(2,1)}, bf16[768,512]{1,0:T(8,128)(2,1)S(1)}, u32[]{:S(2)}) copy-start(bf16[768,512]{1,0:T(8,128)(2,1)S(1)} %collective-permute-done.2.refs_1_.refs_3_) | copy-start | bytes 2359300
  73.5 6.5 %collective-permute-start.15 = (bf16[768,512]{1,0:T(8,128)(2,1)S(1)}, bf16[768,512]{1,0:T(8,128)(2,1)S(1)}, u32[]{:S(2)}, u32[]{:S(2)}) collective-permute-start(bf16[768,512]{1,0:T(8,128)(2,1)S(1)} %collective-permute-done.1.refs_0_.refs_2_), channel_id=1, source_target_pairs={{0,8},{8,0},{16,24},{24,16},{32,40},{40,32},{48,56},{56,48},{64,72... | collective-permute-start | bytes 2359304 | tf_op jit(solution)/shard_map/low_swap/ppermute | solution.py:45
  75.0 5.1 %collective-permute-start.16 = (bf16[768,512]{1,0:T(8,128)(2,1)S(1)}, bf16[768,512]{1,0:T(8,128)(2,1)S(1)}, u32[]{:S(2)}, u32[]{:S(2)}) collective-permute-start(bf16[768,512]{1,0:T(8,128)(2,1)S(1)} %collective-permute-done.2.refs_1_.refs_3_), channel_id=1, source_target_pairs={{0,8},{8,0},{16,24},{24,16},{32,40},{40,32},{48,56},{56,48},{64,72... | collective-permute-start | bytes 2359304 | tf_op jit(solution)/shard_map/high_swap/ppermute | solution.py:45
  75.1 4.4 %collective-permute-start.10 = (bf16[4,128,512]{2,1,0:T(8,128)(2,1)S(1)}, bf16[4,128,512]{2,1,0:T(8,128)(2,1)S(1)}, u32[]{:S(2)}, u32[]{:S(2)}) collective-permute-start(bf16[4,128,512]{2,1,0:T(8,128)(2,1)S(1)} %shard_map.93.refs_0_), channel_id=1, source_target_pairs={{0,8},{8,0},{16,24},{24,16},{32,40},{40,32},{48,56},{56,48},{64,72... | collective-permute-start | bytes 1572872 | tf_op jit(solution)/shard_map/coeffs_swap0/ppermute | solution.py:45
  75.5 33.1 %collective-permute-start.3 = (bf16[768,512]{1,0:T(8,128)(2,1)S(1)}, bf16[768,512]{1,0:T(8,128)(2,1)S(1)}, u32[]{:S(2)}, u32[]{:S(2)}) collective-permute-start(bf16[768,512]{1,0:T(8,128)(2,1)S(1)} %collective-permute-done.1.refs_0_.refs_2_), channel_id=1, source_target_pairs={{0,16},{8,24},{16,32},{24,40},{32,48},{40,56},{48,64},{56,72},{64,... | collective-permute-start | bytes 2359304 | tf_op jit(solution)/shard_map/low_hop2/ppermute | solution.py:45
  78.1 2.0 %copy-start.7 = (bf16[768,512]{1,0:T(8,128)(2,1)}, bf16[768,512]{1,0:T(8,128)(2,1)S(1)}, u32[]{:S(2)}) copy-start(bf16[768,512]{1,0:T(8,128)(2,1)S(1)} %collective-permute-done.14.refs_1_) | copy-start | bytes 2359300
  78.2 30.5 %collective-permute-start.4 = (bf16[768,512]{1,0:T(8,128)(2,1)S(1)}, bf16[768,512]{1,0:T(8,128)(2,1)}, u32[]{:S(2)}, u32[]{:S(2)}) collective-permute-start(bf16[768,512]{1,0:T(8,128)(2,1)S(1)} %collective-permute-done.2.refs_1_.refs_3_), channel_id=1, source_target_pairs={{16,0},{24,8},{32,16},{40,24},{48,32},{56,40},{64,48},{72,56},{80,... | collective-permute-start | bytes 2359304 | tf_op jit(solution)/shard_map/high_hop2/ppermute | solution.py:45
  79.5 1.1 copy-start.12
  79.5 25.5 %collective-permute-start.11 = (bf16[4,128,512]{2,1,0:T(8,128)(2,1)}, bf16[4,128,512]{2,1,0:T(8,128)(2,1)}, u32[]{:S(2)}, u32[]{:S(2)}) collective-permute-start(bf16[4,128,512]{2,1,0:T(8,128)(2,1)} %collective-permute-done.7.refs_1_), channel_id=1, source_target_pairs={{0,8},{8,0},{16,24},{24,16},{32,40},{40,32},{48,56},{56,48},{64,72... | collective-permute-start | bytes 1572872 | tf_op jit(solution)/shard_map/coeffs_swap1/ppermute | solution.py:45
  80.0 0.9 copy-start.8
  80.0 25.0 %collective-permute-start.12 = (bf16[4,128,512]{2,1,0:T(8,128)(2,1)}, bf16[4,128,512]{2,1,0:T(8,128)(2,1)}, u32[]{:S(2)}, u32[]{:S(2)}) collective-permute-start(bf16[4,128,512]{2,1,0:T(8,128)(2,1)} %collective-permute-done.8.refs_2_), channel_id=1, source_target_pairs={{0,8},{8,0},{16,24},{24,16},{32,40},{40,32},{48,56},{56,48},{64,72... | collective-permute-start | bytes 1572872 | tf_op jit(solution)/shard_map/coeffs_swap2/ppermute | solution.py:45
  80.1 1.1 copy-start.9
  80.1 24.9 %collective-permute-start.13 = (bf16[4,128,512]{2,1,0:T(8,128)(2,1)}, bf16[4,128,512]{2,1,0:T(8,128)(2,1)}, u32[]{:S(2)}, u32[]{:S(2)}) collective-permute-start(bf16[4,128,512]{2,1,0:T(8,128)(2,1)} %collective-permute-done.9.refs_3_), channel_id=1, source_target_pairs={{0,8},{8,0},{16,24},{24,16},{32,40},{40,32},{48,56},{56,48},{64,72... | collective-permute-start | bytes 1572872 | tf_op jit(solution)/shard_map/coeffs_swap3/ppermute | solution.py:45
  82.5 22.4 %all-to-all-start.2 = ((bf16[32,16,128]{2,1,0:T(8,128)(2,1)}), bf16[32,16,128]{2,1,0:T(8,128)(2,1)S(1)}, u32[]{:S(2)}, u32[]{:S(2)}) async-start(bf16[32,16,128]{2,1,0:T(8,128)(2,1)} %shard_map.94.refs_6_), calls=%async_computation.2 | async-start | bytes 262144 | tf_op jit(solution)/shard_map/fields/all_to_all | solution.py:50
  105.0 0.7 copy-start.5
  108.6 7.5 %copy-start.6 = (bf16[768,512]{1,0:T(8,128)(2,1)}, bf16[768,512]{1,0:T(8,128)(2,1)S(1)}, u32[]{:S(2)}) copy-start(bf16[768,512]{1,0:T(8,128)(2,1)S(1)} %collective-permute-done.3.refs_0_) | copy-start | bytes 2359300
  108.7 4.9 %collective-permute-start.17 = (bf16[768,512]{1,0:T(8,128)(2,1)S(1)}, bf16[768,512]{1,0:T(8,128)(2,1)S(1)}, u32[]{:S(2)}, u32[]{:S(2)}) collective-permute-start(bf16[768,512]{1,0:T(8,128)(2,1)S(1)} %collective-permute-done.3.refs_0_), channel_id=1, source_target_pairs={{8,0},{24,16},{40,32},{56,48},{72,64},{88,80},{104,96},{120,112},{... | collective-permute-start | bytes 2359304 | tf_op jit(solution)/shard_map/low2_swap/ppermute | solution.py:45
  111.7 4.4 %collective-permute-start.18 = (bf16[768,512]{1,0:T(8,128)(2,1)}, bf16[768,512]{1,0:T(8,128)(2,1)S(1)}, u32[]{:S(2)}, u32[]{:S(2)}) collective-permute-start(bf16[768,512]{1,0:T(8,128)(2,1)} %collective-permute-done.4.refs_1_), channel_id=1, source_target_pairs={{0,8},{16,24},{32,40},{48,56},{64,72},{80,88},{96,104},{112,120},{... | collective-permute-start | bytes 2359304 | tf_op jit(solution)/shard_map/high2_swap/ppermute | solution.py:45
  113.6 2.6 %copy-start.10 = (bf16[768,512]{1,0:T(8,128)(2,1)}, bf16[768,512]{1,0:T(8,128)(2,1)S(1)}, u32[]{:S(2)}) copy-start(bf16[768,512]{1,0:T(8,128)(2,1)S(1)} %collective-permute-done.17.refs_2_) | copy-start | bytes 2359300
  116.1 0.9 copy-start.11

commit v3 on v2

--- a/solution.py
+++ b/solution.py
@@ -393,7 +393,6 @@
     stores = [column] + [send(f"coeffs_y{d}", column, turn(0, d)) for d in range(1, Y)]
 
     beside = send("own_swap", masked, SWAP)
-    (masked,) = after([masked], by_z[-1])
     from_low = send("low_hop", masked, chip_step(1))
     from_high = send("high_hop", masked, chip_step(-1))
 
@@ -412,8 +411,8 @@
     )
     stores += [send(f"coeffs_swap{i}", block, SWAP) for i, block in enumerate(after(stores, parents))]
     field = exchange("fields", field, None).reshape(vecs, rank)
-    far_sum = far_field(me, far, coupling[0, 0], stores, [near, field])
-    from_low2, from_high2 = after([from_low2, from_high2], far_sum)
+    far_sum = far_field(me, far, coupling[0, 0], stores, [near])
+    from_low2, from_high2 = after(after([from_low2, from_high2], far_sum), field)
     low2_beside = send("low2_swap", from_low2, TO_FIRST)
     high2_beside = send("high2_swap", from_high2, TO_SECOND)
     result = near_last(

time: 123 us -> 119 us (0.967)
  starting transfers between devices: 52 us -> 49.3 us
    ppermute x19, starting transfers between devices: 33.9 us -> 29.7 us  [send(): return lax.ppermute(block, axis, route)]
    all_to_all x2, waiting for transfers between devices: 7.47 us -> 4.6 us  [exchange(): lax.all_to_all(blocks, axis, 0, 0, tiled=True, axis_index_groups=groups)]
    ppermute x19, waiting for transfers between devices: 19.4 us -> 21.2 us  [send(): return lax.ppermute(block, axis, route)]
    all_to_all x2, starting transfers between devices: 18.1 us -> 19.7 us  [exchange(): lax.all_to_all(blocks, axis, 0, 0, tiled=True, axis_index_groups=groups)]
  transfers between devices with their start and end apart: 21 -> 21, of which waited for: 6 -> 5; matrix products, arithmetic and copies ran while one was open for 0% -> 0% of each run, Pallas kernels for 12% -> 11%
where the time goes in v3:
time: 119 us
  starting transfers between devices  49.3 us (41%)
  waiting for transfers between devices  25.8 us (22%)
  Pallas kernels  22.6 us (19%)
  blocking collectives  17.7 us (15%)
  local copies, waits for them, and re-layouts  2.43 us (2%)
    ppermute x19, starting transfers between devices, send(): return lax.ppermute(block, axis, route)  29.7 us
    pallas_call x7, Pallas kernels, call(): pl.pallas_call(kernel, out_shape=outs, in_specs=[SMEM] * len(scalars) + [...  22.6 us
    ppermute x19, waiting for transfers between devices, send(): return lax.ppermute(block, axis, route)  21.2 us
    all_to_all x2, starting transfers between devices, exchange(): lax.all_to_all(blocks, axis, 0, 0, tiled=True, axis_index_groups=groups)  19.7 us
    all_to_all x1, blocking collectives, exchange(): lax.all_to_all(blocks, axis, 0, 0, tiled=True, axis_index_groups=groups)  17.7 us
    all_to_all x2, waiting for transfers between devices, exchange(): lax.all_to_all(blocks, axis, 0, 0, tiled=True, axis_index_groups=groups)  4.6 us
    unnamed x26, local copies, waits for them, and re-layouts  2.43 us
  transfers between devices with their start and end apart: 21, of which 5 were waited for; matrix products, arithmetic and copies ran while one was open for 0% of the time, Pallas kernels for 11%

profile of v3, /device:TPU:1, one launch (start us, length us, event | category | flops | bytes accessed | tf_op | source)
XLA Modules:
  0.0 119.0 jit_solution(12195398901876981325)
XLA Ops:
  0.7 2.6 %shard_map.91 = (bf16[768,512]{1,0:T(8,128)(2,1)}, bf16[128,512]{1,0:T(8,128)(2,1)}, bf16[512,128]{1,0:T(8,128)(2,1)}) custom-call(s32[1]{0:T(128)} %bitcast.14.count_ref, bf16[768,512]{1,0:T(8,128)(2,1)} %bitcast.21, bf16[768,128]{1,0:T(8,128)(2,1)} %bitcast.19, bf16[128,128]{1,0:T(8,128)(2,1)} %bitcast.24), custom_call_target="tpu_custom_call" | custom-call | flops 100663296 | bytes 1572864 | tf_op jit(solution)/shard_map/pallas_call | solution.py:74
  3.3 4.1 %collective-permute-start = (bf16[768,512]{1,0:T(8,128)(2,1)}, bf16[768,512]{1,0:T(8,128)(2,1)S(1)}, u32[]{:S(2)}, u32[]{:S(2)}) collective-permute-start(bf16[768,512]{1,0:T(8,128)(2,1)} %get-tuple-element.22.refs_0_), channel_id=1, source_target_pairs={{0,16},{8,24},{16,32},{24,40},{32,48},{40,56},{48,64},{56,72},{64,... | collective-permute-start | bytes 2359304 | tf_op jit(solution)/shard_map/low_hop/ppermute | solution.py:45
  7.4 1.3 %collective-permute-start.1 = (bf16[768,512]{1,0:T(8,128)(2,1)}, bf16[768,512]{1,0:T(8,128)(2,1)S(1)}, u32[]{:S(2)}, u32[]{:S(2)}) collective-permute-start(bf16[768,512]{1,0:T(8,128)(2,1)} %get-tuple-element.22.refs_0_), channel_id=1, source_target_pairs={{16,0},{24,8},{32,16},{40,24},{48,32},{56,40},{64,48},{72,56},{80,... | collective-permute-start | bytes 2359304 | tf_op jit(solution)/shard_map/high_hop/ppermute | solution.py:45
  8.7 10.7 %all-to-all-start = ((bf16[32,16,128]{2,1,0:T(8,128)(2,1)}), bf16[32,16,128]{2,1,0:T(8,128)(2,1)S(1)}, u32[]{:S(2)}, u32[]{:S(2)}) async-start(bf16[32,16,128]{2,1,0:T(8,128)(2,1)} %bitcast.26), calls=%async_computation | async-start | bytes 262144 | tf_op jit(solution)/shard_map/rises/all_to_all | solution.py:50
  19.3 1.5 %collective-permute-start.4 = (bf16[128,512]{1,0:T(8,128)(2,1)}, bf16[128,512]{1,0:T(8,128)(2,1)S(1)}, u32[]{:S(2)}, u32[]{:S(2)}) collective-permute-start(bf16[128,512]{1,0:T(8,128)(2,1)} %get-tuple-element.27.refs_0_), channel_id=1, source_target_pairs={{0,64},{8,72},{16,80},{24,88},{32,96},{40,104},{48,112},{56,120},{... | collective-permute-start | bytes 393224 | tf_op jit(solution)/shard_map/coeffs_z1/ppermute | solution.py:45
  20.8 2.1 %collective-permute-start.5 = (bf16[128,512]{1,0:T(8,128)(2,1)}, bf16[128,512]{1,0:T(8,128)(2,1)S(1)}, u32[]{:S(2)}, u32[]{:S(2)}) collective-permute-start(bf16[128,512]{1,0:T(8,128)(2,1)} %get-tuple-element.27.refs_0_), channel_id=1, source_target_pairs={{0,128},{8,136},{16,144},{24,152},{32,160},{40,168},{48,176},{56,1... | collective-permute-start | bytes 393224 | tf_op jit(solution)/shard_map/coeffs_z2/ppermute | solution.py:45
  22.9 1.1 collective-permute-start.6
  24.1 14.5 %collective-permute-done.4.refs_1_ = bf16[128,512]{1,0:T(8,128)(2,1)S(1)} collective-permute-done((bf16[128,512]{1,0:T(8,128)(2,1)}, bf16[128,512]{1,0:T(8,128)(2,1)S(1)}, u32[]{:S(2)}, u32[]{:S(2)}) %collective-permute-start.4) | collective-permute-done | bytes 131104 | tf_op jit(solution)/shard_map/coeffs_z1/ppermute | solution.py:45
  38.6 3.6 %collective-permute-done.5.refs_2_ = bf16[128,512]{1,0:T(8,128)(2,1)S(1)} collective-permute-done((bf16[128,512]{1,0:T(8,128)(2,1)}, bf16[128,512]{1,0:T(8,128)(2,1)S(1)}, u32[]{:S(2)}, u32[]{:S(2)}) %collective-permute-start.5) | collective-permute-done | bytes 131104 | tf_op jit(solution)/shard_map/coeffs_z2/ppermute | solution.py:45
  42.1 0.0 collective-permute-done.6.refs_3_
  42.1 0.0 all-to-all-done.pieces
  42.1 0.9 copy-done.4
  43.0 1.4 %shard_map.93.refs_0_ = bf16[4,128,512]{2,1,0:T(8,128)(2,1)S(1)} custom-call(bf16[128,512]{1,0:T(8,128)(2,1)S(1)} %copy-done.4, bf16[128,512]{1,0:T(8,128)(2,1)S(1)} %collective-permute-done.4.refs_1_, bf16[128,512]{1,0:T(8,128)(2,1)S(1)} %collective-permute-done.5.refs_2_, bf16[128,512]{1,0:T(8,128)(2,1)S(1)} %collective-permute-done.6.refs_3_), custom_call_target="tpu_custom_call" | custom-call | tf_op jit(solution)/shard_map/pallas_call | solution.py:74
  44.5 0.1 collective-permute-start.7
  44.5 2.9 %collective-permute-start.8 = (bf16[4,128,512]{2,1,0:T(8,128)(2,1)S(1)}, bf16[4,128,512]{2,1,0:T(8,128)(2,1)}, u32[]{:S(2)}, u32[]{:S(2)}) collective-permute-start(bf16[4,128,512]{2,1,0:T(8,128)(2,1)S(1)} %shard_map.93.refs_0_), channel_id=1, source_target_pairs={{0,32},{8,40},{16,48},{24,56},{32,0},{40,8},{48,16},{56,24},{64,96... | collective-permute-start | bytes 1572872 | tf_op jit(solution)/shard_map/coeffs_y2/ppermute | solution.py:45
  47.5 1.9 %collective-permute-start.9 = (bf16[4,128,512]{2,1,0:T(8,128)(2,1)S(1)}, bf16[4,128,512]{2,1,0:T(8,128)(2,1)}, u32[]{:S(2)}, u32[]{:S(2)}) collective-permute-start(bf16[4,128,512]{2,1,0:T(8,128)(2,1)S(1)} %shard_map.93.refs_0_), channel_id=1, source_target_pairs={{0,48},{8,56},{16,0},{24,8},{32,16},{40,24},{48,32},{56,40},{64,11... | collective-permute-start | bytes 1572872 | tf_op jit(solution)/shard_map/coeffs_y3/ppermute | solution.py:45
  49.4 0.0 collective-permute-done.refs_0_.refs_2_
  49.4 2.9 %collective-permute-start.14 = (bf16[768,512]{1,0:T(8,128)(2,1)}, bf16[768,512]{1,0:T(8,128)(2,1)S(1)}, u32[]{:S(2)}, u32[]{:S(2)}) collective-permute-start(bf16[768,512]{1,0:T(8,128)(2,1)} %get-tuple-element.22.refs_0_), channel_id=1, source_target_pairs={{0,8},{8,0},{16,24},{24,16},{32,40},{40,32},{48,56},{56,48},{64,72... | collective-permute-start | bytes 2359304 | tf_op jit(solution)/shard_map/own_swap/ppermute | solution.py:45
  52.3 0.3 shard_map.92
  52.6 17.7 %all_to_all.19.parents_in = bf16[8,16,128]{2,1,0:T(8,128)(2,1)S(1)} all-to-all(bf16[8,16,128]{2,1,0:T(8,128)(2,1)S(1)} %shard_map.92), channel_id=1, replica_groups=mesh['leaf'=32,'top'=8] {'top'}, dimensions={0} | all-to-all | bytes 65536 | tf_op jit(solution)/shard_map/parents/all_to_all | solution.py:50
  70.3 0.0 collective-permute-done.1.refs_1_.refs_3_
  70.3 1.5 %collective-permute-start.15 = (bf16[768,512]{1,0:T(8,128)(2,1)S(1)}, bf16[768,512]{1,0:T(8,128)(2,1)S(1)}, u32[]{:S(2)}, u32[]{:S(2)}) collective-permute-start(bf16[768,512]{1,0:T(8,128)(2,1)S(1)} %collective-permute-done.refs_0_.refs_2_), channel_id=1, source_target_pairs={{0,8},{8,0},{16,24},{24,16},{32,40},{40,32},{48,56},{56,48},{64,72... | collective-permute-start | bytes 2359304 | tf_op jit(solution)/shard_map/low_swap/ppermute | solution.py:45
  71.8 0.0 collective-permute-done.7.refs_1_
  71.8 0.1 collective-permute-start.16
  71.9 0.0 collective-permute-done.8.refs_2_
  71.9 0.4 collective-permute-start.10
  72.3 3.1 %collective-permute-start.2 = (bf16[768,512]{1,0:T(8,128)(2,1)S(1)}, bf16[768,512]{1,0:T(8,128)(2,1)S(1)}, u32[]{:S(2)}, u32[]{:S(2)}) collective-permute-start(bf16[768,512]{1,0:T(8,128)(2,1)S(1)} %collective-permute-done.refs_0_.refs_2_), channel_id=1, source_target_pairs={{0,16},{8,24},{16,32},{24,40},{32,48},{40,56},{48,64},{56,72},{64,... | collective-permute-start | bytes 2359304 | tf_op jit(solution)/shard_map/low_hop2/ppermute | solution.py:45
  75.4 1.3 %collective-permute-start.3 = (bf16[768,512]{1,0:T(8,128)(2,1)S(1)}, bf16[768,512]{1,0:T(8,128)(2,1)}, u32[]{:S(2)}, u32[]{:S(2)}) collective-permute-start(bf16[768,512]{1,0:T(8,128)(2,1)S(1)} %collective-permute-done.1.refs_1_.refs_3_), channel_id=1, source_target_pairs={{16,0},{24,8},{32,16},{40,24},{48,32},{56,40},{64,48},{72,56},{80,... | collective-permute-start | bytes 2359304 | tf_op jit(solution)/shard_map/high_hop2/ppermute | solution.py:45
  76.7 0.0 collective-permute-done.10.refs_4_
  76.8 0.4 collective-permute-start.11
  77.1 0.0 collective-permute-done.15.refs_4_
  77.1 0.2 collective-permute-start.12
  77.4 0.4 collective-permute-start.13
  77.7 0.3 copy-done.7
  78.1 0.3 copy-done.8
  78.4 1.3 %shard_map.94.refs_6_ = bf16[32,16,128]{2,1,0:T(8,128)(2,1)} custom-call(s32[1]{0:T(128)} %bitcast.10.mine_ref, bf16[8,128,128]{2,1,0:T(8,128)(2,1)S(1)} %bitcast.16, bf16[8,16,128]{2,1,0:T(8,128)(2,1)S(1)} %all_to_all.19.parents_in, bf16[768,512]{1,0:T(8,128)(2,1)S(1)} %collective-permute-done.refs_0_.refs_2_, ...), custom_call_target="tpu_custom_call" | custom-call | flops 4194304 | bytes 262144 | tf_op jit(solution)/shard_map/pallas_call | solution.py:74
  79.7 9.0 %all-to-all-start.2 = ((bf16[32,16,128]{2,1,0:T(8,128)(2,1)}), bf16[32,16,128]{2,1,0:T(8,128)(2,1)S(1)}, u32[]{:S(2)}, u32[]{:S(2)}) async-start(bf16[32,16,128]{2,1,0:T(8,128)(2,1)} %shard_map.94.refs_6_), calls=%async_computation.2 | async-start | bytes 262144 | tf_op jit(solution)/shard_map/fields/all_to_all | solution.py:50
  88.7 7.5 %shard_map.95.refs_8_.refs_4_ = f32[768,512]{1,0:T(8,128)} custom-call(s32[1]{0:T(128)} %bitcast.me_ref, s32[8]{0:T(128)} %bitcast.27, bf16[8,768,768]{2,1,0:T(8,128)(2,1)} %bitcast.17, bf16[768,512]{1,0:T(8,128)(2,1)} %get-tuple-element.22.refs_0_, bf16[768,512]{1,0:T(8,128)(2,1)} %copy-done.6, bf16[768,512]{1,0:T(8,128)(2,1)} %copy-done, ...), custom_call_target="tpu_custom_call" | custom-call | flops 3623878656 | bytes 11796480 | tf_op jit(solution)/shard_map/pallas_call | solution.py:74
  96.2 0.0 collective-permute-done.13.refs_7_
  96.3 3.0 %shard_map.96.refs_7_ = f32[128,512]{1,0:T(8,128)} custom-call(s32[1]{0:T(128)} %bitcast.me_ref, s32[7]{0:T(128)} %bitcast.29, bf16[7,128,128]{2,1,0:T(8,128)(2,1)} %bitcast.23, bf16[4,128,512]{2,1,0:T(8,128)(2,1)} %copy-done.2, bf16[4,128,512]{2,1,0:T(8,128)(2,1)} %collective-permute-done.7.refs_1_, bf16[4,128,512]{2,1,0:T(8,128)(2,1)} %collective-permute-done.8.refs_2_, ...), custom_call_target="tpu_custom_call" | custom-call | flops 117440512 | bytes 917504 | tf_op jit(solution)/shard_map/pallas_call | solution.py:74
  99.3 0.0 collective-permute-done.2.refs_0_
  99.3 4.6 %all-to-all-done.2 = bf16[32,16,128]{2,1,0:T(8,128)(2,1)S(1)} async-done(((bf16[32,16,128]{2,1,0:T(8,128)(2,1)}), bf16[32,16,128]{2,1,0:T(8,128)(2,1)S(1)}, u32[]{:S(2)}, u32[]{:S(2)}) %all-to-all-start.2) | async-done | bytes 131104 | tf_op jit(solution)/shard_map/fields/all_to_all | solution.py:50
  103.9 3.1 %collective-permute-start.17 = (bf16[768,512]{1,0:T(8,128)(2,1)S(1)}, bf16[768,512]{1,0:T(8,128)(2,1)S(1)}, u32[]{:S(2)}, u32[]{:S(2)}) collective-permute-start(bf16[768,512]{1,0:T(8,128)(2,1)S(1)} %collective-permute-done.2.refs_0_), channel_id=1, source_target_pairs={{8,0},{24,16},{40,32},{56,48},{72,64},{88,80},{104,96},{120,112},{... | collective-permute-start | bytes 2359304 | tf_op jit(solution)/shard_map/low2_swap/ppermute | solution.py:45
  107.0 1.3 %collective-permute-start.18 = (bf16[768,512]{1,0:T(8,128)(2,1)}, bf16[768,512]{1,0:T(8,128)(2,1)S(1)}, u32[]{:S(2)}, u32[]{:S(2)}) collective-permute-start(bf16[768,512]{1,0:T(8,128)(2,1)} %collective-permute-done.3.refs_1_), channel_id=1, source_target_pairs={{0,8},{16,24},{32,40},{48,56},{64,72},{80,88},{96,104},{112,120},{... | collective-permute-start | bytes 2359304 | tf_op jit(solution)/shard_map/high2_swap/ppermute | solution.py:45
  108.3 0.5 collective-permute-done.17.refs_2_
  108.8 2.5 %collective-permute-done.18.refs_3_ = bf16[768,512]{1,0:T(8,128)(2,1)S(1)} collective-permute-done((bf16[768,512]{1,0:T(8,128)(2,1)}, bf16[768,512]{1,0:T(8,128)(2,1)S(1)}, u32[]{:S(2)}, u32[]{:S(2)}) %collective-permute-start.18) | collective-permute-done | bytes 786464 | tf_op jit(solution)/shard_map/high2_swap/ppermute | solution.py:45
  111.4 0.9 copy-done.10
  112.3 6.5 %shard_map.97 = f32[768,512]{1,0:T(8,128)} custom-call(s32[1]{0:T(128)} %bitcast.me_ref, s32[8]{0:T(128)} %bitcast.28, s32[1]{0:T(128)} %bitcast.15.count_ref, bf16[8,768,768]{2,1,0:T(8,128)(2,1)} %bitcast.18, bf16[768,512]{1,0:T(8,128)(2,1)} %copy-done.5, bf16[768,512]{1,0:T(8,128)(2,1)} %collective-permute-done.3.refs_1_, bf16[768,512]{1,0:T(8,128)(2,1)} %copy-done.9, ...), custom_call_target="tpu_custom_call" | custom-call | flops 2415919104 | bytes 7864320 | tf_op jit(solution)/shard_map/pallas_call | solution.py:74
  (28 shorter events, 0.1 us)
Async XLA Ops:
  0.0 78.4 %copy-start.3 = (bf16[1,8,128,128]{3,2,1,0:T(8,128)(2,1)S(1)}, bf16[1,8,128,128]{3,2,1,0:T(8,128)(2,1)}, u32[]{:S(2)}) copy-start(bf16[1,8,128,128]{3,2,1,0:T(8,128)(2,1)} %param.14) | copy-start | bytes 786436
  3.3 46.1 %collective-permute-start = (bf16[768,512]{1,0:T(8,128)(2,1)}, bf16[768,512]{1,0:T(8,128)(2,1)S(1)}, u32[]{:S(2)}, u32[]{:S(2)}) collective-permute-start(bf16[768,512]{1,0:T(8,128)(2,1)} %get-tuple-element.22.refs_0_), channel_id=1, source_target_pairs={{0,16},{8,24},{16,32},{24,40},{32,48},{40,56},{48,64},{56,72},{64,... | collective-permute-start | bytes 2359304 | tf_op jit(solution)/shard_map/low_hop/ppermute | solution.py:45
  7.4 62.9 %collective-permute-start.1 = (bf16[768,512]{1,0:T(8,128)(2,1)}, bf16[768,512]{1,0:T(8,128)(2,1)S(1)}, u32[]{:S(2)}, u32[]{:S(2)}) collective-permute-start(bf16[768,512]{1,0:T(8,128)(2,1)} %get-tuple-element.22.refs_0_), channel_id=1, source_target_pairs={{16,0},{24,8},{32,16},{40,24},{48,32},{56,40},{64,48},{72,56},{80,... | collective-permute-start | bytes 2359304 | tf_op jit(solution)/shard_map/high_hop/ppermute | solution.py:45
  8.7 33.5 %all-to-all-start = ((bf16[32,16,128]{2,1,0:T(8,128)(2,1)}), bf16[32,16,128]{2,1,0:T(8,128)(2,1)S(1)}, u32[]{:S(2)}, u32[]{:S(2)}) async-start(bf16[32,16,128]{2,1,0:T(8,128)(2,1)} %bitcast.26), calls=%async_computation | async-start | bytes 262144 | tf_op jit(solution)/shard_map/rises/all_to_all | solution.py:50
  19.3 19.2 %collective-permute-start.4 = (bf16[128,512]{1,0:T(8,128)(2,1)}, bf16[128,512]{1,0:T(8,128)(2,1)S(1)}, u32[]{:S(2)}, u32[]{:S(2)}) collective-permute-start(bf16[128,512]{1,0:T(8,128)(2,1)} %get-tuple-element.27.refs_0_), channel_id=1, source_target_pairs={{0,64},{8,72},{16,80},{24,88},{32,96},{40,104},{48,112},{56,120},{... | collective-permute-start | bytes 393224 | tf_op jit(solution)/shard_map/coeffs_z1/ppermute | solution.py:45
  20.8 21.3 %collective-permute-start.5 = (bf16[128,512]{1,0:T(8,128)(2,1)}, bf16[128,512]{1,0:T(8,128)(2,1)S(1)}, u32[]{:S(2)}, u32[]{:S(2)}) collective-permute-start(bf16[128,512]{1,0:T(8,128)(2,1)} %get-tuple-element.27.refs_0_), channel_id=1, source_target_pairs={{0,128},{8,136},{16,144},{24,152},{32,160},{40,168},{48,176},{56,1... | collective-permute-start | bytes 393224 | tf_op jit(solution)/shard_map/coeffs_z2/ppermute | solution.py:45
  22.9 19.2 %collective-permute-start.6 = (bf16[128,512]{1,0:T(8,128)(2,1)}, bf16[128,512]{1,0:T(8,128)(2,1)S(1)}, u32[]{:S(2)}, u32[]{:S(2)}) collective-permute-start(bf16[128,512]{1,0:T(8,128)(2,1)} %get-tuple-element.27.refs_0_), channel_id=1, source_target_pairs={{0,192},{8,200},{16,208},{24,216},{32,224},{40,232},{48,240},{56,2... | collective-permute-start | bytes 393224 | tf_op jit(solution)/shard_map/coeffs_z3/ppermute | solution.py:45
  42.1 0.9 copy-start.4
  44.4 51.8 %copy-start.2 = (bf16[4,128,512]{2,1,0:T(8,128)(2,1)}, bf16[4,128,512]{2,1,0:T(8,128)(2,1)S(1)}, u32[]{:S(2)}) copy-start(bf16[4,128,512]{2,1,0:T(8,128)(2,1)S(1)} %shard_map.93.refs_0_) | copy-start | bytes 1572868
  44.5 27.3 %collective-permute-start.7 = (bf16[4,128,512]{2,1,0:T(8,128)(2,1)S(1)}, bf16[4,128,512]{2,1,0:T(8,128)(2,1)}, u32[]{:S(2)}, u32[]{:S(2)}) collective-permute-start(bf16[4,128,512]{2,1,0:T(8,128)(2,1)S(1)} %shard_map.93.refs_0_), channel_id=1, source_target_pairs={{0,16},{8,24},{16,32},{24,40},{32,48},{40,56},{48,0},{56,8},{64,80... | collective-permute-start | bytes 1572872 | tf_op jit(solution)/shard_map/coeffs_y1/ppermute | solution.py:45
  44.5 27.3 %collective-permute-start.8 = (bf16[4,128,512]{2,1,0:T(8,128)(2,1)S(1)}, bf16[4,128,512]{2,1,0:T(8,128)(2,1)}, u32[]{:S(2)}, u32[]{:S(2)}) collective-permute-start(bf16[4,128,512]{2,1,0:T(8,128)(2,1)S(1)} %shard_map.93.refs_0_), channel_id=1, source_target_pairs={{0,32},{8,40},{16,48},{24,56},{32,0},{40,8},{48,16},{56,24},{64,96... | collective-permute-start | bytes 1572872 | tf_op jit(solution)/shard_map/coeffs_y2/ppermute | solution.py:45
  47.5 24.4 %collective-permute-start.9 = (bf16[4,128,512]{2,1,0:T(8,128)(2,1)S(1)}, bf16[4,128,512]{2,1,0:T(8,128)(2,1)}, u32[]{:S(2)}, u32[]{:S(2)}) collective-permute-start(bf16[4,128,512]{2,1,0:T(8,128)(2,1)S(1)} %shard_map.93.refs_0_), channel_id=1, source_target_pairs={{0,48},{8,56},{16,0},{24,8},{32,16},{40,24},{48,32},{56,40},{64,11... | collective-permute-start | bytes 1572872 | tf_op jit(solution)/shard_map/coeffs_y3/ppermute | solution.py:45
  49.4 39.3 %copy-start = (bf16[768,512]{1,0:T(8,128)(2,1)}, bf16[768,512]{1,0:T(8,128)(2,1)S(1)}, u32[]{:S(2)}) copy-start(bf16[768,512]{1,0:T(8,128)(2,1)S(1)} %collective-permute-done.refs_0_.refs_2_) | copy-start | bytes 2359300
  49.4 26.1 %collective-permute-start.14 = (bf16[768,512]{1,0:T(8,128)(2,1)}, bf16[768,512]{1,0:T(8,128)(2,1)S(1)}, u32[]{:S(2)}, u32[]{:S(2)}) collective-permute-start(bf16[768,512]{1,0:T(8,128)(2,1)} %get-tuple-element.22.refs_0_), channel_id=1, source_target_pairs={{0,8},{8,0},{16,24},{24,16},{32,40},{40,32},{48,56},{56,48},{64,72... | collective-permute-start | bytes 2359304 | tf_op jit(solution)/shard_map/own_swap/ppermute | solution.py:45
  70.3 18.4 %copy-start.1 = (bf16[768,512]{1,0:T(8,128)(2,1)}, bf16[768,512]{1,0:T(8,128)(2,1)S(1)}, u32[]{:S(2)}) copy-start(bf16[768,512]{1,0:T(8,128)(2,1)S(1)} %collective-permute-done.1.refs_1_.refs_3_) | copy-start | bytes 2359300
  70.3 6.8 %collective-permute-start.15 = (bf16[768,512]{1,0:T(8,128)(2,1)S(1)}, bf16[768,512]{1,0:T(8,128)(2,1)S(1)}, u32[]{:S(2)}, u32[]{:S(2)}) collective-permute-start(bf16[768,512]{1,0:T(8,128)(2,1)S(1)} %collective-permute-done.refs_0_.refs_2_), channel_id=1, source_target_pairs={{0,8},{8,0},{16,24},{24,16},{32,40},{40,32},{48,56},{56,48},{64,72... | collective-permute-start | bytes 2359304 | tf_op jit(solution)/shard_map/low_swap/ppermute | solution.py:45
  71.8 5.6 %collective-permute-start.16 = (bf16[768,512]{1,0:T(8,128)(2,1)S(1)}, bf16[768,512]{1,0:T(8,128)(2,1)S(1)}, u32[]{:S(2)}, u32[]{:S(2)}) collective-permute-start(bf16[768,512]{1,0:T(8,128)(2,1)S(1)} %collective-permute-done.1.refs_1_.refs_3_), channel_id=1, source_target_pairs={{0,8},{8,0},{16,24},{24,16},{32,40},{40,32},{48,56},{56,48},{64,72... | collective-permute-start | bytes 2359304 | tf_op jit(solution)/shard_map/high_swap/ppermute | solution.py:45
  71.9 4.9 %collective-permute-start.10 = (bf16[4,128,512]{2,1,0:T(8,128)(2,1)S(1)}, bf16[4,128,512]{2,1,0:T(8,128)(2,1)S(1)}, u32[]{:S(2)}, u32[]{:S(2)}) collective-permute-start(bf16[4,128,512]{2,1,0:T(8,128)(2,1)S(1)} %shard_map.93.refs_0_), channel_id=1, source_target_pairs={{0,8},{8,0},{16,24},{24,16},{32,40},{40,32},{48,56},{56,48},{64,72... | collective-permute-start | bytes 1572872 | tf_op jit(solution)/shard_map/coeffs_swap0/ppermute | solution.py:45
  72.3 27.0 %collective-permute-start.2 = (bf16[768,512]{1,0:T(8,128)(2,1)S(1)}, bf16[768,512]{1,0:T(8,128)(2,1)S(1)}, u32[]{:S(2)}, u32[]{:S(2)}) collective-permute-start(bf16[768,512]{1,0:T(8,128)(2,1)S(1)} %collective-permute-done.refs_0_.refs_2_), channel_id=1, source_target_pairs={{0,16},{8,24},{16,32},{24,40},{32,48},{40,56},{48,64},{56,72},{64,... | collective-permute-start | bytes 2359304 | tf_op jit(solution)/shard_map/low_hop2/ppermute | solution.py:45
  75.4 1.9 %copy-start.6 = (bf16[768,512]{1,0:T(8,128)(2,1)}, bf16[768,512]{1,0:T(8,128)(2,1)S(1)}, u32[]{:S(2)}) copy-start(bf16[768,512]{1,0:T(8,128)(2,1)S(1)} %collective-permute-done.14.refs_1_) | copy-start | bytes 2359300
  75.4 23.8 %collective-permute-start.3 = (bf16[768,512]{1,0:T(8,128)(2,1)S(1)}, bf16[768,512]{1,0:T(8,128)(2,1)}, u32[]{:S(2)}, u32[]{:S(2)}) collective-permute-start(bf16[768,512]{1,0:T(8,128)(2,1)S(1)} %collective-permute-done.1.refs_1_.refs_3_), channel_id=1, source_target_pairs={{16,0},{24,8},{32,16},{40,24},{48,32},{56,40},{64,48},{72,56},{80,... | collective-permute-start | bytes 2359304 | tf_op jit(solution)/shard_map/high_hop2/ppermute | solution.py:45
  76.8 1.0 copy-start.12
  76.8 19.5 %collective-permute-start.11 = (bf16[4,128,512]{2,1,0:T(8,128)(2,1)}, bf16[4,128,512]{2,1,0:T(8,128)(2,1)}, u32[]{:S(2)}, u32[]{:S(2)}) collective-permute-start(bf16[4,128,512]{2,1,0:T(8,128)(2,1)} %collective-permute-done.7.refs_1_), channel_id=1, source_target_pairs={{0,8},{8,0},{16,24},{24,16},{32,40},{40,32},{48,56},{56,48},{64,72... | collective-permute-start | bytes 1572872 | tf_op jit(solution)/shard_map/coeffs_swap1/ppermute | solution.py:45
  77.1 0.9 copy-start.7
  77.1 19.1 %collective-permute-start.12 = (bf16[4,128,512]{2,1,0:T(8,128)(2,1)}, bf16[4,128,512]{2,1,0:T(8,128)(2,1)}, u32[]{:S(2)}, u32[]{:S(2)}) collective-permute-start(bf16[4,128,512]{2,1,0:T(8,128)(2,1)} %collective-permute-done.8.refs_2_), channel_id=1, source_target_pairs={{0,8},{8,0},{16,24},{24,16},{32,40},{40,32},{48,56},{56,48},{64,72... | collective-permute-start | bytes 1572872 | tf_op jit(solution)/shard_map/coeffs_swap2/ppermute | solution.py:45
  77.4 1.0 copy-start.8
  77.4 18.9 %collective-permute-start.13 = (bf16[4,128,512]{2,1,0:T(8,128)(2,1)}, bf16[4,128,512]{2,1,0:T(8,128)(2,1)}, u32[]{:S(2)}, u32[]{:S(2)}) collective-permute-start(bf16[4,128,512]{2,1,0:T(8,128)(2,1)} %collective-permute-done.9.refs_3_), channel_id=1, source_target_pairs={{0,8},{8,0},{16,24},{24,16},{32,40},{40,32},{48,56},{56,48},{64,72... | collective-permute-start | bytes 1572872 | tf_op jit(solution)/shard_map/coeffs_swap3/ppermute | solution.py:45
  79.7 24.2 %all-to-all-start.2 = ((bf16[32,16,128]{2,1,0:T(8,128)(2,1)}), bf16[32,16,128]{2,1,0:T(8,128)(2,1)S(1)}, u32[]{:S(2)}, u32[]{:S(2)}) async-start(bf16[32,16,128]{2,1,0:T(8,128)(2,1)} %shard_map.94.refs_6_), calls=%async_computation.2 | async-start | bytes 262144 | tf_op jit(solution)/shard_map/fields/all_to_all | solution.py:50
  99.3 12.1 %copy-start.5 = (bf16[768,512]{1,0:T(8,128)(2,1)}, bf16[768,512]{1,0:T(8,128)(2,1)S(1)}, u32[]{:S(2)}) copy-start(bf16[768,512]{1,0:T(8,128)(2,1)S(1)} %collective-permute-done.2.refs_0_) | copy-start | bytes 2359300
  103.9 7.5 %copy-start.11 = (bf16[32,16,128]{2,1,0:T(8,128)(2,1)}, bf16[32,16,128]{2,1,0:T(8,128)(2,1)S(1)}, u32[]{:S(2)}) copy-start(bf16[32,16,128]{2,1,0:T(8,128)(2,1)S(1)} %all-to-all-done.2) | copy-start | bytes 393220
  103.9 4.9 %collective-permute-start.17 = (bf16[768,512]{1,0:T(8,128)(2,1)S(1)}, bf16[768,512]{1,0:T(8,128)(2,1)S(1)}, u32[]{:S(2)}, u32[]{:S(2)}) collective-permute-start(bf16[768,512]{1,0:T(8,128)(2,1)S(1)} %collective-permute-done.2.refs_0_), channel_id=1, source_target_pairs={{8,0},{24,16},{40,32},{56,48},{72,64},{88,80},{104,96},{120,112},{... | collective-permute-start | bytes 2359304 | tf_op jit(solution)/shard_map/low2_swap/ppermute | solution.py:45
  107.0 4.4 %collective-permute-start.18 = (bf16[768,512]{1,0:T(8,128)(2,1)}, bf16[768,512]{1,0:T(8,128)(2,1)S(1)}, u32[]{:S(2)}, u32[]{:S(2)}) collective-permute-start(bf16[768,512]{1,0:T(8,128)(2,1)} %collective-permute-done.3.refs_1_), channel_id=1, source_target_pairs={{0,8},{16,24},{32,40},{48,56},{64,72},{80,88},{96,104},{112,120},{... | collective-permute-start | bytes 2359304 | tf_op jit(solution)/shard_map/high2_swap/ppermute | solution.py:45
  108.8 2.6 %copy-start.9 = (bf16[768,512]{1,0:T(8,128)(2,1)}, bf16[768,512]{1,0:T(8,128)(2,1)S(1)}, u32[]{:S(2)}) copy-start(bf16[768,512]{1,0:T(8,128)(2,1)S(1)} %collective-permute-done.17.refs_2_) | copy-start | bytes 2359300
  111.4 0.9 copy-start.10

commit v4 on v3

--- a/solution.py
+++ b/solution.py
@@ -287,7 +287,7 @@
                 total[...] += dot(self.tiles[s], self.sources[s])
 
 
-FIRST, LAST = 6, 4
+FIRST, LAST = 6, 2
 
 
 def near_first_kernel(me_ref, near_ref, tiles, *refs):
@@ -319,14 +319,11 @@
     )[0]
 
 
-def near_last_kernel(me_ref, near_ref, count_ref, tiles, *refs):
+def near_second_kernel(near_ref, tiles, *refs):
     sources, refs = refs[:LAST], refs[LAST:]
     near, basis, transfer, far_in, field_in, out = refs[:6]
     tile_slots, source_slots, total, b, t, local, field, sems = refs[6:]
-    core = me_ref[0] & 1
-    absent = jnp.int32(99)
-    places = (-4, 4, jnp.where(core == 0, -3, absent), jnp.where(core == 1, 3, absent))
-    picks = [tile_for(near_ref, at) for at in places]
+    picks = [tile_for(near_ref, at) for at in (-4, 4)]
     move = Mover(sems)
     arrive = [move(transfer, t), move(far_in, local), move(field_in, field)]
     arrive += [move(near, total), move(basis, b)]
@@ -336,16 +333,14 @@
     local[...] += dot(t[...], field[...], ((1,), (1,)))
     total[...] += dot(b[...], local[...].astype(BF16))
     products.add_to(total)
-    live = lax.broadcasted_iota(jnp.int32, total.shape, 0) < count_ref[0]
-    total[...] = jnp.where(live, total[...], 0.0)
     move(total, out).wait()
 
 
-def near_last(me, near_list, count, tiles, sources, near, basis, transfer, far, field):
+def near_second(near_list, tiles, sources, near, basis, transfer, far, field):
     (rows, vecs), rank = sources[0].shape, basis.shape[1]
     return call(
-        near_last_kernel,
-        [me, near_list, count],
+        near_second_kernel,
+        [near_list],
         [tiles, *sources, near, basis, transfer, far, field],
         [shape((rows, vecs), F32)],
         [
@@ -358,6 +353,40 @@
             pltpu.VMEM((vecs, rank), BF16),
         ],
         2 * LAST + 6,
+        cost(2 * LAST * rows * rows * vecs, LAST * rows * (rows + vecs) * 2),
+        FULL,
+    )[0]
+
+
+def near_last_kernel(me_ref, near_ref, count_ref, tiles, *refs):
+    sources, (near, out, tile_slots, source_slots, total, sems) = refs[:LAST], refs[LAST:]
+    core = me_ref[0] & 1
+    absent = jnp.int32(99)
+    places = (jnp.where(core == 0, -3, absent), jnp.where(core == 1, 3, absent))
+    picks = [tile_for(near_ref, at) for at in places]
+    move = Mover(sems)
+    arrive = move(near, total)
+    products = Products(move, picks, tiles, sources, tile_slots, source_slots)
+    arrive.wait()
+    products.add_to(total)
+    live = lax.broadcasted_iota(jnp.int32, total.shape, 0) < count_ref[0]
+    total[...] = jnp.where(live, total[...], 0.0)
+    move(total, out).wait()
+
+
+def near_last(me, near_list, count, tiles, sources, near):
+    rows, vecs = sources[0].shape
+    return call(
+        near_last_kernel,
+        [me, near_list, count],
+        [tiles, *sources, near],
+        [shape((rows, vecs), F32)],
+        [
+            pltpu.VMEM((LAST, rows, rows), BF16),
+            pltpu.VMEM((LAST, rows, vecs), BF16),
+            pltpu.VMEM((rows, vecs), F32),
+        ],
+        2 * LAST + 2,
         cost(2 * LAST * rows * rows * vecs, LAST * rows * (rows + vecs) * 2),
         FULL,
     )[0]
@@ -415,18 +444,17 @@
     from_low2, from_high2 = after(after([from_low2, from_high2], far_sum), field)
     low2_beside = send("low2_swap", from_low2, TO_FIRST)
     high2_beside = send("high2_swap", from_high2, TO_SECOND)
-    result = near_last(
-        me,
+    near = near_second(
         near_offsets,
-        count,
         tiles,
-        [from_low2, from_high2, low2_beside, high2_beside],
+        [from_low2, from_high2],
         near,
         basis,
         nested,
         far_sum,
         field,
     )
+    result = near_last(me, near_offsets, count, tiles, [low2_beside, high2_beside], near)
     return result[None, None]
 
 

time: 119 us -> 120 us (level)
  waiting for transfers between devices: 25.8 us -> 21.9 us
  Pallas kernels: 22.6 us -> 26.4 us
    pallas_call x7 -> x8, Pallas kernels: 22.6 us -> 26.4 us  [call(): pl.pallas_call(kernel, out_shape=outs, in_specs=[SMEM] * len(scalars) + [...]
    ppermute x19, waiting for transfers between devices: 21.2 us -> 18.1 us  [send(): return lax.ppermute(block, axis, route)]
  transfers between devices with their start and end apart: 21 -> 21, of which waited for: 5 -> 3; matrix products, arithmetic and copies ran while one was open for 0% -> 0% of each run, Pallas kernels for 11% -> 16%
where the time goes in v4:
time: 120 us; the launch traced here: 119 us
  starting transfers between devices  49.4 us (41%)
  Pallas kernels  26.4 us (22%)
  waiting for transfers between devices  21.9 us (18%)
  blocking collectives  17.7 us (15%)
  local copies, waits for them, and re-layouts  2.66 us (2%)
    ppermute x19, starting transfers between devices, send(): return lax.ppermute(block, axis, route)  29.7 us
    pallas_call x8, Pallas kernels, call(): pl.pallas_call(kernel, out_shape=outs, in_specs=[SMEM] * len(scalars) + [...  26.4 us
    all_to_all x2, starting transfers between devices, exchange(): lax.all_to_all(blocks, axis, 0, 0, tiled=True, axis_index_groups=groups)  19.7 us
    ppermute x19, waiting for transfers between devices, send(): return lax.ppermute(block, axis, route)  18.1 us
    all_to_all x1, blocking collectives, exchange(): lax.all_to_all(blocks, axis, 0, 0, tiled=True, axis_index_groups=groups)  17.7 us
    all_to_all x2, waiting for transfers between devices, exchange(): lax.all_to_all(blocks, axis, 0, 0, tiled=True, axis_index_groups=groups)  3.83 us
    unnamed x26, local copies, waits for them, and re-layouts  2.66 us
  transfers between devices with their start and end apart: 21, of which 3 were waited for; matrix products, arithmetic and copies ran while one was open for 0% of the time, Pallas kernels for 16%

profile of v4, /device:TPU:1, one launch (start us, length us, event | category | flops | bytes accessed | tf_op | source)
XLA Modules:
  0.0 119.2 jit_solution(16556785143499954780)
XLA Ops:
  0.7 2.6 %shard_map.91 = (bf16[768,512]{1,0:T(8,128)(2,1)}, bf16[128,512]{1,0:T(8,128)(2,1)}, bf16[512,128]{1,0:T(8,128)(2,1)}) custom-call(s32[1]{0:T(128)} %bitcast.14.count_ref, bf16[768,512]{1,0:T(8,128)(2,1)} %bitcast.22, bf16[768,128]{1,0:T(8,128)(2,1)} %bitcast.20, bf16[128,128]{1,0:T(8,128)(2,1)} %bitcast.25), custom_call_target="tpu_custom_call" | custom-call | flops 100663296 | bytes 1572864 | tf_op jit(solution)/shard_map/pallas_call | solution.py:74
  3.3 4.1 %collective-permute-start = (bf16[768,512]{1,0:T(8,128)(2,1)}, bf16[768,512]{1,0:T(8,128)(2,1)S(1)}, u32[]{:S(2)}, u32[]{:S(2)}) collective-permute-start(bf16[768,512]{1,0:T(8,128)(2,1)} %get-tuple-element.22.refs_0_), channel_id=1, source_target_pairs={{0,16},{8,24},{16,32},{24,40},{32,48},{40,56},{48,64},{56,72},{64,... | collective-permute-start | bytes 2359304 | tf_op jit(solution)/shard_map/low_hop/ppermute | solution.py:45
  7.4 1.3 %collective-permute-start.1 = (bf16[768,512]{1,0:T(8,128)(2,1)}, bf16[768,512]{1,0:T(8,128)(2,1)S(1)}, u32[]{:S(2)}, u32[]{:S(2)}) collective-permute-start(bf16[768,512]{1,0:T(8,128)(2,1)} %get-tuple-element.22.refs_0_), channel_id=1, source_target_pairs={{16,0},{24,8},{32,16},{40,24},{48,32},{56,40},{64,48},{72,56},{80,... | collective-permute-start | bytes 2359304 | tf_op jit(solution)/shard_map/high_hop/ppermute | solution.py:45
  8.7 10.7 %all-to-all-start = ((bf16[32,16,128]{2,1,0:T(8,128)(2,1)}), bf16[32,16,128]{2,1,0:T(8,128)(2,1)S(1)}, u32[]{:S(2)}, u32[]{:S(2)}) async-start(bf16[32,16,128]{2,1,0:T(8,128)(2,1)} %bitcast.27), calls=%async_computation | async-start | bytes 262144 | tf_op jit(solution)/shard_map/rises/all_to_all | solution.py:50
  19.3 1.5 %collective-permute-start.4 = (bf16[128,512]{1,0:T(8,128)(2,1)}, bf16[128,512]{1,0:T(8,128)(2,1)S(1)}, u32[]{:S(2)}, u32[]{:S(2)}) collective-permute-start(bf16[128,512]{1,0:T(8,128)(2,1)} %get-tuple-element.27.refs_0_), channel_id=1, source_target_pairs={{0,64},{8,72},{16,80},{24,88},{32,96},{40,104},{48,112},{56,120},{... | collective-permute-start | bytes 393224 | tf_op jit(solution)/shard_map/coeffs_z1/ppermute | solution.py:45
  20.8 2.1 %collective-permute-start.5 = (bf16[128,512]{1,0:T(8,128)(2,1)}, bf16[128,512]{1,0:T(8,128)(2,1)S(1)}, u32[]{:S(2)}, u32[]{:S(2)}) collective-permute-start(bf16[128,512]{1,0:T(8,128)(2,1)} %get-tuple-element.27.refs_0_), channel_id=1, source_target_pairs={{0,128},{8,136},{16,144},{24,152},{32,160},{40,168},{48,176},{56,1... | collective-permute-start | bytes 393224 | tf_op jit(solution)/shard_map/coeffs_z2/ppermute | solution.py:45
  22.9 1.1 collective-permute-start.6
  24.1 14.5 %collective-permute-done.4.refs_1_ = bf16[128,512]{1,0:T(8,128)(2,1)S(1)} collective-permute-done((bf16[128,512]{1,0:T(8,128)(2,1)}, bf16[128,512]{1,0:T(8,128)(2,1)S(1)}, u32[]{:S(2)}, u32[]{:S(2)}) %collective-permute-start.4) | collective-permute-done | bytes 131104 | tf_op jit(solution)/shard_map/coeffs_z1/ppermute | solution.py:45
  38.6 3.6 %collective-permute-done.5.refs_2_ = bf16[128,512]{1,0:T(8,128)(2,1)S(1)} collective-permute-done((bf16[128,512]{1,0:T(8,128)(2,1)}, bf16[128,512]{1,0:T(8,128)(2,1)S(1)}, u32[]{:S(2)}, u32[]{:S(2)}) %collective-permute-start.5) | collective-permute-done | bytes 131104 | tf_op jit(solution)/shard_map/coeffs_z2/ppermute | solution.py:45
  42.1 0.0 collective-permute-done.6.refs_3_
  42.1 0.0 all-to-all-done.pieces
  42.1 0.9 copy-done.4
  43.0 1.4 %shard_map.93.refs_0_ = bf16[4,128,512]{2,1,0:T(8,128)(2,1)S(1)} custom-call(bf16[128,512]{1,0:T(8,128)(2,1)S(1)} %copy-done.4, bf16[128,512]{1,0:T(8,128)(2,1)S(1)} %collective-permute-done.4.refs_1_, bf16[128,512]{1,0:T(8,128)(2,1)S(1)} %collective-permute-done.5.refs_2_, bf16[128,512]{1,0:T(8,128)(2,1)S(1)} %collective-permute-done.6.refs_3_), custom_call_target="tpu_custom_call" | custom-call | tf_op jit(solution)/shard_map/pallas_call | solution.py:74
  44.5 0.1 collective-permute-start.7
  44.5 2.9 %collective-permute-start.8 = (bf16[4,128,512]{2,1,0:T(8,128)(2,1)S(1)}, bf16[4,128,512]{2,1,0:T(8,128)(2,1)}, u32[]{:S(2)}, u32[]{:S(2)}) collective-permute-start(bf16[4,128,512]{2,1,0:T(8,128)(2,1)S(1)} %shard_map.93.refs_0_), channel_id=1, source_target_pairs={{0,32},{8,40},{16,48},{24,56},{32,0},{40,8},{48,16},{56,24},{64,96... | collective-permute-start | bytes 1572872 | tf_op jit(solution)/shard_map/coeffs_y2/ppermute | solution.py:45
  47.5 1.9 %collective-permute-start.9 = (bf16[4,128,512]{2,1,0:T(8,128)(2,1)S(1)}, bf16[4,128,512]{2,1,0:T(8,128)(2,1)}, u32[]{:S(2)}, u32[]{:S(2)}) collective-permute-start(bf16[4,128,512]{2,1,0:T(8,128)(2,1)S(1)} %shard_map.93.refs_0_), channel_id=1, source_target_pairs={{0,48},{8,56},{16,0},{24,8},{32,16},{40,24},{48,32},{56,40},{64,11... | collective-permute-start | bytes 1572872 | tf_op jit(solution)/shard_map/coeffs_y3/ppermute | solution.py:45
  49.4 2.9 %collective-permute-start.14 = (bf16[768,512]{1,0:T(8,128)(2,1)}, bf16[768,512]{1,0:T(8,128)(2,1)S(1)}, u32[]{:S(2)}, u32[]{:S(2)}) collective-permute-start(bf16[768,512]{1,0:T(8,128)(2,1)} %get-tuple-element.22.refs_0_), channel_id=1, source_target_pairs={{0,8},{8,0},{16,24},{24,16},{32,40},{40,32},{48,56},{56,48},{64,72... | collective-permute-start | bytes 2359304 | tf_op jit(solution)/shard_map/own_swap/ppermute | solution.py:45
  52.3 0.3 shard_map.92
  52.6 17.7 %all_to_all.19.parents_in = bf16[8,16,128]{2,1,0:T(8,128)(2,1)S(1)} all-to-all(bf16[8,16,128]{2,1,0:T(8,128)(2,1)S(1)} %shard_map.92), channel_id=1, replica_groups=mesh['leaf'=32,'top'=8] {'top'}, dimensions={0} | all-to-all | bytes 65536 | tf_op jit(solution)/shard_map/parents/all_to_all | solution.py:50
  70.3 1.5 %collective-permute-start.15 = (bf16[768,512]{1,0:T(8,128)(2,1)S(1)}, bf16[768,512]{1,0:T(8,128)(2,1)S(1)}, u32[]{:S(2)}, u32[]{:S(2)}) collective-permute-start(bf16[768,512]{1,0:T(8,128)(2,1)S(1)} %collective-permute-done.refs_0_.refs_2_), channel_id=1, source_target_pairs={{0,8},{8,0},{16,24},{24,16},{32,40},{40,32},{48,56},{56,48},{64,72... | collective-permute-start | bytes 2359304 | tf_op jit(solution)/shard_map/low_swap/ppermute | solution.py:45
  71.8 0.1 collective-permute-start.16
  71.9 0.0 collective-permute-done.8.refs_2_
  71.9 0.0 collective-permute-done.9.refs_3_
  71.9 0.4 collective-permute-start.10
  72.3 3.1 %collective-permute-start.2 = (bf16[768,512]{1,0:T(8,128)(2,1)S(1)}, bf16[768,512]{1,0:T(8,128)(2,1)S(1)}, u32[]{:S(2)}, u32[]{:S(2)}) collective-permute-start(bf16[768,512]{1,0:T(8,128)(2,1)S(1)} %collective-permute-done.refs_0_.refs_2_), channel_id=1, source_target_pairs={{0,16},{8,24},{16,32},{24,40},{32,48},{40,56},{48,64},{56,72},{64,... | collective-permute-start | bytes 2359304 | tf_op jit(solution)/shard_map/low_hop2/ppermute | solution.py:45
  75.4 0.0 collective-permute-done.14.refs_1_
  75.4 1.3 %collective-permute-start.3 = (bf16[768,512]{1,0:T(8,128)(2,1)S(1)}, bf16[768,512]{1,0:T(8,128)(2,1)}, u32[]{:S(2)}, u32[]{:S(2)}) collective-permute-start(bf16[768,512]{1,0:T(8,128)(2,1)S(1)} %collective-permute-done.1.refs_1_.refs_3_), channel_id=1, source_target_pairs={{16,0},{24,8},{32,16},{40,24},{48,32},{56,40},{64,48},{72,56},{80,... | collective-permute-start | bytes 2359304 | tf_op jit(solution)/shard_map/high_hop2/ppermute | solution.py:45
  76.7 0.0 collective-permute-done.10.refs_4_
  76.8 0.4 collective-permute-start.11
  77.1 0.0 collective-permute-done.15.refs_4_
  77.1 0.2 collective-permute-start.12
  77.4 0.4 collective-permute-start.13
  77.7 0.3 copy-done.7
  78.0 0.3 copy-done.8
  78.3 1.3 %shard_map.94.refs_6_ = bf16[32,16,128]{2,1,0:T(8,128)(2,1)} custom-call(s32[1]{0:T(128)} %bitcast.10.mine_ref, bf16[8,128,128]{2,1,0:T(8,128)(2,1)S(1)} %bitcast.16, bf16[8,16,128]{2,1,0:T(8,128)(2,1)S(1)} %all_to_all.19.parents_in, bf16[768,512]{1,0:T(8,128)(2,1)S(1)} %collective-permute-done.refs_0_.refs_2_, ...), custom_call_target="tpu_custom_call" | custom-call | flops 4194304 | bytes 262144 | tf_op jit(solution)/shard_map/pallas_call | solution.py:74
  79.7 9.0 %all-to-all-start.2 = ((bf16[32,16,128]{2,1,0:T(8,128)(2,1)}), bf16[32,16,128]{2,1,0:T(8,128)(2,1)S(1)}, u32[]{:S(2)}, u32[]{:S(2)}) async-start(bf16[32,16,128]{2,1,0:T(8,128)(2,1)} %shard_map.94.refs_6_), calls=%async_computation.2 | async-start | bytes 262144 | tf_op jit(solution)/shard_map/fields/all_to_all | solution.py:50
  88.7 8.2 %shard_map.95.refs_8_.refs_2_ = f32[768,512]{1,0:T(8,128)} custom-call(s32[1]{0:T(128)} %bitcast.me_ref, s32[8]{0:T(128)} %bitcast.28, bf16[8,768,768]{2,1,0:T(8,128)(2,1)} %bitcast.17, bf16[768,512]{1,0:T(8,128)(2,1)} %get-tuple-element.22.refs_0_, bf16[768,512]{1,0:T(8,128)(2,1)} %copy-done.6, bf16[768,512]{1,0:T(8,128)(2,1)} %copy-done, ...), custom_call_target="tpu_custom_call" | custom-call | flops 3623878656 | bytes 11796480 | tf_op jit(solution)/shard_map/pallas_call | solution.py:74
  97.0 0.0 collective-permute-done.12.refs_6_
  97.0 0.0 collective-permute-done.13.refs_7_
  97.0 3.0 %shard_map.96.refs_5_ = f32[128,512]{1,0:T(8,128)} custom-call(s32[1]{0:T(128)} %bitcast.me_ref, s32[7]{0:T(128)} %bitcast.31, bf16[7,128,128]{2,1,0:T(8,128)(2,1)} %bitcast.24, bf16[4,128,512]{2,1,0:T(8,128)(2,1)} %copy-done.2, bf16[4,128,512]{2,1,0:T(8,128)(2,1)} %collective-permute-done.7.refs_1_, bf16[4,128,512]{2,1,0:T(8,128)(2,1)} %collective-permute-done.8.refs_2_, ...), custom_call_target="tpu_custom_call" | custom-call | flops 117440512 | bytes 917504 | tf_op jit(solution)/shard_map/pallas_call | solution.py:74
  100.0 0.0 collective-permute-done.2.refs_0_
  100.1 3.8 %all-to-all-done.2 = bf16[32,16,128]{2,1,0:T(8,128)(2,1)S(1)} async-done(((bf16[32,16,128]{2,1,0:T(8,128)(2,1)}), bf16[32,16,128]{2,1,0:T(8,128)(2,1)S(1)}, u32[]{:S(2)}, u32[]{:S(2)}) %all-to-all-start.2) | async-done | bytes 131104 | tf_op jit(solution)/shard_map/fields/all_to_all | solution.py:50
  103.9 3.1 %collective-permute-start.17 = (bf16[768,512]{1,0:T(8,128)(2,1)S(1)}, bf16[768,512]{1,0:T(8,128)(2,1)S(1)}, u32[]{:S(2)}, u32[]{:S(2)}) collective-permute-start(bf16[768,512]{1,0:T(8,128)(2,1)S(1)} %collective-permute-done.2.refs_0_), channel_id=1, source_target_pairs={{8,0},{24,16},{40,32},{56,48},{72,64},{88,80},{104,96},{120,112},{... | collective-permute-start | bytes 2359304 | tf_op jit(solution)/shard_map/low2_swap/ppermute | solution.py:45
  107.0 1.3 %collective-permute-start.18 = (bf16[768,512]{1,0:T(8,128)(2,1)}, bf16[768,512]{1,0:T(8,128)(2,1)S(1)}, u32[]{:S(2)}, u32[]{:S(2)}) collective-permute-start(bf16[768,512]{1,0:T(8,128)(2,1)} %collective-permute-done.3.refs_1_), channel_id=1, source_target_pairs={{0,8},{16,24},{32,40},{48,56},{64,72},{80,88},{96,104},{112,120},{... | collective-permute-start | bytes 2359304 | tf_op jit(solution)/shard_map/high2_swap/ppermute | solution.py:45
  108.3 4.9 %shard_map.97.refs_2_ = f32[768,512]{1,0:T(8,128)} custom-call(s32[8]{0:T(128)} %bitcast.29, bf16[8,768,768]{2,1,0:T(8,128)(2,1)} %bitcast.18, bf16[768,512]{1,0:T(8,128)(2,1)} %copy-done.5, bf16[768,512]{1,0:T(8,128)(2,1)} %collective-permute-done.3.refs_1_, f32[768,512]{1,0:T(8,128)} %shard_map.95.refs_8_.refs_2_, bf16[768,128]{1,0:T(8,128)(2,1)} %bitcast.21, ...), custom_call_target="tpu_custom_call" | custom-call | flops 1207959552 | bytes 3932160 | tf_op jit(solution)/shard_map/pallas_call | solution.py:74
  113.2 0.9 copy-done.9
  114.1 0.3 copy-done.10
  114.4 4.7 %shard_map.98 = f32[768,512]{1,0:T(8,128)} custom-call(s32[1]{0:T(128)} %bitcast.me_ref, s32[8]{0:T(128)} %bitcast.30, s32[1]{0:T(128)} %bitcast.15.count_ref, bf16[8,768,768]{2,1,0:T(8,128)(2,1)} %bitcast.19, bf16[768,512]{1,0:T(8,128)(2,1)} %copy-done.9, bf16[768,512]{1,0:T(8,128)(2,1)} %copy-done.10, f32[768,512]{1,0:T(8,128)} %shard_map.97.refs_2_), custom_call_target="tpu_custom_call" | custom-call | flops 1207959552 | bytes 3932160 | tf_op jit(solution)/shard_map/pallas_call | solution.py:74
  (29 shorter events, 0.1 us)
Async XLA Ops:
  0.0 78.3 %copy-start.3 = (bf16[1,8,128,128]{3,2,1,0:T(8,128)(2,1)S(1)}, bf16[1,8,128,128]{3,2,1,0:T(8,128)(2,1)}, u32[]{:S(2)}) copy-start(bf16[1,8,128,128]{3,2,1,0:T(8,128)(2,1)} %param.14) | copy-start | bytes 786436
  3.3 46.1 %collective-permute-start = (bf16[768,512]{1,0:T(8,128)(2,1)}, bf16[768,512]{1,0:T(8,128)(2,1)S(1)}, u32[]{:S(2)}, u32[]{:S(2)}) collective-permute-start(bf16[768,512]{1,0:T(8,128)(2,1)} %get-tuple-element.22.refs_0_), channel_id=1, source_target_pairs={{0,16},{8,24},{16,32},{24,40},{32,48},{40,56},{48,64},{56,72},{64,... | collective-permute-start | bytes 2359304 | tf_op jit(solution)/shard_map/low_hop/ppermute | solution.py:45
  7.4 62.9 %collective-permute-start.1 = (bf16[768,512]{1,0:T(8,128)(2,1)}, bf16[768,512]{1,0:T(8,128)(2,1)S(1)}, u32[]{:S(2)}, u32[]{:S(2)}) collective-permute-start(bf16[768,512]{1,0:T(8,128)(2,1)} %get-tuple-element.22.refs_0_), channel_id=1, source_target_pairs={{16,0},{24,8},{32,16},{40,24},{48,32},{56,40},{64,48},{72,56},{80,... | collective-permute-start | bytes 2359304 | tf_op jit(solution)/shard_map/high_hop/ppermute | solution.py:45
  8.7 33.5 %all-to-all-start = ((bf16[32,16,128]{2,1,0:T(8,128)(2,1)}), bf16[32,16,128]{2,1,0:T(8,128)(2,1)S(1)}, u32[]{:S(2)}, u32[]{:S(2)}) async-start(bf16[32,16,128]{2,1,0:T(8,128)(2,1)} %bitcast.27), calls=%async_computation | async-start | bytes 262144 | tf_op jit(solution)/shard_map/rises/all_to_all | solution.py:50
  19.3 19.2 %collective-permute-start.4 = (bf16[128,512]{1,0:T(8,128)(2,1)}, bf16[128,512]{1,0:T(8,128)(2,1)S(1)}, u32[]{:S(2)}, u32[]{:S(2)}) collective-permute-start(bf16[128,512]{1,0:T(8,128)(2,1)} %get-tuple-element.27.refs_0_), channel_id=1, source_target_pairs={{0,64},{8,72},{16,80},{24,88},{32,96},{40,104},{48,112},{56,120},{... | collective-permute-start | bytes 393224 | tf_op jit(solution)/shard_map/coeffs_z1/ppermute | solution.py:45
  20.8 21.3 %collective-permute-start.5 = (bf16[128,512]{1,0:T(8,128)(2,1)}, bf16[128,512]{1,0:T(8,128)(2,1)S(1)}, u32[]{:S(2)}, u32[]{:S(2)}) collective-permute-start(bf16[128,512]{1,0:T(8,128)(2,1)} %get-tuple-element.27.refs_0_), channel_id=1, source_target_pairs={{0,128},{8,136},{16,144},{24,152},{32,160},{40,168},{48,176},{56,1... | collective-permute-start | bytes 393224 | tf_op jit(solution)/shard_map/coeffs_z2/ppermute | solution.py:45
  22.9 19.2 %collective-permute-start.6 = (bf16[128,512]{1,0:T(8,128)(2,1)}, bf16[128,512]{1,0:T(8,128)(2,1)S(1)}, u32[]{:S(2)}, u32[]{:S(2)}) collective-permute-start(bf16[128,512]{1,0:T(8,128)(2,1)} %get-tuple-element.27.refs_0_), channel_id=1, source_target_pairs={{0,192},{8,200},{16,208},{24,216},{32,224},{40,232},{48,240},{56,2... | collective-permute-start | bytes 393224 | tf_op jit(solution)/shard_map/coeffs_z3/ppermute | solution.py:45
  42.1 0.9 copy-start.4
  44.4 52.5 %copy-start.2 = (bf16[4,128,512]{2,1,0:T(8,128)(2,1)}, bf16[4,128,512]{2,1,0:T(8,128)(2,1)S(1)}, u32[]{:S(2)}) copy-start(bf16[4,128,512]{2,1,0:T(8,128)(2,1)S(1)} %shard_map.93.refs_0_) | copy-start | bytes 1572868
  44.5 27.3 %collective-permute-start.7 = (bf16[4,128,512]{2,1,0:T(8,128)(2,1)S(1)}, bf16[4,128,512]{2,1,0:T(8,128)(2,1)}, u32[]{:S(2)}, u32[]{:S(2)}) collective-permute-start(bf16[4,128,512]{2,1,0:T(8,128)(2,1)S(1)} %shard_map.93.refs_0_), channel_id=1, source_target_pairs={{0,16},{8,24},{16,32},{24,40},{32,48},{40,56},{48,0},{56,8},{64,80... | collective-permute-start | bytes 1572872 | tf_op jit(solution)/shard_map/coeffs_y1/ppermute | solution.py:45
  44.5 27.3 %collective-permute-start.8 = (bf16[4,128,512]{2,1,0:T(8,128)(2,1)S(1)}, bf16[4,128,512]{2,1,0:T(8,128)(2,1)}, u32[]{:S(2)}, u32[]{:S(2)}) collective-permute-start(bf16[4,128,512]{2,1,0:T(8,128)(2,1)S(1)} %shard_map.93.refs_0_), channel_id=1, source_target_pairs={{0,32},{8,40},{16,48},{24,56},{32,0},{40,8},{48,16},{56,24},{64,96... | collective-permute-start | bytes 1572872 | tf_op jit(solution)/shard_map/coeffs_y2/ppermute | solution.py:45
  47.5 24.4 %collective-permute-start.9 = (bf16[4,128,512]{2,1,0:T(8,128)(2,1)S(1)}, bf16[4,128,512]{2,1,0:T(8,128)(2,1)}, u32[]{:S(2)}, u32[]{:S(2)}) collective-permute-start(bf16[4,128,512]{2,1,0:T(8,128)(2,1)S(1)} %shard_map.93.refs_0_), channel_id=1, source_target_pairs={{0,48},{8,56},{16,0},{24,8},{32,16},{40,24},{48,32},{56,40},{64,11... | collective-permute-start | bytes 1572872 | tf_op jit(solution)/shard_map/coeffs_y3/ppermute | solution.py:45
  49.4 39.3 %copy-start = (bf16[768,512]{1,0:T(8,128)(2,1)}, bf16[768,512]{1,0:T(8,128)(2,1)S(1)}, u32[]{:S(2)}) copy-start(bf16[768,512]{1,0:T(8,128)(2,1)S(1)} %collective-permute-done.refs_0_.refs_2_) | copy-start | bytes 2359300
  49.4 26.1 %collective-permute-start.14 = (bf16[768,512]{1,0:T(8,128)(2,1)}, bf16[768,512]{1,0:T(8,128)(2,1)S(1)}, u32[]{:S(2)}, u32[]{:S(2)}) collective-permute-start(bf16[768,512]{1,0:T(8,128)(2,1)} %get-tuple-element.22.refs_0_), channel_id=1, source_target_pairs={{0,8},{8,0},{16,24},{24,16},{32,40},{40,32},{48,56},{56,48},{64,72... | collective-permute-start | bytes 2359304 | tf_op jit(solution)/shard_map/own_swap/ppermute | solution.py:45
  70.3 18.4 %copy-start.1 = (bf16[768,512]{1,0:T(8,128)(2,1)}, bf16[768,512]{1,0:T(8,128)(2,1)S(1)}, u32[]{:S(2)}) copy-start(bf16[768,512]{1,0:T(8,128)(2,1)S(1)} %collective-permute-done.1.refs_1_.refs_3_) | copy-start | bytes 2359300
  70.3 6.8 %collective-permute-start.15 = (bf16[768,512]{1,0:T(8,128)(2,1)S(1)}, bf16[768,512]{1,0:T(8,128)(2,1)S(1)}, u32[]{:S(2)}, u32[]{:S(2)}) collective-permute-start(bf16[768,512]{1,0:T(8,128)(2,1)S(1)} %collective-permute-done.refs_0_.refs_2_), channel_id=1, source_target_pairs={{0,8},{8,0},{16,24},{24,16},{32,40},{40,32},{48,56},{56,48},{64,72... | collective-permute-start | bytes 2359304 | tf_op jit(solution)/shard_map/low_swap/ppermute | solution.py:45
  71.8 5.6 %collective-permute-start.16 = (bf16[768,512]{1,0:T(8,128)(2,1)S(1)}, bf16[768,512]{1,0:T(8,128)(2,1)S(1)}, u32[]{:S(2)}, u32[]{:S(2)}) collective-permute-start(bf16[768,512]{1,0:T(8,128)(2,1)S(1)} %collective-permute-done.1.refs_1_.refs_3_), channel_id=1, source_target_pairs={{0,8},{8,0},{16,24},{24,16},{32,40},{40,32},{48,56},{56,48},{64,72... | collective-permute-start | bytes 2359304 | tf_op jit(solution)/shard_map/high_swap/ppermute | solution.py:45
  71.9 4.9 %collective-permute-start.10 = (bf16[4,128,512]{2,1,0:T(8,128)(2,1)S(1)}, bf16[4,128,512]{2,1,0:T(8,128)(2,1)S(1)}, u32[]{:S(2)}, u32[]{:S(2)}) collective-permute-start(bf16[4,128,512]{2,1,0:T(8,128)(2,1)S(1)} %shard_map.93.refs_0_), channel_id=1, source_target_pairs={{0,8},{8,0},{16,24},{24,16},{32,40},{40,32},{48,56},{56,48},{64,72... | collective-permute-start | bytes 1572872 | tf_op jit(solution)/shard_map/coeffs_swap0/ppermute | solution.py:45
  72.3 27.8 %collective-permute-start.2 = (bf16[768,512]{1,0:T(8,128)(2,1)S(1)}, bf16[768,512]{1,0:T(8,128)(2,1)S(1)}, u32[]{:S(2)}, u32[]{:S(2)}) collective-permute-start(bf16[768,512]{1,0:T(8,128)(2,1)S(1)} %collective-permute-done.refs_0_.refs_2_), channel_id=1, source_target_pairs={{0,16},{8,24},{16,32},{24,40},{32,48},{40,56},{48,64},{56,72},{64,... | collective-permute-start | bytes 2359304 | tf_op jit(solution)/shard_map/low_hop2/ppermute | solution.py:45
  75.4 1.9 %copy-start.6 = (bf16[768,512]{1,0:T(8,128)(2,1)}, bf16[768,512]{1,0:T(8,128)(2,1)S(1)}, u32[]{:S(2)}) copy-start(bf16[768,512]{1,0:T(8,128)(2,1)S(1)} %collective-permute-done.14.refs_1_) | copy-start | bytes 2359300
  75.4 24.6 %collective-permute-start.3 = (bf16[768,512]{1,0:T(8,128)(2,1)S(1)}, bf16[768,512]{1,0:T(8,128)(2,1)}, u32[]{:S(2)}, u32[]{:S(2)}) collective-permute-start(bf16[768,512]{1,0:T(8,128)(2,1)S(1)} %collective-permute-done.1.refs_1_.refs_3_), channel_id=1, source_target_pairs={{16,0},{24,8},{32,16},{40,24},{48,32},{56,40},{64,48},{72,56},{80,... | collective-permute-start | bytes 2359304 | tf_op jit(solution)/shard_map/high_hop2/ppermute | solution.py:45
  76.8 1.0 copy-start.12
  76.8 20.2 %collective-permute-start.11 = (bf16[4,128,512]{2,1,0:T(8,128)(2,1)}, bf16[4,128,512]{2,1,0:T(8,128)(2,1)}, u32[]{:S(2)}, u32[]{:S(2)}) collective-permute-start(bf16[4,128,512]{2,1,0:T(8,128)(2,1)} %collective-permute-done.7.refs_1_), channel_id=1, source_target_pairs={{0,8},{8,0},{16,24},{24,16},{32,40},{40,32},{48,56},{56,48},{64,72... | collective-permute-start | bytes 1572872 | tf_op jit(solution)/shard_map/coeffs_swap1/ppermute | solution.py:45
  77.1 0.9 copy-start.7
  77.1 19.9 %collective-permute-start.12 = (bf16[4,128,512]{2,1,0:T(8,128)(2,1)}, bf16[4,128,512]{2,1,0:T(8,128)(2,1)}, u32[]{:S(2)}, u32[]{:S(2)}) collective-permute-start(bf16[4,128,512]{2,1,0:T(8,128)(2,1)} %collective-permute-done.8.refs_2_), channel_id=1, source_target_pairs={{0,8},{8,0},{16,24},{24,16},{32,40},{40,32},{48,56},{56,48},{64,72... | collective-permute-start | bytes 1572872 | tf_op jit(solution)/shard_map/coeffs_swap2/ppermute | solution.py:45
  77.4 1.0 copy-start.8
  77.4 19.6 %collective-permute-start.13 = (bf16[4,128,512]{2,1,0:T(8,128)(2,1)}, bf16[4,128,512]{2,1,0:T(8,128)(2,1)}, u32[]{:S(2)}, u32[]{:S(2)}) collective-permute-start(bf16[4,128,512]{2,1,0:T(8,128)(2,1)} %collective-permute-done.9.refs_3_), channel_id=1, source_target_pairs={{0,8},{8,0},{16,24},{24,16},{32,40},{40,32},{48,56},{56,48},{64,72... | collective-permute-start | bytes 1572872 | tf_op jit(solution)/shard_map/coeffs_swap3/ppermute | solution.py:45
  79.7 24.2 %all-to-all-start.2 = ((bf16[32,16,128]{2,1,0:T(8,128)(2,1)}), bf16[32,16,128]{2,1,0:T(8,128)(2,1)S(1)}, u32[]{:S(2)}, u32[]{:S(2)}) async-start(bf16[32,16,128]{2,1,0:T(8,128)(2,1)} %shard_map.94.refs_6_), calls=%async_computation.2 | async-start | bytes 262144 | tf_op jit(solution)/shard_map/fields/all_to_all | solution.py:50
  100.1 8.2 %copy-start.5 = (bf16[768,512]{1,0:T(8,128)(2,1)}, bf16[768,512]{1,0:T(8,128)(2,1)S(1)}, u32[]{:S(2)}) copy-start(bf16[768,512]{1,0:T(8,128)(2,1)S(1)} %collective-permute-done.2.refs_0_) | copy-start | bytes 2359300
  103.9 4.4 %copy-start.11 = (bf16[32,16,128]{2,1,0:T(8,128)(2,1)}, bf16[32,16,128]{2,1,0:T(8,128)(2,1)S(1)}, u32[]{:S(2)}) copy-start(bf16[32,16,128]{2,1,0:T(8,128)(2,1)S(1)} %all-to-all-done.2) | copy-start | bytes 393220
  103.9 9.3 %collective-permute-start.17 = (bf16[768,512]{1,0:T(8,128)(2,1)S(1)}, bf16[768,512]{1,0:T(8,128)(2,1)S(1)}, u32[]{:S(2)}, u32[]{:S(2)}) collective-permute-start(bf16[768,512]{1,0:T(8,128)(2,1)S(1)} %collective-permute-done.2.refs_0_), channel_id=1, source_target_pairs={{8,0},{24,16},{40,32},{56,48},{72,64},{88,80},{104,96},{120,112},{... | collective-permute-start | bytes 2359304 | tf_op jit(solution)/shard_map/low2_swap/ppermute | solution.py:45
  107.0 6.2 %collective-permute-start.18 = (bf16[768,512]{1,0:T(8,128)(2,1)}, bf16[768,512]{1,0:T(8,128)(2,1)S(1)}, u32[]{:S(2)}, u32[]{:S(2)}) collective-permute-start(bf16[768,512]{1,0:T(8,128)(2,1)} %collective-permute-done.3.refs_1_), channel_id=1, source_target_pairs={{0,8},{16,24},{32,40},{48,56},{64,72},{80,88},{96,104},{112,120},{... | collective-permute-start | bytes 2359304 | tf_op jit(solution)/shard_map/high2_swap/ppermute | solution.py:45
  113.2 0.9 copy-start.9
  113.2 1.1 copy-start.10

commit v5 on v3

--- a/solution.py
+++ b/solution.py
@@ -36,8 +36,6 @@
 
 
 SWAP = [(i, i ^ 1) for i in range(2 * CHIPS)]
-TO_FIRST = [(2 * p + 1, 2 * p) for p in range(CHIPS)]
-TO_SECOND = [(2 * p, 2 * p + 1) for p in range(CHIPS)]
 
 
 def send(name, block, route, axis="leaf"):
@@ -287,7 +285,7 @@
                 total[...] += dot(self.tiles[s], self.sources[s])
 
 
-FIRST, LAST = 6, 4
+FIRST, LAST = 6, 3
 
 
 def near_first_kernel(me_ref, near_ref, tiles, *refs):
@@ -323,9 +321,7 @@
     sources, refs = refs[:LAST], refs[LAST:]
     near, basis, transfer, far_in, field_in, out = refs[:6]
     tile_slots, source_slots, total, b, t, local, field, sems = refs[6:]
-    core = me_ref[0] & 1
-    absent = jnp.int32(99)
-    places = (-4, 4, jnp.where(core == 0, -3, absent), jnp.where(core == 1, 3, absent))
+    places = (-4, 4, jnp.where((me_ref[0] & 1) == 0, -3, 3))
     picks = [tile_for(near_ref, at) for at in places]
     move = Mover(sems)
     arrive = [move(transfer, t), move(far_in, local), move(field_in, field)]
@@ -413,14 +409,14 @@
     field = exchange("fields", field, None).reshape(vecs, rank)
     far_sum = far_field(me, far, coupling[0, 0], stores, [near])
     from_low2, from_high2 = after(after([from_low2, from_high2], far_sum), field)
-    low2_beside = send("low2_swap", from_low2, TO_FIRST)
-    high2_beside = send("high2_swap", from_high2, TO_SECOND)
+    wanted = jnp.where(leaf % 2 == 0, from_high2, from_low2)
+    beside2 = send("second_swap", wanted, SWAP)
     result = near_last(
         me,
         near_offsets,
         count,
         tiles,
-        [from_low2, from_high2, low2_beside, high2_beside],
+        [from_low2, from_high2, beside2],
         near,
         basis,
         nested,

time: 119 us -> 116 us (0.975)
  starting transfers between devices: 49.3 us -> 47.4 us
  waiting for transfers between devices: 25.8 us -> 24.6 us
    ppermute x19 -> x18, starting transfers between devices: 29.7 us -> 27.7 us  [send(): return lax.ppermute(block, axis, route)]
    ppermute x19 -> x18, waiting for transfers between devices: 21.2 us -> 20 us  [send(): return lax.ppermute(block, axis, route)]
    unnamed x26 -> x24, local copies, waits for them, and re-layouts: 2.43 us -> 2.42 us
  transfers between devices with their start and end apart: 21 -> 20, of which waited for: 5 -> 4; matrix products, arithmetic and copies ran while one was open for 0% -> 0% of each run, Pallas kernels for 11% -> 12%
where the time goes in v5:
time: 116 us
  starting transfers between devices  47.4 us (41%)
  waiting for transfers between devices  24.6 us (21%)
  Pallas kernels  22.6 us (19%)
  blocking collectives  17.7 us (15%)
  local copies, waits for them, and re-layouts  2.42 us (2%)
    ppermute x18, starting transfers between devices, send(): return lax.ppermute(block, axis, route)  27.7 us
    pallas_call x7, Pallas kernels, call(): pl.pallas_call(kernel, out_shape=outs, in_specs=[SMEM] * len(scalars) + [...  22.6 us
    ppermute x18, waiting for transfers between devices, send(): return lax.ppermute(block, axis, route)  20 us
    all_to_all x2, starting transfers between devices, exchange(): lax.all_to_all(blocks, axis, 0, 0, tiled=True, axis_index_groups=groups)  19.7 us
    all_to_all x1, blocking collectives, exchange(): lax.all_to_all(blocks, axis, 0, 0, tiled=True, axis_index_groups=groups)  17.7 us
    all_to_all x2, waiting for transfers between devices, exchange(): lax.all_to_all(blocks, axis, 0, 0, tiled=True, axis_index_groups=groups)  4.59 us
    unnamed x24, local copies, waits for them, and re-layouts  2.42 us
  transfers between devices with their start and end apart: 20, of which 4 were waited for; matrix products, arithmetic and copies ran while one was open for 0% of the time, Pallas kernels for 12%

profile of v5, /device:TPU:1, one launch (start us, length us, event | category | flops | bytes accessed | tf_op | source)
XLA Modules:
  0.0 115.9 jit_solution(16652211005322912551)
XLA Ops:
  0.7 2.6 %shard_map.91 = (bf16[768,512]{1,0:T(8,128)(2,1)}, bf16[128,512]{1,0:T(8,128)(2,1)}, bf16[512,128]{1,0:T(8,128)(2,1)}) custom-call(s32[1]{0:T(128)} %bitcast.14.count_ref, bf16[768,512]{1,0:T(8,128)(2,1)} %bitcast.21, bf16[768,128]{1,0:T(8,128)(2,1)} %bitcast.19, bf16[128,128]{1,0:T(8,128)(2,1)} %bitcast.24), custom_call_target="tpu_custom_call" | custom-call | flops 100663296 | bytes 1572864 | tf_op jit(solution)/shard_map/pallas_call | solution.py:72
  3.3 4.1 %collective-permute-start = (bf16[768,512]{1,0:T(8,128)(2,1)}, bf16[768,512]{1,0:T(8,128)(2,1)S(1)}, u32[]{:S(2)}, u32[]{:S(2)}) collective-permute-start(bf16[768,512]{1,0:T(8,128)(2,1)} %get-tuple-element.22.refs_0_), channel_id=1, source_target_pairs={{0,16},{8,24},{16,32},{24,40},{32,48},{40,56},{48,64},{56,72},{64,... | collective-permute-start | bytes 2359304 | tf_op jit(solution)/shard_map/low_hop/ppermute | solution.py:43
  7.4 1.3 %collective-permute-start.1 = (bf16[768,512]{1,0:T(8,128)(2,1)}, bf16[768,512]{1,0:T(8,128)(2,1)S(1)}, u32[]{:S(2)}, u32[]{:S(2)}) collective-permute-start(bf16[768,512]{1,0:T(8,128)(2,1)} %get-tuple-element.22.refs_0_), channel_id=1, source_target_pairs={{16,0},{24,8},{32,16},{40,24},{48,32},{56,40},{64,48},{72,56},{80,... | collective-permute-start | bytes 2359304 | tf_op jit(solution)/shard_map/high_hop/ppermute | solution.py:43
  8.7 10.7 %all-to-all-start = ((bf16[32,16,128]{2,1,0:T(8,128)(2,1)}), bf16[32,16,128]{2,1,0:T(8,128)(2,1)S(1)}, u32[]{:S(2)}, u32[]{:S(2)}) async-start(bf16[32,16,128]{2,1,0:T(8,128)(2,1)} %bitcast.26), calls=%async_computation | async-start | bytes 262144 | tf_op jit(solution)/shard_map/rises/all_to_all | solution.py:48
  19.3 1.5 %collective-permute-start.4 = (bf16[128,512]{1,0:T(8,128)(2,1)}, bf16[128,512]{1,0:T(8,128)(2,1)S(1)}, u32[]{:S(2)}, u32[]{:S(2)}) collective-permute-start(bf16[128,512]{1,0:T(8,128)(2,1)} %get-tuple-element.27.refs_0_), channel_id=1, source_target_pairs={{0,64},{8,72},{16,80},{24,88},{32,96},{40,104},{48,112},{56,120},{... | collective-permute-start | bytes 393224 | tf_op jit(solution)/shard_map/coeffs_z1/ppermute | solution.py:43
  20.8 2.1 %collective-permute-start.5 = (bf16[128,512]{1,0:T(8,128)(2,1)}, bf16[128,512]{1,0:T(8,128)(2,1)S(1)}, u32[]{:S(2)}, u32[]{:S(2)}) collective-permute-start(bf16[128,512]{1,0:T(8,128)(2,1)} %get-tuple-element.27.refs_0_), channel_id=1, source_target_pairs={{0,128},{8,136},{16,144},{24,152},{32,160},{40,168},{48,176},{56,1... | collective-permute-start | bytes 393224 | tf_op jit(solution)/shard_map/coeffs_z2/ppermute | solution.py:43
  22.9 1.1 collective-permute-start.6
  24.1 14.5 %collective-permute-done.4.refs_1_ = bf16[128,512]{1,0:T(8,128)(2,1)S(1)} collective-permute-done((bf16[128,512]{1,0:T(8,128)(2,1)}, bf16[128,512]{1,0:T(8,128)(2,1)S(1)}, u32[]{:S(2)}, u32[]{:S(2)}) %collective-permute-start.4) | collective-permute-done | bytes 131104 | tf_op jit(solution)/shard_map/coeffs_z1/ppermute | solution.py:43
  38.5 3.6 %collective-permute-done.5.refs_2_ = bf16[128,512]{1,0:T(8,128)(2,1)S(1)} collective-permute-done((bf16[128,512]{1,0:T(8,128)(2,1)}, bf16[128,512]{1,0:T(8,128)(2,1)S(1)}, u32[]{:S(2)}, u32[]{:S(2)}) %collective-permute-start.5) | collective-permute-done | bytes 131104 | tf_op jit(solution)/shard_map/coeffs_z2/ppermute | solution.py:43
  42.1 0.0 collective-permute-done.6.refs_3_
  42.1 0.0 all-to-all-done.pieces
  42.1 0.9 copy-done.4
  43.0 1.4 %shard_map.93.refs_0_ = bf16[4,128,512]{2,1,0:T(8,128)(2,1)S(1)} custom-call(bf16[128,512]{1,0:T(8,128)(2,1)S(1)} %copy-done.4, bf16[128,512]{1,0:T(8,128)(2,1)S(1)} %collective-permute-done.4.refs_1_, bf16[128,512]{1,0:T(8,128)(2,1)S(1)} %collective-permute-done.5.refs_2_, bf16[128,512]{1,0:T(8,128)(2,1)S(1)} %collective-permute-done.6.refs_3_), custom_call_target="tpu_custom_call" | custom-call | tf_op jit(solution)/shard_map/pallas_call | solution.py:72
  44.4 0.1 collective-permute-start.7
  44.5 2.9 %collective-permute-start.8 = (bf16[4,128,512]{2,1,0:T(8,128)(2,1)S(1)}, bf16[4,128,512]{2,1,0:T(8,128)(2,1)}, u32[]{:S(2)}, u32[]{:S(2)}) collective-permute-start(bf16[4,128,512]{2,1,0:T(8,128)(2,1)S(1)} %shard_map.93.refs_0_), channel_id=1, source_target_pairs={{0,32},{8,40},{16,48},{24,56},{32,0},{40,8},{48,16},{56,24},{64,96... | collective-permute-start | bytes 1572872 | tf_op jit(solution)/shard_map/coeffs_y2/ppermute | solution.py:43
  47.5 1.9 %collective-permute-start.9 = (bf16[4,128,512]{2,1,0:T(8,128)(2,1)S(1)}, bf16[4,128,512]{2,1,0:T(8,128)(2,1)}, u32[]{:S(2)}, u32[]{:S(2)}) collective-permute-start(bf16[4,128,512]{2,1,0:T(8,128)(2,1)S(1)} %shard_map.93.refs_0_), channel_id=1, source_target_pairs={{0,48},{8,56},{16,0},{24,8},{32,16},{40,24},{48,32},{56,40},{64,11... | collective-permute-start | bytes 1572872 | tf_op jit(solution)/shard_map/coeffs_y3/ppermute | solution.py:43
  49.4 0.0 collective-permute-done.refs_0_.refs_2_
  49.4 2.9 %collective-permute-start.14 = (bf16[768,512]{1,0:T(8,128)(2,1)}, bf16[768,512]{1,0:T(8,128)(2,1)S(1)}, u32[]{:S(2)}, u32[]{:S(2)}) collective-permute-start(bf16[768,512]{1,0:T(8,128)(2,1)} %get-tuple-element.22.refs_0_), channel_id=1, source_target_pairs={{0,8},{8,0},{16,24},{24,16},{32,40},{40,32},{48,56},{56,48},{64,72... | collective-permute-start | bytes 2359304 | tf_op jit(solution)/shard_map/own_swap/ppermute | solution.py:43
  52.3 0.3 shard_map.92
  52.6 17.7 %all_to_all.19.parents_in = bf16[8,16,128]{2,1,0:T(8,128)(2,1)S(1)} all-to-all(bf16[8,16,128]{2,1,0:T(8,128)(2,1)S(1)} %shard_map.92), channel_id=1, replica_groups=mesh['leaf'=32,'top'=8] {'top'}, dimensions={0} | all-to-all | bytes 65536 | tf_op jit(solution)/shard_map/parents/all_to_all | solution.py:48
  70.3 0.0 collective-permute-done.1.refs_1_.refs_3_
  70.3 1.5 %collective-permute-start.15 = (bf16[768,512]{1,0:T(8,128)(2,1)S(1)}, bf16[768,512]{1,0:T(8,128)(2,1)S(1)}, u32[]{:S(2)}, u32[]{:S(2)}) collective-permute-start(bf16[768,512]{1,0:T(8,128)(2,1)S(1)} %collective-permute-done.refs_0_.refs_2_), channel_id=1, source_target_pairs={{0,8},{8,0},{16,24},{24,16},{32,40},{40,32},{48,56},{56,48},{64,72... | collective-permute-start | bytes 2359304 | tf_op jit(solution)/shard_map/low_swap/ppermute | solution.py:43
  71.7 0.0 collective-permute-done.7.refs_1_
  71.7 0.1 collective-permute-start.16
  71.8 0.0 collective-permute-done.8.refs_2_
  71.8 0.0 collective-permute-done.9.refs_3_
  71.9 0.4 collective-permute-start.10
  72.3 3.1 %collective-permute-start.2 = (bf16[768,512]{1,0:T(8,128)(2,1)S(1)}, bf16[768,512]{1,0:T(8,128)(2,1)S(1)}, u32[]{:S(2)}, u32[]{:S(2)}) collective-permute-start(bf16[768,512]{1,0:T(8,128)(2,1)S(1)} %collective-permute-done.refs_0_.refs_2_), channel_id=1, source_target_pairs={{0,16},{8,24},{16,32},{24,40},{32,48},{40,56},{48,64},{56,72},{64,... | collective-permute-start | bytes 2359304 | tf_op jit(solution)/shard_map/low_hop2/ppermute | solution.py:43
  75.4 0.0 collective-permute-done.14.refs_1_
  75.4 1.3 %collective-permute-start.3 = (bf16[768,512]{1,0:T(8,128)(2,1)S(1)}, bf16[768,512]{1,0:T(8,128)(2,1)}, u32[]{:S(2)}, u32[]{:S(2)}) collective-permute-start(bf16[768,512]{1,0:T(8,128)(2,1)S(1)} %collective-permute-done.1.refs_1_.refs_3_), channel_id=1, source_target_pairs={{16,0},{24,8},{32,16},{40,24},{48,32},{56,40},{64,48},{72,56},{80,... | collective-permute-start | bytes 2359304 | tf_op jit(solution)/shard_map/high_hop2/ppermute | solution.py:43
  76.7 0.0 collective-permute-done.10.refs_4_
  76.7 0.4 collective-permute-start.11
  77.1 0.0 collective-permute-done.15.refs_4_
  77.1 0.2 collective-permute-start.12
  77.4 0.4 collective-permute-start.13
  77.7 0.3 copy-done.7
  78.0 0.3 copy-done.8
  78.3 1.3 %shard_map.94.refs_6_ = bf16[32,16,128]{2,1,0:T(8,128)(2,1)} custom-call(s32[1]{0:T(128)} %bitcast.10.mine_ref, bf16[8,128,128]{2,1,0:T(8,128)(2,1)S(1)} %bitcast.16, bf16[8,16,128]{2,1,0:T(8,128)(2,1)S(1)} %all_to_all.19.parents_in, bf16[768,512]{1,0:T(8,128)(2,1)S(1)} %collective-permute-done.refs_0_.refs_2_, ...), custom_call_target="tpu_custom_call" | custom-call | flops 4194304 | bytes 262144 | tf_op jit(solution)/shard_map/pallas_call | solution.py:72
  79.7 9.0 %all-to-all-start.2 = ((bf16[32,16,128]{2,1,0:T(8,128)(2,1)}), bf16[32,16,128]{2,1,0:T(8,128)(2,1)S(1)}, u32[]{:S(2)}, u32[]{:S(2)}) async-start(bf16[32,16,128]{2,1,0:T(8,128)(2,1)} %shard_map.94.refs_6_), calls=%async_computation.2 | async-start | bytes 262144 | tf_op jit(solution)/shard_map/fields/all_to_all | solution.py:48
  88.7 7.5 %shard_map.95.refs_8_.refs_3_ = f32[768,512]{1,0:T(8,128)} custom-call(s32[1]{0:T(128)} %bitcast.me_ref, s32[8]{0:T(128)} %bitcast.27, bf16[8,768,768]{2,1,0:T(8,128)(2,1)} %bitcast.17, bf16[768,512]{1,0:T(8,128)(2,1)} %get-tuple-element.22.refs_0_, bf16[768,512]{1,0:T(8,128)(2,1)} %copy-done.6, bf16[768,512]{1,0:T(8,128)(2,1)} %copy-done, ...), custom_call_target="tpu_custom_call" | custom-call | flops 3623878656 | bytes 11796480 | tf_op jit(solution)/shard_map/pallas_call | solution.py:72
  96.2 0.0 collective-permute-done.11.refs_5_
  96.2 3.0 %shard_map.96.refs_6_ = f32[128,512]{1,0:T(8,128)} custom-call(s32[1]{0:T(128)} %bitcast.me_ref, s32[7]{0:T(128)} %bitcast.29, bf16[7,128,128]{2,1,0:T(8,128)(2,1)} %bitcast.23, bf16[4,128,512]{2,1,0:T(8,128)(2,1)} %copy-done.2, bf16[4,128,512]{2,1,0:T(8,128)(2,1)} %collective-permute-done.7.refs_1_, bf16[4,128,512]{2,1,0:T(8,128)(2,1)} %collective-permute-done.8.refs_2_, ...), custom_call_target="tpu_custom_call" | custom-call | flops 117440512 | bytes 917504 | tf_op jit(solution)/shard_map/pallas_call | solution.py:72
  99.3 4.6 %all-to-all-done.2 = bf16[32,16,128]{2,1,0:T(8,128)(2,1)S(1)} async-done(((bf16[32,16,128]{2,1,0:T(8,128)(2,1)}), bf16[32,16,128]{2,1,0:T(8,128)(2,1)S(1)}, u32[]{:S(2)}, u32[]{:S(2)}) %all-to-all-start.2) | async-done | bytes 131104 | tf_op jit(solution)/shard_map/fields/all_to_all | solution.py:48
  103.9 0.1 broadcast_select_fusion
  104.0 2.4 %collective-permute-start.17 = (bf16[768,512]{1,0:T(8,128)(2,1)S(1)}, bf16[768,512]{1,0:T(8,128)(2,1)S(1)}, u32[]{:S(2)}, u32[]{:S(2)}) collective-permute-start(bf16[768,512]{1,0:T(8,128)(2,1)S(1)} %broadcast_select_fusion), channel_id=1, source_target_pairs={{0,8},{8,0},{16,24},{24,16},{32,40},{40,32},{48,56},{56,48},{64,72... | collective-permute-start | bytes 2359304 | tf_op jit(solution)/shard_map/second_swap/ppermute | solution.py:43
  106.4 1.9 %collective-permute-done.17.refs_2_ = bf16[768,512]{1,0:T(8,128)(2,1)S(1)} collective-permute-done((bf16[768,512]{1,0:T(8,128)(2,1)S(1)}, bf16[768,512]{1,0:T(8,128)(2,1)S(1)}, u32[]{:S(2)}, u32[]{:S(2)}) %collective-permute-start.17) | collective-permute-done | bytes 786464 | tf_op jit(solution)/shard_map/second_swap/ppermute | solution.py:43
  108.3 0.9 copy-done.9
  109.2 6.5 %shard_map.97 = f32[768,512]{1,0:T(8,128)} custom-call(s32[1]{0:T(128)} %bitcast.me_ref, s32[8]{0:T(128)} %bitcast.28, s32[1]{0:T(128)} %bitcast.15.count_ref, bf16[8,768,768]{2,1,0:T(8,128)(2,1)} %bitcast.18, bf16[768,512]{1,0:T(8,128)(2,1)} %copy-done.5, bf16[768,512]{1,0:T(8,128)(2,1)} %collective-permute-done.3.refs_1_, bf16[768,512]{1,0:T(8,128)(2,1)} %copy-done.9, ...), custom_call_target="tpu_custom_call" | custom-call | flops 1811939328 | bytes 5898240 | tf_op jit(solution)/shard_map/pallas_call | solution.py:72
  (25 shorter events, 0.1 us)
Async XLA Ops:
  0.0 78.3 %copy-start.3 = (bf16[1,8,128,128]{3,2,1,0:T(8,128)(2,1)S(1)}, bf16[1,8,128,128]{3,2,1,0:T(8,128)(2,1)}, u32[]{:S(2)}) copy-start(bf16[1,8,128,128]{3,2,1,0:T(8,128)(2,1)} %param.14) | copy-start | bytes 786436
  3.3 46.1 %collective-permute-start = (bf16[768,512]{1,0:T(8,128)(2,1)}, bf16[768,512]{1,0:T(8,128)(2,1)S(1)}, u32[]{:S(2)}, u32[]{:S(2)}) collective-permute-start(bf16[768,512]{1,0:T(8,128)(2,1)} %get-tuple-element.22.refs_0_), channel_id=1, source_target_pairs={{0,16},{8,24},{16,32},{24,40},{32,48},{40,56},{48,64},{56,72},{64,... | collective-permute-start | bytes 2359304 | tf_op jit(solution)/shard_map/low_hop/ppermute | solution.py:43
  7.4 62.9 %collective-permute-start.1 = (bf16[768,512]{1,0:T(8,128)(2,1)}, bf16[768,512]{1,0:T(8,128)(2,1)S(1)}, u32[]{:S(2)}, u32[]{:S(2)}) collective-permute-start(bf16[768,512]{1,0:T(8,128)(2,1)} %get-tuple-element.22.refs_0_), channel_id=1, source_target_pairs={{16,0},{24,8},{32,16},{40,24},{48,32},{56,40},{64,48},{72,56},{80,... | collective-permute-start | bytes 2359304 | tf_op jit(solution)/shard_map/high_hop/ppermute | solution.py:43
  8.7 33.5 %all-to-all-start = ((bf16[32,16,128]{2,1,0:T(8,128)(2,1)}), bf16[32,16,128]{2,1,0:T(8,128)(2,1)S(1)}, u32[]{:S(2)}, u32[]{:S(2)}) async-start(bf16[32,16,128]{2,1,0:T(8,128)(2,1)} %bitcast.26), calls=%async_computation | async-start | bytes 262144 | tf_op jit(solution)/shard_map/rises/all_to_all | solution.py:48
  19.3 19.2 %collective-permute-start.4 = (bf16[128,512]{1,0:T(8,128)(2,1)}, bf16[128,512]{1,0:T(8,128)(2,1)S(1)}, u32[]{:S(2)}, u32[]{:S(2)}) collective-permute-start(bf16[128,512]{1,0:T(8,128)(2,1)} %get-tuple-element.27.refs_0_), channel_id=1, source_target_pairs={{0,64},{8,72},{16,80},{24,88},{32,96},{40,104},{48,112},{56,120},{... | collective-permute-start | bytes 393224 | tf_op jit(solution)/shard_map/coeffs_z1/ppermute | solution.py:43
  20.8 21.3 %collective-permute-start.5 = (bf16[128,512]{1,0:T(8,128)(2,1)}, bf16[128,512]{1,0:T(8,128)(2,1)S(1)}, u32[]{:S(2)}, u32[]{:S(2)}) collective-permute-start(bf16[128,512]{1,0:T(8,128)(2,1)} %get-tuple-element.27.refs_0_), channel_id=1, source_target_pairs={{0,128},{8,136},{16,144},{24,152},{32,160},{40,168},{48,176},{56,1... | collective-permute-start | bytes 393224 | tf_op jit(solution)/shard_map/coeffs_z2/ppermute | solution.py:43
  22.9 19.2 %collective-permute-start.6 = (bf16[128,512]{1,0:T(8,128)(2,1)}, bf16[128,512]{1,0:T(8,128)(2,1)S(1)}, u32[]{:S(2)}, u32[]{:S(2)}) collective-permute-start(bf16[128,512]{1,0:T(8,128)(2,1)} %get-tuple-element.27.refs_0_), channel_id=1, source_target_pairs={{0,192},{8,200},{16,208},{24,216},{32,224},{40,232},{48,240},{56,2... | collective-permute-start | bytes 393224 | tf_op jit(solution)/shard_map/coeffs_z3/ppermute | solution.py:43
  42.1 0.9 copy-start.4
  44.4 51.8 %copy-start.2 = (bf16[4,128,512]{2,1,0:T(8,128)(2,1)}, bf16[4,128,512]{2,1,0:T(8,128)(2,1)S(1)}, u32[]{:S(2)}) copy-start(bf16[4,128,512]{2,1,0:T(8,128)(2,1)S(1)} %shard_map.93.refs_0_) | copy-start | bytes 1572868
  44.4 27.3 %collective-permute-start.7 = (bf16[4,128,512]{2,1,0:T(8,128)(2,1)S(1)}, bf16[4,128,512]{2,1,0:T(8,128)(2,1)}, u32[]{:S(2)}, u32[]{:S(2)}) collective-permute-start(bf16[4,128,512]{2,1,0:T(8,128)(2,1)S(1)} %shard_map.93.refs_0_), channel_id=1, source_target_pairs={{0,16},{8,24},{16,32},{24,40},{32,48},{40,56},{48,0},{56,8},{64,80... | collective-permute-start | bytes 1572872 | tf_op jit(solution)/shard_map/coeffs_y1/ppermute | solution.py:43
  44.5 27.3 %collective-permute-start.8 = (bf16[4,128,512]{2,1,0:T(8,128)(2,1)S(1)}, bf16[4,128,512]{2,1,0:T(8,128)(2,1)}, u32[]{:S(2)}, u32[]{:S(2)}) collective-permute-start(bf16[4,128,512]{2,1,0:T(8,128)(2,1)S(1)} %shard_map.93.refs_0_), channel_id=1, source_target_pairs={{0,32},{8,40},{16,48},{24,56},{32,0},{40,8},{48,16},{56,24},{64,96... | collective-permute-start | bytes 1572872 | tf_op jit(solution)/shard_map/coeffs_y2/ppermute | solution.py:43
  47.5 24.4 %collective-permute-start.9 = (bf16[4,128,512]{2,1,0:T(8,128)(2,1)S(1)}, bf16[4,128,512]{2,1,0:T(8,128)(2,1)}, u32[]{:S(2)}, u32[]{:S(2)}) collective-permute-start(bf16[4,128,512]{2,1,0:T(8,128)(2,1)S(1)} %shard_map.93.refs_0_), channel_id=1, source_target_pairs={{0,48},{8,56},{16,0},{24,8},{32,16},{40,24},{48,32},{56,40},{64,11... | collective-permute-start | bytes 1572872 | tf_op jit(solution)/shard_map/coeffs_y3/ppermute | solution.py:43
  49.4 39.3 %copy-start = (bf16[768,512]{1,0:T(8,128)(2,1)}, bf16[768,512]{1,0:T(8,128)(2,1)S(1)}, u32[]{:S(2)}) copy-start(bf16[768,512]{1,0:T(8,128)(2,1)S(1)} %collective-permute-done.refs_0_.refs_2_) | copy-start | bytes 2359300
  49.4 26.1 %collective-permute-start.14 = (bf16[768,512]{1,0:T(8,128)(2,1)}, bf16[768,512]{1,0:T(8,128)(2,1)S(1)}, u32[]{:S(2)}, u32[]{:S(2)}) collective-permute-start(bf16[768,512]{1,0:T(8,128)(2,1)} %get-tuple-element.22.refs_0_), channel_id=1, source_target_pairs={{0,8},{8,0},{16,24},{24,16},{32,40},{40,32},{48,56},{56,48},{64,72... | collective-permute-start | bytes 2359304 | tf_op jit(solution)/shard_map/own_swap/ppermute | solution.py:43
  70.3 18.4 %copy-start.1 = (bf16[768,512]{1,0:T(8,128)(2,1)}, bf16[768,512]{1,0:T(8,128)(2,1)S(1)}, u32[]{:S(2)}) copy-start(bf16[768,512]{1,0:T(8,128)(2,1)S(1)} %collective-permute-done.1.refs_1_.refs_3_) | copy-start | bytes 2359300
  70.3 6.8 %collective-permute-start.15 = (bf16[768,512]{1,0:T(8,128)(2,1)S(1)}, bf16[768,512]{1,0:T(8,128)(2,1)S(1)}, u32[]{:S(2)}, u32[]{:S(2)}) collective-permute-start(bf16[768,512]{1,0:T(8,128)(2,1)S(1)} %collective-permute-done.refs_0_.refs_2_), channel_id=1, source_target_pairs={{0,8},{8,0},{16,24},{24,16},{32,40},{40,32},{48,56},{56,48},{64,72... | collective-permute-start | bytes 2359304 | tf_op jit(solution)/shard_map/low_swap/ppermute | solution.py:43
  71.7 5.6 %collective-permute-start.16 = (bf16[768,512]{1,0:T(8,128)(2,1)S(1)}, bf16[768,512]{1,0:T(8,128)(2,1)S(1)}, u32[]{:S(2)}, u32[]{:S(2)}) collective-permute-start(bf16[768,512]{1,0:T(8,128)(2,1)S(1)} %collective-permute-done.1.refs_1_.refs_3_), channel_id=1, source_target_pairs={{0,8},{8,0},{16,24},{24,16},{32,40},{40,32},{48,56},{56,48},{64,72... | collective-permute-start | bytes 2359304 | tf_op jit(solution)/shard_map/high_swap/ppermute | solution.py:43
  71.9 4.9 %collective-permute-start.10 = (bf16[4,128,512]{2,1,0:T(8,128)(2,1)S(1)}, bf16[4,128,512]{2,1,0:T(8,128)(2,1)S(1)}, u32[]{:S(2)}, u32[]{:S(2)}) collective-permute-start(bf16[4,128,512]{2,1,0:T(8,128)(2,1)S(1)} %shard_map.93.refs_0_), channel_id=1, source_target_pairs={{0,8},{8,0},{16,24},{24,16},{32,40},{40,32},{48,56},{56,48},{64,72... | collective-permute-start | bytes 1572872 | tf_op jit(solution)/shard_map/coeffs_swap0/ppermute | solution.py:43
  72.3 27.0 %collective-permute-start.2 = (bf16[768,512]{1,0:T(8,128)(2,1)S(1)}, bf16[768,512]{1,0:T(8,128)(2,1)S(1)}, u32[]{:S(2)}, u32[]{:S(2)}) collective-permute-start(bf16[768,512]{1,0:T(8,128)(2,1)S(1)} %collective-permute-done.refs_0_.refs_2_), channel_id=1, source_target_pairs={{0,16},{8,24},{16,32},{24,40},{32,48},{40,56},{48,64},{56,72},{64,... | collective-permute-start | bytes 2359304 | tf_op jit(solution)/shard_map/low_hop2/ppermute | solution.py:43
  75.4 1.9 %copy-start.6 = (bf16[768,512]{1,0:T(8,128)(2,1)}, bf16[768,512]{1,0:T(8,128)(2,1)S(1)}, u32[]{:S(2)}) copy-start(bf16[768,512]{1,0:T(8,128)(2,1)S(1)} %collective-permute-done.14.refs_1_) | copy-start | bytes 2359300
  75.4 23.9 %collective-permute-start.3 = (bf16[768,512]{1,0:T(8,128)(2,1)S(1)}, bf16[768,512]{1,0:T(8,128)(2,1)}, u32[]{:S(2)}, u32[]{:S(2)}) collective-permute-start(bf16[768,512]{1,0:T(8,128)(2,1)S(1)} %collective-permute-done.1.refs_1_.refs_3_), channel_id=1, source_target_pairs={{16,0},{24,8},{32,16},{40,24},{48,32},{56,40},{64,48},{72,56},{80,... | collective-permute-start | bytes 2359304 | tf_op jit(solution)/shard_map/high_hop2/ppermute | solution.py:43
  76.7 1.0 copy-start.11
  76.7 19.5 %collective-permute-start.11 = (bf16[4,128,512]{2,1,0:T(8,128)(2,1)}, bf16[4,128,512]{2,1,0:T(8,128)(2,1)}, u32[]{:S(2)}, u32[]{:S(2)}) collective-permute-start(bf16[4,128,512]{2,1,0:T(8,128)(2,1)} %collective-permute-done.7.refs_1_), channel_id=1, source_target_pairs={{0,8},{8,0},{16,24},{24,16},{32,40},{40,32},{48,56},{56,48},{64,72... | collective-permute-start | bytes 1572872 | tf_op jit(solution)/shard_map/coeffs_swap1/ppermute | solution.py:43
  77.1 0.9 copy-start.7
  77.1 19.1 %collective-permute-start.12 = (bf16[4,128,512]{2,1,0:T(8,128)(2,1)}, bf16[4,128,512]{2,1,0:T(8,128)(2,1)}, u32[]{:S(2)}, u32[]{:S(2)}) collective-permute-start(bf16[4,128,512]{2,1,0:T(8,128)(2,1)} %collective-permute-done.8.refs_2_), channel_id=1, source_target_pairs={{0,8},{8,0},{16,24},{24,16},{32,40},{40,32},{48,56},{56,48},{64,72... | collective-permute-start | bytes 1572872 | tf_op jit(solution)/shard_map/coeffs_swap2/ppermute | solution.py:43
  77.4 1.0 copy-start.8
  77.4 18.9 %collective-permute-start.13 = (bf16[4,128,512]{2,1,0:T(8,128)(2,1)}, bf16[4,128,512]{2,1,0:T(8,128)(2,1)}, u32[]{:S(2)}, u32[]{:S(2)}) collective-permute-start(bf16[4,128,512]{2,1,0:T(8,128)(2,1)} %collective-permute-done.9.refs_3_), channel_id=1, source_target_pairs={{0,8},{8,0},{16,24},{24,16},{32,40},{40,32},{48,56},{56,48},{64,72... | collective-permute-start | bytes 1572872 | tf_op jit(solution)/shard_map/coeffs_swap3/ppermute | solution.py:43
  79.7 24.2 %all-to-all-start.2 = ((bf16[32,16,128]{2,1,0:T(8,128)(2,1)}), bf16[32,16,128]{2,1,0:T(8,128)(2,1)S(1)}, u32[]{:S(2)}, u32[]{:S(2)}) async-start(bf16[32,16,128]{2,1,0:T(8,128)(2,1)} %shard_map.94.refs_6_), calls=%async_computation.2 | async-start | bytes 262144 | tf_op jit(solution)/shard_map/fields/all_to_all | solution.py:48
  99.3 9.0 %copy-start.5 = (bf16[768,512]{1,0:T(8,128)(2,1)}, bf16[768,512]{1,0:T(8,128)(2,1)S(1)}, u32[]{:S(2)}) copy-start(bf16[768,512]{1,0:T(8,128)(2,1)S(1)} %collective-permute-done.2.refs_0_) | copy-start | bytes 2359300
  103.9 4.4 %copy-start.10 = (bf16[32,16,128]{2,1,0:T(8,128)(2,1)}, bf16[32,16,128]{2,1,0:T(8,128)(2,1)S(1)}, u32[]{:S(2)}) copy-start(bf16[32,16,128]{2,1,0:T(8,128)(2,1)S(1)} %all-to-all-done.2) | copy-start | bytes 393220
  104.0 4.3 %collective-permute-start.17 = (bf16[768,512]{1,0:T(8,128)(2,1)S(1)}, bf16[768,512]{1,0:T(8,128)(2,1)S(1)}, u32[]{:S(2)}, u32[]{:S(2)}) collective-permute-start(bf16[768,512]{1,0:T(8,128)(2,1)S(1)} %broadcast_select_fusion), channel_id=1, source_target_pairs={{0,8},{8,0},{16,24},{24,16},{32,40},{40,32},{48,56},{56,48},{64,72... | collective-permute-start | bytes 2359304 | tf_op jit(solution)/shard_map/second_swap/ppermute | solution.py:43
  108.3 0.9 copy-start.9
